TPU v7x, 768 devices: a whole 4x8x12 slice. The times are simulated.
768 devices in a mesh: lon: 16 (over y, z_hi), lat: 48 (over z_lo, x, core).
Axes of the slice: x: 4, y: 8, z: 12 (z_hi: 2, z_lo: 6; z = z_hi * 6 + z_lo), core: 2. Of those that a mesh axis runs over, the one named last changes fastest.
Arguments:
- gradient: float32 [2, 768, 4096], P(None, 'lat', 'lon'), may hold values from -6 to 6
- norm_factor: float32 [2, 768, 4096], P(None, 'lat', 'lon'), may hold values from 0.5 to 4
- diff_east: float32 [2, 768, 4096], P(None, 'lat', 'lon'), may hold values from 0.02 to 0.25
- diff_north: float32 [2, 768, 4096], P(None, 'lat', 'lon'), may hold values from 0.02 to 0.25
- cell_area: float32 [768, 4096], P('lat', 'lon'), may hold values from 1 to 2.5
- sea_mask: int32 [768, 4096], P('lat', 'lon'), may hold values 0 or 1
- partner: int32 [4096], replicated, may hold values from 0 to 4095, as said below
Outputs:
- adjoint_field: float32 [2, 768, 4096], P(None, 'lat', 'lon')
Inputs may be any that keep to these rules, and one draw needn't show every extreme that they name: partner is a reflection of the columns: partner[j] = (c - j) modulo 4096 for one column c, so partner[partner[j]] = j.
All inputs are finite; a program needn't handle non-finite values. No bound on the sum of `sea_mask` on one device may be relied on, other than what follows from the above.
Results may differ from a plain program's by a relative error of at most 0.00002.
Values sent between devices are 32-bit elements; how exact they have to be, the bound alone decides.
No kernel may reach another device: no remote copies, remote signals or barrier semaphores. Data moves between devices by JAX's collectives and lax.ppermute only.
A program may use at most 128 MiB of HBM per device.

v0:
```python
import jax
import jax.numpy as jnp
from jax import lax
from jax.sharding import PartitionSpec as P

ITERS = 10


def padded_2(shard, sides, width, wrap):
    for axis, dim in sides:
        count, length = (lax.axis_size(axis), shard.shape[dim])
        up = [(i, (i + 1) % count) for i in range(count if wrap else count - 1)]
        down = [(j, i) for i, j in up]
        last = lax.slice_in_dim(shard, length - width, length, axis=dim)
        initial = lax.slice_in_dim(shard, 0, width, axis=dim)
        before = lax.ppermute(last, axis, up)
        after = lax.ppermute(initial, axis, down)
        shard = jnp.concatenate([before, shard, after], axis=dim)
    return shard


def extend(source, partner_near, lat_place, lat_count):
    across = padded_2(source, (("lon", 2),), 1, True)
    upward = padded_2(source, (("lat", 1),), 1, False)
    padded = jnp.pad(upward, ((0, 0), (0, 0), (1, 1))).at[:, 1:-1, :].set(across)
    top_row = source[:, -1, :]
    whole_row = lax.all_gather(top_row, "lon", axis=1, tiled=True)
    mirrored = jnp.take(whole_row, partner_near, axis=1)
    northern = jnp.where(lat_place == lat_count - 1, mirrored, padded[:, -1, 1:-1])
    return padded.at[:, -1, 1:-1].set(northern)


def per_device(gradient, norm_factor, diff_east, diff_north, cell_area, sea_mask, partner):
    level_count, row_count, col_count = gradient.shape
    lat_place = lax.axis_index("lat")
    lat_count = lax.axis_size("lat")
    lon_place = lax.axis_index("lon")
    partner_near = lax.dynamic_slice_in_dim(partner, lon_place * col_count, col_count, 0)
    ocean = sea_mask.astype(jnp.float32)
    stacked = jnp.concatenate([ocean[None], diff_east, diff_north], 0)
    grown = extend(stacked, partner_near, lat_place, lat_count)
    ocean_grown = grown[0]
    east_grown = grown[1 : 1 + level_count]
    north_grown = grown[1 + level_count :]
    east_coef = diff_east * ocean * ocean_grown[1:-1, 2:]
    west_coef = east_grown[:, 1:-1, :-2] * ocean_grown[1:-1, :-2] * ocean
    global_row = lat_place * row_count + lax.broadcasted_iota(jnp.int32, (row_count, col_count), 0)
    at_top = global_row == row_count * lat_count - 1
    north_coef = (
        jnp.where(at_top, 0.5 * (diff_north + north_grown[:, 2:, 1:-1]), diff_north)
        * ocean
        * ocean_grown[2:, 1:-1]
    )
    south_coef = north_grown[:, :-2, 1:-1] * ocean_grown[:-2, 1:-1] * ocean

    def advance(turn, current):
        weighted = ocean * current / cell_area
        widened = extend(weighted, partner_near, lat_place, lat_count)
        return (
            current
            + east_coef * (widened[:, 1:-1, 2:] - weighted)
            + west_coef * (widened[:, 1:-1, :-2] - weighted)
            + north_coef * (widened[:, 2:, 1:-1] - weighted)
            + south_coef * (widened[:, :-2, 1:-1] - weighted)
        )

    current = lax.fori_loop(0, ITERS, advance, norm_factor * gradient)
    return current / jnp.sqrt(cell_area)


def solution(mesh):
    return jax.shard_map(
        per_device,
        mesh=mesh,
        in_specs=(
            P(None, "lat", "lon"),
            P(None, "lat", "lon"),
            P(None, "lat", "lon"),
            P(None, "lat", "lon"),
            P("lat", "lon"),
            P("lat", "lon"),
            P(),
        ),
        out_specs=P(None, "lat", "lon"),
        check_vma=False,
    )
```

profile of v0, /device:TPU:22, one launch (start us, length us, event | category | flops | bytes accessed | tf_op | source)
XLA Modules:
  0.0 2073.1 jit_solution(14104535741871498068)
XLA Ops:
  8.0 15.1 collective-permute-start.6
  25.0 62.1 %all-gather.1 = f32[5,1,4096]{2,1,0:T(1,128)S(1)} all-gather(f32[5,1,256]{2,1,0:T(1,128)S(1)} %get-tuple-element.259), channel_id=3, replica_groups=mesh['lon'=16,'lat'=48] {'lon'}, dimensions={2}, use_global_device_ids=true | all-gather | bytes 87040 | tf_op jit(solution)/shard_map/all_gather | solution.py:27
  105.1 1965.2 %while.17 = (s32[]{:T(128)}, f32[2,16,256]{0,2,1:T(8,128)}, f32[16,256]{1,0:T(8,128)S(1)}, f32[16,256]{1,0:T(8,128)S(1)}, pred[]{:T(512)}, /*index=5*/s32[256]{0...) while((s32[]{:T(128)}, f32[2,16,256]{0,2,1:T(8,128)}, ...), condition=%wide.region_1.2_spmd, body=%wide.region_0.1_spmd.sunk | while | flops 226242 | bytes 5156474 | solution.py:67
  117.3 8.1 collective-permute-start.3
  125.5 155.1 %all-gather.3 = f32[2,1,4096]{0,2,1:T(8,128)S(1)} all-gather(f32[2,1,256]{0,2,1:T(8,128)S(1)} %get-tuple-element.334), channel_id=2, replica_groups=mesh['lon'=16,'lat'=48] {'lon'}, dimensions={2}, use_global_device_ids=true | all-gather | bytes 34816 | tf_op jit(solution)/shard_map/while/body/eval_jaxpr/all_gather | solution.py:27
  294.9 12.2 collective-permute-start
  319.3 151.6 %all-gather.3 = f32[2,1,4096]{0,2,1:T(8,128)S(1)} all-gather(f32[2,1,256]{0,2,1:T(8,128)S(1)} %get-tuple-element.334), channel_id=2, replica_groups=mesh['lon'=16,'lat'=48] {'lon'}, dimensions={2}, use_global_device_ids=true | all-gather | bytes 34816 | tf_op jit(solution)/shard_map/while/body/eval_jaxpr/all_gather | solution.py:27
  501.2 149.4 %all-gather.3 = f32[2,1,4096]{0,2,1:T(8,128)S(1)} all-gather(f32[2,1,256]{0,2,1:T(8,128)S(1)} %get-tuple-element.334), channel_id=2, replica_groups=mesh['lon'=16,'lat'=48] {'lon'}, dimensions={2}, use_global_device_ids=true | all-gather | bytes 34816 | tf_op jit(solution)/shard_map/while/body/eval_jaxpr/all_gather | solution.py:27
  663.1 22.1 %collective-permute-start.1 = (f32[2,1,256]{0,2,1:T(8,128)S(1)}, f32[2,1,256]{0,2,1:T(8,128)S(1)}, u32[]{:S(2)}, u32[]{:S(2)}) collective-permute-start(f32[2,1,256]{0,2,1:T(8,128)S(1)} %get-tuple-element.334), channel_id=1, source_target_pairs={{0,1},{1,2},{2,3},{3,4},{4,5},{5,6},{6,7},{7,8},{8,9},{9,10},{10,1... | collective-permute-start | bytes 6152 | tf_op jit(solution)/shard_map/while/body/eval_jaxpr/ppermute | solution.py:16
  687.1 9.7 collective-permute-start.2
  699.5 156.1 %all-gather.3 = f32[2,1,4096]{0,2,1:T(8,128)S(1)} all-gather(f32[2,1,256]{0,2,1:T(8,128)S(1)} %get-tuple-element.334), channel_id=2, replica_groups=mesh['lon'=16,'lat'=48] {'lon'}, dimensions={2}, use_global_device_ids=true | all-gather | bytes 34816 | tf_op jit(solution)/shard_map/while/body/eval_jaxpr/all_gather | solution.py:27
  885.8 183.6 %all-gather.3 = f32[2,1,4096]{0,2,1:T(8,128)S(1)} all-gather(f32[2,1,256]{0,2,1:T(8,128)S(1)} %get-tuple-element.334), channel_id=2, replica_groups=mesh['lon'=16,'lat'=48] {'lon'}, dimensions={2}, use_global_device_ids=true | all-gather | bytes 34816 | tf_op jit(solution)/shard_map/while/body/eval_jaxpr/all_gather | solution.py:27
  1087.5 9.5 collective-permute-start.2
  1099.7 149.5 %all-gather.3 = f32[2,1,4096]{0,2,1:T(8,128)S(1)} all-gather(f32[2,1,256]{0,2,1:T(8,128)S(1)} %get-tuple-element.334), channel_id=2, replica_groups=mesh['lon'=16,'lat'=48] {'lon'}, dimensions={2}, use_global_device_ids=true | all-gather | bytes 34816 | tf_op jit(solution)/shard_map/while/body/eval_jaxpr/all_gather | solution.py:27
  1261.7 11.8 collective-permute-start.1
  1275.4 10.8 collective-permute-start.2
  1288.2 176.3 %all-gather.3 = f32[2,1,4096]{0,2,1:T(8,128)S(1)} all-gather(f32[2,1,256]{0,2,1:T(8,128)S(1)} %get-tuple-element.334), channel_id=2, replica_groups=mesh['lon'=16,'lat'=48] {'lon'}, dimensions={2}, use_global_device_ids=true | all-gather | bytes 34816 | tf_op jit(solution)/shard_map/while/body/eval_jaxpr/all_gather | solution.py:27
  1482.5 8.6 collective-permute-start.2
  1495.4 157.8 %all-gather.3 = f32[2,1,4096]{0,2,1:T(8,128)S(1)} all-gather(f32[2,1,256]{0,2,1:T(8,128)S(1)} %get-tuple-element.334), channel_id=2, replica_groups=mesh['lon'=16,'lat'=48] {'lon'}, dimensions={2}, use_global_device_ids=true | all-gather | bytes 34816 | tf_op jit(solution)/shard_map/while/body/eval_jaxpr/all_gather | solution.py:27
  1667.5 7.7 collective-permute-start
  1675.3 8.1 collective-permute-start.2
  1687.5 165.8 %all-gather.3 = f32[2,1,4096]{0,2,1:T(8,128)S(1)} all-gather(f32[2,1,256]{0,2,1:T(8,128)S(1)} %get-tuple-element.334), channel_id=2, replica_groups=mesh['lon'=16,'lat'=48] {'lon'}, dimensions={2}, use_global_device_ids=true | all-gather | bytes 34816 | tf_op jit(solution)/shard_map/while/body/eval_jaxpr/all_gather | solution.py:27
  1873.3 10.7 collective-permute-start.3
  1884.0 176.3 %all-gather.3 = f32[2,1,4096]{0,2,1:T(8,128)S(1)} all-gather(f32[2,1,256]{0,2,1:T(8,128)S(1)} %get-tuple-element.334), channel_id=2, replica_groups=mesh['lon'=16,'lat'=48] {'lon'}, dimensions={2}, use_global_device_ids=true | all-gather | bytes 34816 | tf_op jit(solution)/shard_map/while/body/eval_jaxpr/all_gather | solution.py:27
  (275 shorter events, 253.4 us)
Async XLA Ops:
  107.7 173.6 %collective-permute-start.1 = (f32[2,1,256]{0,2,1:T(8,128)S(1)}, f32[2,1,256]{0,2,1:T(8,128)S(1)}, u32[]{:S(2)}, u32[]{:S(2)}) collective-permute-start(f32[2,1,256]{0,2,1:T(8,128)S(1)} %get-tuple-element.334), channel_id=1, source_target_pairs={{0,1},{1,2},{2,3},{3,4},{4,5},{5,6},{6,7},{7,8},{8,9},{9,10},{10,1... | collective-permute-start | bytes 6152 | tf_op jit(solution)/shard_map/while/body/eval_jaxpr/ppermute | solution.py:16
  109.6 171.7 %collective-permute-start = (f32[2,1,256]{0,2,1:T(8,128)S(1)}, f32[2,1,256]{0,2,1:T(8,128)S(1)}, u32[]{:S(2)}, u32[]{:S(2)}) collective-permute-start(f32[2,1,256]{0,2,1:T(8,128)S(1)} %get-tuple-element.333), channel_id=1, source_target_pairs={{1,0},{2,1},{3,2},{4,3},{5,4},{6,5},{7,6},{8,7},{9,8},{10,9},{11,1... | collective-permute-start | bytes 6152 | tf_op jit(solution)/shard_map/while/body/eval_jaxpr/ppermute | solution.py:17
  293.0 178.7 %collective-permute-start.1 = (f32[2,1,256]{0,2,1:T(8,128)S(1)}, f32[2,1,256]{0,2,1:T(8,128)S(1)}, u32[]{:S(2)}, u32[]{:S(2)}) collective-permute-start(f32[2,1,256]{0,2,1:T(8,128)S(1)} %get-tuple-element.334), channel_id=1, source_target_pairs={{0,1},{1,2},{2,3},{3,4},{4,5},{5,6},{6,7},{7,8},{8,9},{9,10},{10,1... | collective-permute-start | bytes 6152 | tf_op jit(solution)/shard_map/while/body/eval_jaxpr/ppermute | solution.py:16
  294.9 176.8 %collective-permute-start = (f32[2,1,256]{0,2,1:T(8,128)S(1)}, f32[2,1,256]{0,2,1:T(8,128)S(1)}, u32[]{:S(2)}, u32[]{:S(2)}) collective-permute-start(f32[2,1,256]{0,2,1:T(8,128)S(1)} %get-tuple-element.333), channel_id=1, source_target_pairs={{1,0},{2,1},{3,2},{4,3},{5,4},{6,5},{7,6},{8,7},{9,8},{10,9},{11,1... | collective-permute-start | bytes 6152 | tf_op jit(solution)/shard_map/while/body/eval_jaxpr/ppermute | solution.py:17
  663.1 193.2 %collective-permute-start.1 = (f32[2,1,256]{0,2,1:T(8,128)S(1)}, f32[2,1,256]{0,2,1:T(8,128)S(1)}, u32[]{:S(2)}, u32[]{:S(2)}) collective-permute-start(f32[2,1,256]{0,2,1:T(8,128)S(1)} %get-tuple-element.334), channel_id=1, source_target_pairs={{0,1},{1,2},{2,3},{3,4},{4,5},{5,6},{6,7},{7,8},{8,9},{9,10},{10,1... | collective-permute-start | bytes 6152 | tf_op jit(solution)/shard_map/while/body/eval_jaxpr/ppermute | solution.py:16
  868.0 202.1 %collective-permute-start.1 = (f32[2,1,256]{0,2,1:T(8,128)S(1)}, f32[2,1,256]{0,2,1:T(8,128)S(1)}, u32[]{:S(2)}, u32[]{:S(2)}) collective-permute-start(f32[2,1,256]{0,2,1:T(8,128)S(1)} %get-tuple-element.334), channel_id=1, source_target_pairs={{0,1},{1,2},{2,3},{3,4},{4,5},{5,6},{6,7},{7,8},{8,9},{9,10},{10,1... | collective-permute-start | bytes 6152 | tf_op jit(solution)/shard_map/while/body/eval_jaxpr/ppermute | solution.py:16
  870.0 200.2 %collective-permute-start = (f32[2,1,256]{0,2,1:T(8,128)S(1)}, f32[2,1,256]{0,2,1:T(8,128)S(1)}, u32[]{:S(2)}, u32[]{:S(2)}) collective-permute-start(f32[2,1,256]{0,2,1:T(8,128)S(1)} %get-tuple-element.333), channel_id=1, source_target_pairs={{1,0},{2,1},{3,2},{4,3},{5,4},{6,5},{7,6},{8,7},{9,8},{10,9},{11,1... | collective-permute-start | bytes 6152 | tf_op jit(solution)/shard_map/while/body/eval_jaxpr/ppermute | solution.py:17
  873.6 198.5 %collective-permute-start.2 = (f32[2,16,1]{0,2,1:T(1,128)S(1)}, f32[2,16,1]{0,2,1:T(1,128)S(1)}, u32[]{:S(2)}, u32[]{:S(2)}) collective-permute-start(f32[2,16,1]{0,2,1:T(1,128)S(1)} %get-tuple-element.335), channel_id=1, source_target_pairs={{48,0},{96,48},{144,96},{192,144},{240,192},{288,240},{336,288},{3... | collective-permute-start | bytes 392 | tf_op jit(solution)/shard_map/while/body/eval_jaxpr/ppermute | solution.py:17
  880.6 191.6 %collective-permute-start.3 = (f32[2,16,1]{0,2,1:T(1,128)S(1)}, f32[2,16,1]{0,2,1:T(1,128)S(1)}, u32[]{:S(2)}, u32[]{:S(2)}) collective-permute-start(f32[2,16,1]{0,2,1:T(1,128)S(1)} %get-tuple-element.336), channel_id=1, source_target_pairs={{0,48},{48,96},{96,144},{144,192},{192,240},{240,288},{288,336},{3... | collective-permute-start | bytes 392 | tf_op jit(solution)/shard_map/while/body/eval_jaxpr/ppermute | solution.py:16
  1261.7 203.5 %collective-permute-start.1 = (f32[2,1,256]{0,2,1:T(8,128)S(1)}, f32[2,1,256]{0,2,1:T(8,128)S(1)}, u32[]{:S(2)}, u32[]{:S(2)}) collective-permute-start(f32[2,1,256]{0,2,1:T(8,128)S(1)} %get-tuple-element.334), channel_id=1, source_target_pairs={{0,1},{1,2},{2,3},{3,4},{4,5},{5,6},{6,7},{7,8},{8,9},{9,10},{10,1... | collective-permute-start | bytes 6152 | tf_op jit(solution)/shard_map/while/body/eval_jaxpr/ppermute | solution.py:16
  1273.4 191.8 %collective-permute-start = (f32[2,1,256]{0,2,1:T(8,128)S(1)}, f32[2,1,256]{0,2,1:T(8,128)S(1)}, u32[]{:S(2)}, u32[]{:S(2)}) collective-permute-start(f32[2,1,256]{0,2,1:T(8,128)S(1)} %get-tuple-element.333), channel_id=1, source_target_pairs={{1,0},{2,1},{3,2},{4,3},{5,4},{6,5},{7,6},{8,7},{9,8},{10,9},{11,1... | collective-permute-start | bytes 6152 | tf_op jit(solution)/shard_map/while/body/eval_jaxpr/ppermute | solution.py:17
  1275.4 191.8 %collective-permute-start.2 = (f32[2,16,1]{0,2,1:T(1,128)S(1)}, f32[2,16,1]{0,2,1:T(1,128)S(1)}, u32[]{:S(2)}, u32[]{:S(2)}) collective-permute-start(f32[2,16,1]{0,2,1:T(1,128)S(1)} %get-tuple-element.335), channel_id=1, source_target_pairs={{48,0},{96,48},{144,96},{192,144},{240,192},{288,240},{336,288},{3... | collective-permute-start | bytes 392 | tf_op jit(solution)/shard_map/while/body/eval_jaxpr/ppermute | solution.py:17
  1286.2 181.0 %collective-permute-start.3 = (f32[2,16,1]{0,2,1:T(1,128)S(1)}, f32[2,16,1]{0,2,1:T(1,128)S(1)}, u32[]{:S(2)}, u32[]{:S(2)}) collective-permute-start(f32[2,16,1]{0,2,1:T(1,128)S(1)} %get-tuple-element.336), channel_id=1, source_target_pairs={{0,48},{48,96},{96,144},{144,192},{192,240},{240,288},{288,336},{3... | collective-permute-start | bytes 392 | tf_op jit(solution)/shard_map/while/body/eval_jaxpr/ppermute | solution.py:16
  1476.9 177.0 %collective-permute-start.1 = (f32[2,1,256]{0,2,1:T(8,128)S(1)}, f32[2,1,256]{0,2,1:T(8,128)S(1)}, u32[]{:S(2)}, u32[]{:S(2)}) collective-permute-start(f32[2,1,256]{0,2,1:T(8,128)S(1)} %get-tuple-element.334), channel_id=1, source_target_pairs={{0,1},{1,2},{2,3},{3,4},{4,5},{5,6},{6,7},{7,8},{8,9},{9,10},{10,1... | collective-permute-start | bytes 6152 | tf_op jit(solution)/shard_map/while/body/eval_jaxpr/ppermute | solution.py:16
  1478.8 175.1 %collective-permute-start = (f32[2,1,256]{0,2,1:T(8,128)S(1)}, f32[2,1,256]{0,2,1:T(8,128)S(1)}, u32[]{:S(2)}, u32[]{:S(2)}) collective-permute-start(f32[2,1,256]{0,2,1:T(8,128)S(1)} %get-tuple-element.333), channel_id=1, source_target_pairs={{1,0},{2,1},{3,2},{4,3},{5,4},{6,5},{7,6},{8,7},{9,8},{10,9},{11,1... | collective-permute-start | bytes 6152 | tf_op jit(solution)/shard_map/while/body/eval_jaxpr/ppermute | solution.py:17
  1482.5 173.4 %collective-permute-start.2 = (f32[2,16,1]{0,2,1:T(1,128)S(1)}, f32[2,16,1]{0,2,1:T(1,128)S(1)}, u32[]{:S(2)}, u32[]{:S(2)}) collective-permute-start(f32[2,16,1]{0,2,1:T(1,128)S(1)} %get-tuple-element.335), channel_id=1, source_target_pairs={{48,0},{96,48},{144,96},{192,144},{240,192},{288,240},{336,288},{3... | collective-permute-start | bytes 392 | tf_op jit(solution)/shard_map/while/body/eval_jaxpr/ppermute | solution.py:17
  1665.6 188.5 %collective-permute-start.1 = (f32[2,1,256]{0,2,1:T(8,128)S(1)}, f32[2,1,256]{0,2,1:T(8,128)S(1)}, u32[]{:S(2)}, u32[]{:S(2)}) collective-permute-start(f32[2,1,256]{0,2,1:T(8,128)S(1)} %get-tuple-element.334), channel_id=1, source_target_pairs={{0,1},{1,2},{2,3},{3,4},{4,5},{5,6},{6,7},{7,8},{8,9},{9,10},{10,1... | collective-permute-start | bytes 6152 | tf_op jit(solution)/shard_map/while/body/eval_jaxpr/ppermute | solution.py:16
  1667.5 186.5 %collective-permute-start = (f32[2,1,256]{0,2,1:T(8,128)S(1)}, f32[2,1,256]{0,2,1:T(8,128)S(1)}, u32[]{:S(2)}, u32[]{:S(2)}) collective-permute-start(f32[2,1,256]{0,2,1:T(8,128)S(1)} %get-tuple-element.333), channel_id=1, source_target_pairs={{1,0},{2,1},{3,2},{4,3},{5,4},{6,5},{7,6},{8,7},{9,8},{10,9},{11,1... | collective-permute-start | bytes 6152 | tf_op jit(solution)/shard_map/while/body/eval_jaxpr/ppermute | solution.py:17
  1675.3 180.8 %collective-permute-start.2 = (f32[2,16,1]{0,2,1:T(1,128)S(1)}, f32[2,16,1]{0,2,1:T(1,128)S(1)}, u32[]{:S(2)}, u32[]{:S(2)}) collective-permute-start(f32[2,16,1]{0,2,1:T(1,128)S(1)} %get-tuple-element.335), channel_id=1, source_target_pairs={{48,0},{96,48},{144,96},{192,144},{240,192},{288,240},{336,288},{3... | collective-permute-start | bytes 392 | tf_op jit(solution)/shard_map/while/body/eval_jaxpr/ppermute | solution.py:17
  1683.4 172.7 %collective-permute-start.3 = (f32[2,16,1]{0,2,1:T(1,128)S(1)}, f32[2,16,1]{0,2,1:T(1,128)S(1)}, u32[]{:S(2)}, u32[]{:S(2)}) collective-permute-start(f32[2,16,1]{0,2,1:T(1,128)S(1)} %get-tuple-element.336), channel_id=1, source_target_pairs={{0,48},{48,96},{96,144},{144,192},{192,240},{240,288},{288,336},{3... | collective-permute-start | bytes 392 | tf_op jit(solution)/shard_map/while/body/eval_jaxpr/ppermute | solution.py:16
  1865.8 195.3 %collective-permute-start.1 = (f32[2,1,256]{0,2,1:T(8,128)S(1)}, f32[2,1,256]{0,2,1:T(8,128)S(1)}, u32[]{:S(2)}, u32[]{:S(2)}) collective-permute-start(f32[2,1,256]{0,2,1:T(8,128)S(1)} %get-tuple-element.334), channel_id=1, source_target_pairs={{0,1},{1,2},{2,3},{3,4},{4,5},{5,6},{6,7},{7,8},{8,9},{9,10},{10,1... | collective-permute-start | bytes 6152 | tf_op jit(solution)/shard_map/while/body/eval_jaxpr/ppermute | solution.py:16
  1867.7 193.4 %collective-permute-start = (f32[2,1,256]{0,2,1:T(8,128)S(1)}, f32[2,1,256]{0,2,1:T(8,128)S(1)}, u32[]{:S(2)}, u32[]{:S(2)}) collective-permute-start(f32[2,1,256]{0,2,1:T(8,128)S(1)} %get-tuple-element.333), channel_id=1, source_target_pairs={{1,0},{2,1},{3,2},{4,3},{5,4},{6,5},{7,6},{8,7},{9,8},{10,9},{11,1... | collective-permute-start | bytes 6152 | tf_op jit(solution)/shard_map/while/body/eval_jaxpr/ppermute | solution.py:17
  1871.4 191.7 %collective-permute-start.2 = (f32[2,16,1]{0,2,1:T(1,128)S(1)}, f32[2,16,1]{0,2,1:T(1,128)S(1)}, u32[]{:S(2)}, u32[]{:S(2)}) collective-permute-start(f32[2,16,1]{0,2,1:T(1,128)S(1)} %get-tuple-element.335), channel_id=1, source_target_pairs={{48,0},{96,48},{144,96},{192,144},{240,192},{288,240},{336,288},{3... | collective-permute-start | bytes 392 | tf_op jit(solution)/shard_map/while/body/eval_jaxpr/ppermute | solution.py:17
  1873.3 189.8 %collective-permute-start.3 = (f32[2,16,1]{0,2,1:T(1,128)S(1)}, f32[2,16,1]{0,2,1:T(1,128)S(1)}, u32[]{:S(2)}, u32[]{:S(2)}) collective-permute-start(f32[2,16,1]{0,2,1:T(1,128)S(1)} %get-tuple-element.336), channel_id=1, source_target_pairs={{0,48},{48,96},{96,144},{144,192},{192,240},{240,288},{288,336},{3... | collective-permute-start | bytes 392 | tf_op jit(solution)/shard_map/while/body/eval_jaxpr/ppermute | solution.py:16
  (45 other events, 3204.5 us)
where the time goes:
time: 2080 us; the launch traced here: 2070 us
  blocking collectives  1680 us (81%)
  starting transfers between devices  241 us (12%)
  other arithmetic  116 us (6%)
  local copies, waits for them, and re-layouts  31.3 us (2%)
    all_gather x11, blocking collectives, extend(): whole_row = lax.all_gather(top_row, 'lon', axis=1, tiled=True)  1680 us
    ppermute x22, starting transfers between devices, padded_2(): after = lax.ppermute(initial, axis, down)  124 us
    ppermute x22, starting transfers between devices, padded_2(): before = lax.ppermute(last, axis, up)  116 us
    add x10, other arithmetic, advance(): current + east_coef * (widened[:, 1:-1, 2:] - weighted)  60.1 us
  transfers between devices with their start and end apart: 44, of which 0 were waited for; matrix products, arithmetic and copies ran while one was open for 2% of the time, Pallas kernels for 0%

commit v1 on v0

v1 whole, which is shorter than its diff:
```python
import jax
import jax.numpy as jnp
from jax import lax
from jax.experimental import pallas as pl
from jax.experimental.pallas import tpu as pltpu
from jax.sharding import PartitionSpec as P

ITERS = 10
LANES = 128
TILE = 8
AXES = ("lon", "lat")


def pack_kernel(grad, norm, de, dn, area, mask, packed):
    levels = grad.shape[0]
    packed[0:levels] = norm[...] * grad[...]
    packed[levels : 2 * levels] = de[...]
    packed[2 * levels : 3 * levels] = dn[...]
    packed[3 * levels] = mask[...].astype(jnp.float32) / area[...]


def reversed_lanes(x):
    index = LANES - 1 - lax.broadcasted_iota(jnp.int32, (x.shape[0], LANES), 1)
    pieces = []
    for start in range(x.shape[1] - LANES, -1, -LANES):
        piece = x[:, start : start + LANES]
        pieces.append(jnp.take_along_axis(piece, index, axis=1, mode="promise_in_bounds"))
    return pieces


def halo_slots(arrays, tiles):
    per_row = LANES // ITERS
    places = [(k, t) for k in range(arrays) for t in range(tiles)]
    return [(k, t, m // per_row, (m % per_row) * ITERS) for m, (k, t) in enumerate(places)]


def grow_kernel(lat_count, levels, centre, own, upward, downward, last, grown, to_east, to_west):
    arrays, rows, cols = own.shape
    lat_place = lax.axis_index("lat")
    top = lat_count - 1
    grown[:, rows : 2 * rows] = own[...]

    @pl.when(lat_place < top)
    def _():
        grown[:, 0:rows] = upward[...]

    @pl.when(lat_place < top - 1)
    def _():
        grown[:, 2 * rows : 3 * rows] = downward[...]

    @pl.when(lat_place == top - 1)
    def _():
        grown[:, 2 * rows : 3 * rows] = last[...]

    @pl.when(lat_place == top)
    def _():
        grown[:, 0:rows] = last[...]
        offset = lax.rem(centre[0], cols)
        for k in range(arrays):
            east_face = levels <= k < 2 * levels
            north_face = 2 * levels <= k < 3 * levels
            wide = jnp.concatenate(reversed_lanes(upward[k]) + reversed_lanes(downward[k]), axis=1)
            shift = offset + (cols if east_face else cols + 1)
            mirrored = pltpu.roll(wide, shift, 1)[:, :cols]
            if north_face:
                face = own[k, rows - 1 : rows]
                grown[k, 2 * rows - 1 : 2 * rows] = 0.5 * (face + mirrored[rows - 1 : rows])
            skip = 1 if north_face else 0
            for row in range(rows):
                source = max(rows - 1 - skip - row, 0)
                grown[k, 2 * rows + row : 2 * rows + row + 1] = mirrored[source : source + 1]

    row_index = lax.broadcasted_iota(jnp.int32, (TILE, LANES), 0)
    lane = lax.broadcasted_iota(jnp.int32, (TILE, LANES), 1)
    tiles = 3 * rows // TILE

    def piece(k, t, col):
        def tile(at):
            return grown[k, at * TILE : (at + 1) * TILE, col : col + LANES]

        if t == 0:
            return jnp.where(row_index == TILE - 1, tile(0), tile(tiles - 1))
        return tile(t)

    for out, col, first in ((to_east, cols - LANES, LANES - ITERS), (to_west, 0, 0)):
        held = {}
        for k, t, row, place in halo_slots(arrays, tiles - 1):
            moved = pltpu.roll(piece(k, t, col), (place - first) % LANES, 1)
            inside = (lane >= place) & (lane < place + ITERS)
            held[row] = jnp.where(inside, moved, held.get(row, jnp.zeros_like(moved)))
        for row, value in held.items():
            out[row * TILE : (row + 1) * TILE] = value


def steps_kernel(levels, grown, from_east, from_west, area, out):
    arrays, tall, cols = grown.shape
    rows = tall // 3
    tiles = tall // TILE
    lane = lax.broadcasted_iota(jnp.int32, (TILE, LANES), 1)
    edge = {}
    for k, t, row, place in halo_slots(arrays, tiles - 1):
        rows_held = slice(row * TILE, (row + 1) * TILE)
        east = pltpu.roll(from_east[rows_held], (-place) % LANES, 1)
        west = pltpu.roll(from_west[rows_held], (LANES - ITERS - place) % LANES, 1)
        edge[k, t] = jnp.where(lane < ITERS, east, jnp.where(lane >= LANES - ITERS, west, 0.0))

    def whole(k):
        side = jnp.concatenate([edge[k, t % (tiles - 1)] for t in range(tiles)], axis=0)
        return jnp.concatenate([grown[k], side], axis=1)

    wide = cols + LANES

    def east_of(x):
        return pltpu.roll(x, wide - 1, 1)

    def west_of(x):
        return pltpu.roll(x, 1, 1)

    def north_of(x):
        return pltpu.roll(x, x.shape[0] - 1, 0)

    def south_of(x):
        return pltpu.roll(x, 1, 0)

    weight = whole(3 * levels)
    sea = jnp.where(weight > 0.0, 1.0, 0.0)
    sea_pair_east = sea * east_of(sea)
    sea_pair_north = sea * north_of(sea)
    root = jnp.sqrt(area[...])
    for level in range(levels):
        state = whole(level)
        east_face = whole(levels + level) * sea_pair_east
        north_face = whole(2 * levels + level) * sea_pair_north
        held = weight
        for turn in range(ITERS):
            weighted = held * state
            east_flow = east_face * (east_of(weighted) - weighted)
            north_flow = north_face * (north_of(weighted) - weighted)
            state = state + ((east_flow - west_of(east_flow)) + (north_flow - south_of(north_flow)))
            if turn == 1:
                inner = slice(TILE, tall - TILE)
                state, held = state[inner], held[inner]
                east_face, north_face = east_face[inner], north_face[inner]
        start = rows - TILE
        out[level] = state[start : start + rows, :cols] / root


def vmem(count):
    return [pl.BlockSpec(memory_space=pltpu.VMEM)] * count


def per_device(gradient, norm_factor, diff_east, diff_north, cell_area, sea_mask, partner):
    levels, rows, cols = gradient.shape
    arrays = 3 * levels + 1
    lon_count, lat_count = lax.axis_size("lon"), lax.axis_size("lat")
    centre = partner[:1]
    f32 = jnp.float32
    block = jax.ShapeDtypeStruct((arrays, rows, cols), f32)
    packed = pl.pallas_call(
        pack_kernel, out_shape=block, in_specs=vmem(6), out_specs=vmem(1)[0]
    )(gradient, norm_factor, diff_east, diff_north, cell_area, sea_mask)

    def flat(lon, lat):
        return (lon % lon_count) * lat_count + lat

    top = lat_count - 1
    places = range(lon_count)
    north_going = [(flat(p, i), flat(p, i + 1)) for p in places for i in range(top - 1)]
    south_going = [(b, a) for a, b in north_going]
    last_north = [(flat(p, top - 1), flat(p, top)) for p in places]
    last_south = [(b, a) for a, b in last_north]

    def mirror(block_sum):
        return [(flat(block_sum - p, top), flat(p, top)) for p in places]

    def exchange(block_sum):
        def run(x):
            upward = lax.ppermute(x, AXES, north_going + mirror(block_sum))
            downward = lax.ppermute(x, AXES, south_going + mirror(block_sum - 1))
            return upward, downward

        return run

    last = lax.ppermute(packed, AXES, last_north + last_south)
    upward, downward = lax.switch(
        centre[0] // cols, [exchange(k) for k in places], packed
    )
    slots = halo_slots(arrays, 3 * rows // TILE - 1)
    edge = jax.ShapeDtypeStruct(((slots[-1][2] + 1) * TILE, LANES), f32)

    def grow(*refs):
        grow_kernel(lat_count, levels, *refs)

    grown, to_east, to_west = pl.pallas_call(
        grow,
        out_shape=(jax.ShapeDtypeStruct((arrays, 3 * rows, cols), f32), edge, edge),
        in_specs=[pl.BlockSpec(memory_space=pltpu.SMEM)] + vmem(4),
        out_specs=tuple(vmem(3)),
    )(centre, packed, upward, downward, last)
    east_going = [(p, (p + 1) % lon_count) for p in range(lon_count)]
    from_west = lax.ppermute(to_east, "lon", east_going)
    from_east = lax.ppermute(to_west, "lon", [(b, a) for a, b in east_going])

    def steps(*refs):
        steps_kernel(levels, *refs)

    return pl.pallas_call(
        steps,
        out_shape=jax.ShapeDtypeStruct((levels, rows, cols), f32),
        in_specs=vmem(4),
        out_specs=vmem(1)[0],
    )(grown, from_east, from_west, cell_area)


def solution(mesh):
    return jax.shard_map(
        per_device,
        mesh=mesh,
        in_specs=(
            P(None, "lat", "lon"),
            P(None, "lat", "lon"),
            P(None, "lat", "lon"),
            P(None, "lat", "lon"),
            P("lat", "lon"),
            P("lat", "lon"),
            P(),
        ),
        out_specs=P(None, "lat", "lon"),
        check_vma=False,
    )
```

time: 2080 us -> 56.9 us (0.03)
  the two profiles are of different devices: /device:TPU:22 before, /device:TPU:128 now
where the time goes in v1:
time: 56.9 us; the launch traced here: 56.5 us
  starting transfers between devices  26.7 us (47%)
  waiting for transfers between devices  18.7 us (33%)
  Pallas kernels  6.35 us (11%)
  local copies, waits for them, and re-layouts  2.45 us (4%)
  between operations  2.37 us (4%)
    ppermute x1, starting transfers between devices, per_device(): from_east = lax.ppermute(to_west, 'lon', [(b, a) for a, b in east_going])  18.9 us
    ppermute x1, waiting for transfers between devices, per_device(): from_west = lax.ppermute(to_east, 'lon', east_going)  12.3 us
    ppermute x1, waiting for transfers between devices, run(): upward = lax.ppermute(x, AXES, north_going + mirror(block_sum))  5.98 us
    ppermute x1, starting transfers between devices, run(): downward = lax.ppermute(x, AXES, south_going + mirror(block_sum - 1))  3.2 us
    pallas_call x1, Pallas kernels, per_device(): pl.pallas_call(steps, out_shape=jax.ShapeDtypeStruct((levels, rows, cols)...  3.18 us
    pallas_call x1, Pallas kernels, per_device(): pl.pallas_call(grow, out_shape=(jax.ShapeDtypeStruct((arrays, 3 * rows, c...  2.35 us
    ppermute x1, starting transfers between devices, run(): upward = lax.ppermute(x, AXES, north_going + mirror(block_sum))  1.92 us
    ppermute x1, starting transfers between devices, per_device(): from_west = lax.ppermute(to_east, 'lon', east_going)  1.92 us
  transfers between devices with their start and end apart: 5, of which 3 were waited for; matrix products, arithmetic and copies ran while one was open for 2% of the time, Pallas kernels for 0%

profile of v1, /device:TPU:128, one launch (start us, length us, event | category | flops | bytes accessed | tf_op | source)
XLA Modules:
  0.0 56.5 jit_solution(773094520912735377)
XLA Ops:
  0.0 0.8 %shard_map.73.refs_1_ = f32[7,16,256]{2,1,0:T(8,128)S(1)} custom-call(f32[2,16,256]{2,1,0:T(8,128)} %grad.1, f32[2,16,256]{2,1,0:T(8,128)} %norm.1, f32[2,16,256]{2,1,0:T(8,128)} %de.1, f32[2,16,256]{2,1,0:T(8,128)} %dn.1, f32[16,256]{1,0:T(8,128)} %refs_3_.1, s32[16,256]{1,0:T(8,128)} %mask.1), custom_call_target="tpu_custom_call" | custom-call | tf_op jit(solution)/shard_map/pallas_call | solution.py:159
  0.8 0.7 %collective-permute-start.32 = (f32[7,16,256]{2,1,0:T(8,128)S(1)}, f32[7,16,256]{2,1,0:T(8,128)S(1)}, u32[]{:S(2)}, u32[]{:S(2)}) collective-permute-start(f32[7,16,256]{2,1,0:T(8,128)S(1)} %shard_map.73.refs_1_), channel_id=1, source_target_pairs={{46,47},{94,95},{142,143},{190,191},{238,239},{286,287},{334,335},... | collective-permute-start | bytes 344072 | tf_op jit(solution)/shard_map/ppermute | solution.py:184
  1.5 1.2 %slice.3.refs_0_ = s32[1]{0:T(128)} slice(s32[4096]{0:T(1024)} %param.29), slice={[0:1]} | slice | bytes 8 | tf_op jit(solution)/shard_map/slice | solution.py:156
  5.0 11.6 %conditional.1 = (f32[7,16,256]{2,1,0:T(8,128)}, f32[7,16,256]{2,1,0:T(8,128)}) conditional(s32[]{:T(128)} %clamp.3, f32[7,16,256]{2,1,0:T(8,128)S(1)} %shard_map.73.refs_1_, f32[7,16,256]{2,1,0:T(8,128)S(1)} %shard_map.73.refs_1_, f32[7,16,256]{2,1,0:T(8,128)S(1)} %shard_map.73.refs_1_, ...), branch_computations={%region_0.1_spmd, %region_1.2_spmd, %region_2.3_spmd, %region_3.4_... | conditional | bytes 917600 | solution.py:185
  5.0 3.2 %collective-permute-start.17 = (f32[7,16,256]{2,1,0:T(8,128)S(1)}, f32[7,16,256]{2,1,0:T(8,128)}, u32[]{:S(2)}, u32[]{:S(2)}) collective-permute-start(f32[7,16,256]{2,1,0:T(8,128)S(1)} %param.8), channel_id=1, source_target_pairs={{1,0},{2,1},{3,2},{4,3},{5,4},{6,5},{7,6},{8,7},{9,8},{10,9},{11,1... | collective-permute-start | bytes 344072 | tf_op jit(solution)/shard_map/cond/branch_8_fun/ppermute | solution.py:179
  8.3 1.9 %collective-permute-start.16 = (f32[7,16,256]{2,1,0:T(8,128)S(1)}, f32[7,16,256]{2,1,0:T(8,128)}, u32[]{:S(2)}, u32[]{:S(2)}) collective-permute-start(f32[7,16,256]{2,1,0:T(8,128)S(1)} %param.8), channel_id=1, source_target_pairs={{0,1},{1,2},{2,3},{3,4},{4,5},{5,6},{6,7},{7,8},{8,9},{9,10},{10,1... | collective-permute-start | bytes 344072 | tf_op jit(solution)/shard_map/cond/branch_8_fun/ppermute | solution.py:178
  10.2 0.4 collective-permute-done.17
  10.6 6.0 %collective-permute-done.16 = f32[7,16,256]{2,1,0:T(8,128)} collective-permute-done((f32[7,16,256]{2,1,0:T(8,128)S(1)}, f32[7,16,256]{2,1,0:T(8,128)}, u32[]{:S(2)}, u32[]{:S(2)}) %collective-permute-start.16) | collective-permute-done | bytes 114720 | tf_op jit(solution)/shard_map/cond/branch_8_fun/ppermute | solution.py:178
  16.6 0.0 collective-permute-done.32.refs_4_
  16.6 0.0 copy-start
  16.6 0.6 %copy-done = f32[7,16,256]{2,1,0:T(8,128)} copy-done((f32[7,16,256]{2,1,0:T(8,128)}, f32[7,16,256]{2,1,0:T(8,128)S(1)}, u32[]{:S(2)}) %copy-start) | copy-done | bytes 114712
  17.2 2.3 %shard_map.74 = (f32[7,48,256]{2,1,0:T(8,128)}, f32[24,128]{1,0:T(8,128)}, f32[24,128]{1,0:T(8,128)}) custom-call(s32[1]{0:T(128)} %slice.3.refs_0_, f32[7,16,256]{2,1,0:T(8,128)S(1)} %shard_map.73.refs_1_, f32[7,16,256]{2,1,0:T(8,128)} %get-tuple-element.26.refs_2_, f32[7,16,256]{2,1,0:T(8,128)} %get-tuple-element.27.refs_3_, f32[7,16,256]{2,1,0:T(8,128)} %copy-done), custom_call_target="tpu_custom_call" | custom-call | tf_op jit(solution)/shard_map/pallas_call | solution.py:194
  19.6 18.9 %collective-permute-start.33 = (f32[24,128]{1,0:T(8,128)}, f32[24,128]{1,0:T(8,128)S(1)}, u32[]{:S(2)}, u32[]{:S(2)}) collective-permute-start(f32[24,128]{1,0:T(8,128)} %get-tuple-element.29), channel_id=1, source_target_pairs={{48,0},{96,48},{144,96},{192,144},{240,192},{288,240},{336,288},{3... | collective-permute-start | bytes 36872 | tf_op jit(solution)/shard_map/ppermute | solution.py:202
  38.5 1.9 %collective-permute-start.34 = (f32[24,128]{1,0:T(8,128)}, f32[24,128]{1,0:T(8,128)S(1)}, u32[]{:S(2)}, u32[]{:S(2)}) collective-permute-start(f32[24,128]{1,0:T(8,128)} %get-tuple-element.30), channel_id=1, source_target_pairs={{0,48},{48,96},{96,144},{144,192},{192,240},{240,288},{288,336},{3... | collective-permute-start | bytes 36872 | tf_op jit(solution)/shard_map/ppermute | solution.py:201
  40.5 0.0 collective-permute-done.33.refs_1_
  40.5 0.0 copy-start.1
  40.5 12.3 %collective-permute-done.34.refs_2_ = f32[24,128]{1,0:T(8,128)S(1)} collective-permute-done((f32[24,128]{1,0:T(8,128)}, f32[24,128]{1,0:T(8,128)S(1)}, u32[]{:S(2)}, u32[]{:S(2)}) %collective-permute-start.34) | collective-permute-done | bytes 12320 | tf_op jit(solution)/shard_map/ppermute | solution.py:201
  52.7 0.0 copy-start.2
  52.7 0.0 copy-done.1
  52.7 0.6 %copy-done.2 = f32[24,128]{1,0:T(8,128)} copy-done((f32[24,128]{1,0:T(8,128)}, f32[24,128]{1,0:T(8,128)S(1)}, u32[]{:S(2)}) %copy-start.2) | copy-done | bytes 12312
  53.3 3.2 %shard_map.75 = f32[2,16,256]{2,1,0:T(8,128)} custom-call(f32[7,48,256]{2,1,0:T(8,128)} %get-tuple-element.28.refs_0_, f32[24,128]{1,0:T(8,128)} %copy-done.1, f32[24,128]{1,0:T(8,128)} %copy-done.2, f32[16,256]{1,0:T(8,128)} %refs_3_.1), custom_call_target="tpu_custom_call" | custom-call | tf_op jit(solution)/shard_map/pallas_call | solution.py:207
Async XLA Ops:
  0.8 15.8 %collective-permute-start.32 = (f32[7,16,256]{2,1,0:T(8,128)S(1)}, f32[7,16,256]{2,1,0:T(8,128)S(1)}, u32[]{:S(2)}, u32[]{:S(2)}) collective-permute-start(f32[7,16,256]{2,1,0:T(8,128)S(1)} %shard_map.73.refs_1_), channel_id=1, source_target_pairs={{46,47},{94,95},{142,143},{190,191},{238,239},{286,287},{334,335},... | collective-permute-start | bytes 344072 | tf_op jit(solution)/shard_map/ppermute | solution.py:184
  5.0 5.6 %collective-permute-start.17 = (f32[7,16,256]{2,1,0:T(8,128)S(1)}, f32[7,16,256]{2,1,0:T(8,128)}, u32[]{:S(2)}, u32[]{:S(2)}) collective-permute-start(f32[7,16,256]{2,1,0:T(8,128)S(1)} %param.8), channel_id=1, source_target_pairs={{1,0},{2,1},{3,2},{4,3},{5,4},{6,5},{7,6},{8,7},{9,8},{10,9},{11,1... | collective-permute-start | bytes 344072 | tf_op jit(solution)/shard_map/cond/branch_8_fun/ppermute | solution.py:179
  8.3 8.3 %collective-permute-start.16 = (f32[7,16,256]{2,1,0:T(8,128)S(1)}, f32[7,16,256]{2,1,0:T(8,128)}, u32[]{:S(2)}, u32[]{:S(2)}) collective-permute-start(f32[7,16,256]{2,1,0:T(8,128)S(1)} %param.8), channel_id=1, source_target_pairs={{0,1},{1,2},{2,3},{3,4},{4,5},{5,6},{6,7},{7,8},{8,9},{9,10},{10,1... | collective-permute-start | bytes 344072 | tf_op jit(solution)/shard_map/cond/branch_8_fun/ppermute | solution.py:178
  16.6 0.6 %copy-start = (f32[7,16,256]{2,1,0:T(8,128)}, f32[7,16,256]{2,1,0:T(8,128)S(1)}, u32[]{:S(2)}) copy-start(f32[7,16,256]{2,1,0:T(8,128)S(1)} %collective-permute-done.32.refs_4_) | copy-start | bytes 344068
  19.6 20.9 %collective-permute-start.33 = (f32[24,128]{1,0:T(8,128)}, f32[24,128]{1,0:T(8,128)S(1)}, u32[]{:S(2)}, u32[]{:S(2)}) collective-permute-start(f32[24,128]{1,0:T(8,128)} %get-tuple-element.29), channel_id=1, source_target_pairs={{48,0},{96,48},{144,96},{192,144},{240,192},{288,240},{336,288},{3... | collective-permute-start | bytes 36872 | tf_op jit(solution)/shard_map/ppermute | solution.py:202
  38.5 14.2 %collective-permute-start.34 = (f32[24,128]{1,0:T(8,128)}, f32[24,128]{1,0:T(8,128)S(1)}, u32[]{:S(2)}, u32[]{:S(2)}) collective-permute-start(f32[24,128]{1,0:T(8,128)} %get-tuple-element.30), channel_id=1, source_target_pairs={{0,48},{48,96},{96,144},{144,192},{192,240},{240,288},{288,336},{3... | collective-permute-start | bytes 36872 | tf_op jit(solution)/shard_map/ppermute | solution.py:201
  40.5 12.3 %copy-start.1 = (f32[24,128]{1,0:T(8,128)}, f32[24,128]{1,0:T(8,128)S(1)}, u32[]{:S(2)}) copy-start(f32[24,128]{1,0:T(8,128)S(1)} %collective-permute-done.33.refs_1_) | copy-start | bytes 36868
  52.7 0.6 %copy-start.2 = (f32[24,128]{1,0:T(8,128)}, f32[24,128]{1,0:T(8,128)S(1)}, u32[]{:S(2)}) copy-start(f32[24,128]{1,0:T(8,128)S(1)} %collective-permute-done.34.refs_2_) | copy-start | bytes 36868

commit v2 on v0

v2 whole, which is shorter than its diff:
```python
import jax
import jax.numpy as jnp
from jax import lax
from jax.experimental import pallas as pl
from jax.experimental.pallas import tpu as pltpu
from jax.sharding import PartitionSpec as P

ITERS = 10
LANES = 128
TILE = 8
PER_ROW = LANES // ITERS
AXES = ("lon", "lat")


def lane_index(rows=TILE):
    return lax.broadcasted_iota(jnp.int32, (rows, LANES), 1)


def slots(arrays):
    places = [(k, t) for k in range(arrays) for t in range(2)]
    return [(k, t, m // PER_ROW, (m % PER_ROW) * ITERS) for m, (k, t) in enumerate(places)]


def pack_kernel(partner, grad, norm, de, dn, area, mask, block, edges, x_rows, y_rows, place, held, arrived):
    levels, rows, cols = grad.shape
    arrays = block.shape[0]
    copy = pltpu.make_async_copy(partner.at[pl.ds(0, held.shape[0])], held, arrived)
    copy.start()
    block[0:levels] = norm[...] * grad[...]
    block[levels : 2 * levels] = de[...]
    block[2 * levels : 3 * levels] = dn[...]
    block[3 * levels] = mask[...].astype(jnp.float32) / area[...]
    lane = lane_index()
    lon_even = lax.rem(lax.axis_index("lon"), 2) == 0
    lat_even = lax.rem(lax.axis_index("lat"), 2) == 0

    def packed(col, first):
        out = {}
        for k, t, row, at in slots(arrays):
            tile = block[k, t * TILE : (t + 1) * TILE, col : col + LANES]
            moved = pltpu.roll(tile, (at - first) % LANES, 1)
            inside = (lane >= at) & (lane < at + ITERS)
            out[row] = jnp.where(inside, moved, out.get(row, jnp.zeros_like(moved)))
        return out

    east, west = packed(cols - LANES, LANES - ITERS), packed(0, 0)
    count = len(east)
    for row in range(count):
        here = slice(row * TILE, (row + 1) * TILE)
        there = slice((count + row) * TILE, (count + row + 1) * TILE)
        edges[here] = jnp.where(lon_even, east[row], west[row])
        edges[there] = jnp.where(lon_even, west[row], east[row])

    sub = lax.broadcasted_iota(jnp.int32, (TILE, LANES), 0)
    for c in range(cols // LANES):
        at = slice(c * LANES, (c + 1) * LANES)
        base = c * (arrays + 2) * TILE
        extra = {}
        for k in range(arrays):
            low, high = block[k, 0:TILE, at], block[k, TILE : 2 * TILE, at]
            here = slice(base + k * TILE, base + (k + 1) * TILE)
            x_rows[here] = jnp.where(lat_even, high, low)
            y_rows[here] = jnp.where(lat_even, low, high)
            lift = 2 * (k % 4)
            inside = (sub >= lift) & (sub < lift + 2)
            north = pltpu.roll(low, (lift + 2) % TILE, 0)
            south = pltpu.roll(high, lift, 0)
            north_held, south_held = extra.get(k // 4, (jnp.zeros_like(low),) * 2)
            extra[k // 4] = (jnp.where(inside, north, north_held), jnp.where(inside, south, south_held))
        for e, (north, south) in extra.items():
            here = slice(base + (arrays + e) * TILE, base + (arrays + e + 1) * TILE)
            x_rows[here] = jnp.where(lat_even, north, south)
            y_rows[here] = jnp.where(lat_even, south, north)
    copy.wait()
    moved = held[0] + ITERS
    q = lax.rem(lax.div(moved, cols), lax.axis_size("lon"))
    offset = lax.rem(moved, cols) - ITERS
    place[0] = 2 * q + jnp.where(offset < ITERS - 1, 1, 0)
    place[1] = offset


def near_kernel(x_rows, y_rows, first, second, after, x_out, y_out):
    del after
    rows, tall = x_rows.shape[0], first.shape[0]
    half = tall // 2
    x_out[0:rows] = x_rows[...]
    x_out[rows : rows + tall] = first[...]
    x_out[rows + tall : rows + 2 * tall] = second[...]
    y_out[0:rows] = y_rows[...]
    y_out[rows : rows + half] = first[0:half]
    y_out[rows + half : rows + tall] = second[0:half]


def reversed_lanes(x):
    index = LANES - 1 - lane_index(x.shape[0])
    return jnp.take_along_axis(x, index, axis=1, mode="promise_in_bounds")


def steps_kernel(levels, place, own, first, second, x_in, y_in, f0, f1, f2, area, out, ext):
    arrays, rows, cols = own.shape
    wide, tall = cols + LANES, 3 * rows
    tiles_across = cols // LANES
    band = (arrays + 2) * TILE
    data = band * tiles_across
    edge = first.shape[0] // 2
    lon_even = lax.rem(lax.axis_index("lon"), 2) == 0
    lat = lax.axis_index("lat")
    lat_even = lax.rem(lat, 2) == 0
    at_top = lat == lax.axis_size("lat") - 1
    below_top = lat == lax.axis_size("lat") - 2
    lane = lane_index()

    def put_sides(start, a, b):
        from_east, from_west = jnp.where(lon_even, a, b), jnp.where(lon_even, b, a)
        for k, t, row, at in slots(arrays):
            here = slice(row * TILE, (row + 1) * TILE)
            east = pltpu.roll(from_east[here], (-at) % LANES, 1)
            west = pltpu.roll(from_west[here], (LANES - ITERS - at) % LANES, 1)
            side = jnp.where(lane < ITERS, east, jnp.where(lane >= LANES - ITERS, west, 0.0))
            ext[k, start + t * TILE : start + (t + 1) * TILE, cols:wide] = side

    def put_rows(start, main, spare, lift_base, rows_of):
        for c in range(tiles_across):
            at = slice(c * LANES, (c + 1) * LANES)
            for k in range(arrays):
                base = c * band
                ext[k, start + main * TILE : start + (main + 1) * TILE, at] = rows_of(base + k * TILE)
                few = rows_of(base + (arrays + k // 4) * TILE)
                lift = (lift_base - 2 * (k % 4)) % TILE
                ext[k, start + spare * TILE : start + (spare + 1) * TILE, at] = pltpu.roll(few, lift, 0)

    for k in range(arrays):
        ext[k, rows : 2 * rows, 0:cols] = own[k]
    x_first, x_second = x_in[data : data + edge], x_in[data + 2 * edge : data + 3 * edge]
    x_mate_first, x_mate_second = x_in[data + edge : data + 2 * edge], x_in[data + 3 * edge : data + 4 * edge]
    y_first, y_second = y_in[data : data + edge], y_in[data + edge : data + 2 * edge]
    put_sides(
        rows,
        jnp.where(at_top, x_mate_first, first[0:edge]),
        jnp.where(at_top, x_mate_second, second[0:edge]),
    )

    def south_rows(at):
        return jnp.where(lat_even, y_in[at : at + TILE], x_in[at : at + TILE])

    def north_rows(at):
        return jnp.where(lat_even, x_in[at : at + TILE], y_in[at : at + TILE])

    put_rows(0, 1, 0, TILE - 2, south_rows)
    put_sides(0, jnp.where(lat_even, y_first, x_first), jnp.where(lat_even, y_second, x_second))

    @pl.when(jnp.logical_not(at_top))
    def _():
        put_rows(2 * rows, 0, 1, 0, north_rows)
        put_sides(
            2 * rows,
            jnp.where(below_top, first[edge : 2 * edge], jnp.where(lat_even, x_first, y_first)),
            jnp.where(below_top, second[edge : 2 * edge], jnp.where(lat_even, x_second, y_second)),
        )

    @pl.when(at_top)
    def _():
        offset = place[1]
        span = 3 * cols
        for k in range(arrays):
            east_face = levels <= k < 2 * levels
            north_face = 2 * levels <= k < 3 * levels
            pieces = []
            for f in (f0, f1, f2):
                for c in range(tiles_across - 1, -1, -1):
                    main = f[c * band + k * TILE : c * band + (k + 1) * TILE]
                    few = f[c * band + (arrays + k // 4) * TILE : c * band + (arrays + k // 4 + 1) * TILE]
                    few = pltpu.roll(few, (TILE - 2 - 2 * (k % 4)) % TILE, 0)
                    pieces.append(reversed_lanes(jnp.concatenate([few, main], axis=0)))
            shift = offset + span - cols + (0 if east_face else 1)
            turned = pltpu.roll(jnp.concatenate(pieces, axis=1), shift, 1)
            far = lane_index(rows)
            beyond = turned[:, cols : cols + LANES]
            before = turned[:, span - LANES :]
            side = jnp.where(far < ITERS, beyond, jnp.where(far >= LANES - ITERS, before, 0.0))
            mirrored = jnp.concatenate([turned[:, :cols], side], axis=1)
            if north_face:
                face = ext[k, 2 * rows - 1 : 2 * rows]
                ext[k, 2 * rows - 1 : 2 * rows] = 0.5 * (face + mirrored[rows - 1 : rows])
            skip = 1 if north_face else 0
            for row in range(rows):
                source = max(rows - 1 - skip - row, 0)
                ext[k, 2 * rows + row : 2 * rows + row + 1] = mirrored[source : source + 1]

    def east_of(x):
        return pltpu.roll(x, wide - 1, 1)

    def west_of(x):
        return pltpu.roll(x, 1, 1)

    def north_of(x):
        return pltpu.roll(x, x.shape[0] - 1, 0)

    def south_of(x):
        return pltpu.roll(x, 1, 0)

    weight = ext[3 * levels]
    sea = jnp.where(weight > 0.0, 1.0, 0.0)
    sea_east = sea * east_of(sea)
    sea_north = sea * north_of(sea)
    root = jnp.sqrt(area[...])
    for level in range(levels):
        state = ext[level]
        east_face = ext[levels + level] * sea_east
        north_face = ext[2 * levels + level] * sea_north
        held = weight
        for turn in range(ITERS):
            weighted = held * state
            east_flow = east_face * (east_of(weighted) - weighted)
            north_flow = north_face * (north_of(weighted) - weighted)
            state = state + ((east_flow - west_of(east_flow)) + (north_flow - south_of(north_flow)))
            if turn == 1:
                inner = slice(TILE, tall - TILE)
                state, held = state[inner], held[inner]
                east_face, north_face = east_face[inner], north_face[inner]
        start = rows - TILE
        out[level] = state[start : start + rows, :cols] / root


VMEM = pl.BlockSpec(memory_space=pltpu.VMEM)
SMEM = pl.BlockSpec(memory_space=pltpu.SMEM)
ANY = pl.BlockSpec(memory_space=pl.ANY)
PARAMS = pltpu.CompilerParams(vmem_limit_bytes=8 * 1024 * 1024)


def per_device(gradient, norm_factor, diff_east, diff_north, cell_area, sea_mask, partner):
    levels, rows, cols = gradient.shape
    arrays = 3 * levels + 1
    lon_count, lat_count = lax.axis_size("lon"), lax.axis_size("lat")

    def held(*shape):
        return jax.ShapeDtypeStruct(shape, jnp.float32)

    edge = (slots(arrays)[-1][2] + 1) * TILE
    data = (arrays + 2) * TILE * (cols // LANES)
    block, edges, x_rows, y_rows, place = pl.pallas_call(
        pack_kernel,
        out_shape=(
            held(arrays, rows, cols),
            held(2 * edge, LANES),
            held(data, LANES),
            held(data, LANES),
            jax.ShapeDtypeStruct((2,), jnp.int32),
        ),
        in_specs=[ANY] + [VMEM] * 6,
        out_specs=(VMEM, VMEM, VMEM, VMEM, SMEM),
        scratch_shapes=[pltpu.SMEM((LANES,), jnp.int32), pltpu.SemaphoreType.DMA],
        compiler_params=PARAMS,
    )(partner, gradient, norm_factor, diff_east, diff_north, cell_area, sea_mask)

    def flat(lon, lat):
        return (lon % lon_count) * lat_count + lat

    top = lat_count - 1
    around = range(lon_count)

    def swap(pairs):
        return [pair for a, b in pairs for pair in ((a, b), (b, a))]

    def lon_swap(start):
        return swap([(flat(p, i), flat(p + 1, i)) for p in around[start::2] for i in range(top)])

    def lat_swap(start):
        return swap([(flat(p, i), flat(p, i + 1)) for p in around for i in range(start, top, 2)])

    def mirror(total):
        return [(flat(total - p, top), flat(p, top)) for p in around]

    mate = lax.ppermute(edges, AXES, [(flat(p, top), flat(p, top - 1)) for p in around])
    first = lax.ppermute(jnp.concatenate([edges[:edge], mate[:edge]]), AXES, lon_swap(0))
    second = lax.ppermute(jnp.concatenate([edges[edge:], mate[edge:]]), AXES, lon_swap(1))

    def fold(total, third):
        def run(x):
            f0 = lax.ppermute(x, AXES, mirror(total))
            f1 = lax.ppermute(x, AXES, mirror(total - 1))
            f2 = lax.ppermute(x, AXES, mirror(total - 2)) if third else jnp.zeros_like(x)
            return f0, f1, f2

        return run

    branches = [fold(total, third) for total in around for third in (False, True)]
    f0, f1, f2 = lax.switch(place[0], branches, y_rows)
    x_out, y_out = pl.pallas_call(
        near_kernel,
        out_shape=(held(data + 4 * edge, LANES), held(data + 2 * edge, LANES)),
        in_specs=[VMEM] * 4 + [ANY],
        out_specs=(VMEM, VMEM),
        compiler_params=PARAMS,
    )(x_rows, y_rows, first, second, f0)
    x_in = lax.ppermute(x_out, AXES, lat_swap(0))
    y_in = lax.ppermute(y_out, AXES, lat_swap(1))

    def steps(*refs):
        steps_kernel(levels, *refs)

    return pl.pallas_call(
        steps,
        out_shape=held(levels, rows, cols),
        in_specs=[SMEM] + [VMEM] * 9,
        out_specs=VMEM,
        scratch_shapes=[pltpu.VMEM((arrays, 3 * rows, cols + LANES), jnp.float32)],
        compiler_params=PARAMS,
    )(place, block, first, second, x_in, y_in, f0, f1, f2, cell_area)


def solution(mesh):
    return jax.shard_map(
        per_device,
        mesh=mesh,
        in_specs=(
            P(None, "lat", "lon"),
            P(None, "lat", "lon"),
            P(None, "lat", "lon"),
            P(None, "lat", "lon"),
            P("lat", "lon"),
            P("lat", "lon"),
            P(),
        ),
        out_specs=P(None, "lat", "lon"),
        check_vma=False,
    )
```

time: 2080 us -> 51.7 us (0.02)
  the two profiles are of different devices: /device:TPU:22 before, /device:TPU:7 now
where the time goes in v2:
time: 51.7 us; the launch traced here: 51 us
  starting transfers between devices  29.8 us (58%)
  waiting for transfers between devices  10.6 us (21%)
  local copies, waits for them, and re-layouts  5.83 us (11%)
  Pallas kernels  4.5 us (9%)
    ppermute x1, starting transfers between devices, per_device(): lax.ppermute(jnp.concatenate([edges[edge:], mate[edge:]]), AXES, lon_swap...  17.8 us
    ppermute x1, waiting for transfers between devices, per_device(): lax.ppermute(jnp.concatenate([edges[:edge], mate[:edge]]), AXES, lon_swap...  5.56 us
    unnamed x16, local copies, waits for them, and re-layouts  5.18 us
    ppermute x1, waiting for transfers between devices, per_device(): y_in = lax.ppermute(y_out, AXES, lat_swap(1))  5.04 us
    ppermute x1, starting transfers between devices, per_device(): x_in = lax.ppermute(x_out, AXES, lat_swap(0))  4.01 us
    pallas_call x1, Pallas kernels, per_device(): pl.pallas_call(steps, out_shape=held(levels, rows, cols), in_specs=[SMEM]...  3.32 us
    ppermute x1, starting transfers between devices, per_device(): y_in = lax.ppermute(y_out, AXES, lat_swap(1))  2.91 us
    ppermute x1, starting transfers between devices, per_device(): lax.ppermute(jnp.concatenate([edges[:edge], mate[:edge]]), AXES, lon_swap...  1.92 us
  transfers between devices with their start and end apart: 7, of which 2 were waited for; matrix products, arithmetic and copies ran while one was open for 1% of the time, Pallas kernels for 0%

profile of v2, /device:TPU:7, one launch (start us, length us, event | category | flops | bytes accessed | tf_op | source)
XLA Modules:
  0.0 51.0 jit_solution(4700520790577739582)
XLA Ops:
  0.0 0.7 %copy-done = f32[16,256]{1,0:T(8,128)S(1)} copy-done((f32[16,256]{1,0:T(8,128)S(1)}, f32[16,256]{1,0:T(8,128)}, u32[]{:S(2)}) %copy-start) | copy-done | bytes 16408
  0.7 0.8 %copy-done.2 = f32[2,16,256]{2,1,0:T(8,128)S(1)} copy-done((f32[2,16,256]{2,1,0:T(8,128)S(1)}, f32[2,16,256]{2,1,0:T(8,128)}, u32[]{:S(2)}) %copy-start.2) | copy-done | bytes 32792
  1.5 0.8 %copy-done.3 = f32[2,16,256]{2,1,0:T(8,128)S(1)} copy-done((f32[2,16,256]{2,1,0:T(8,128)S(1)}, f32[2,16,256]{2,1,0:T(8,128)}, u32[]{:S(2)}) %copy-start.3) | copy-done | bytes 32792
  2.2 0.8 %copy-done.4 = f32[2,16,256]{2,1,0:T(8,128)S(1)} copy-done((f32[2,16,256]{2,1,0:T(8,128)S(1)}, f32[2,16,256]{2,1,0:T(8,128)}, u32[]{:S(2)}) %copy-start.4) | copy-done | bytes 32792
  3.0 0.8 %copy-done.5 = f32[2,16,256]{2,1,0:T(8,128)S(1)} copy-done((f32[2,16,256]{2,1,0:T(8,128)S(1)}, f32[2,16,256]{2,1,0:T(8,128)}, u32[]{:S(2)}) %copy-start.5) | copy-done | bytes 32792
  3.8 0.7 %copy-done.6 = s32[4096]{0:T(1024)S(1)} copy-done((s32[4096]{0:T(1024)S(1)}, s32[4096]{0:T(1024)}, u32[]{:S(2)}) %copy-start.6) | copy-done | bytes 16408
  4.5 0.7 %copy-done.7 = s32[16,256]{1,0:T(8,128)S(1)} copy-done((s32[16,256]{1,0:T(8,128)S(1)}, s32[16,256]{1,0:T(8,128)}, u32[]{:S(2)}) %copy-start.7) | copy-done | bytes 16408
  5.2 1.2 %shard_map.73 = (f32[7,16,256]{2,1,0:T(8,128)S(1)}, f32[32,128]{1,0:T(8,128)S(1)}, f32[144,128]{1,0:T(8,128)S(1)}, f32[144,128]{1,0:T(8,128)S(1)}, s32[2]{0:T(128)S(1)}) custom-call(s32[4096]{0:T(1024)S(1)} %copy-done.6, f32[2,16,256]{2,1,0:T(8,128)S(1)} %copy-done.2, f32[2,16,256]{2,1,0:T(8,128)S(1)} %copy-done.3, f32[2,16,256]{2,1,0:T(8,128)S(1)} %copy-done.4, ...), custom_call_target="tpu_custom_call" | custom-call | tf_op jit(solution)/shard_map/pallas_call | solution.py:241
  6.4 0.7 %collective-permute-start.80 = (f32[32,128]{1,0:T(8,128)S(1)}, f32[32,128]{1,0:T(8,128)S(1)}, u32[]{:S(2)}, u32[]{:S(2)}) collective-permute-start(f32[32,128]{1,0:T(8,128)S(1)} %get-tuple-element.49), channel_id=1, source_target_pairs={{47,46},{95,94},{143,142},{191,190},{239,238},{287,286},{335,334},... | collective-permute-start | bytes 49160 | tf_op jit(solution)/shard_map/ppermute | solution.py:274
  7.0 0.0 collective-permute-done.80
  7.1 17.8 %collective-permute-start.82 = (f32[32,128]{1,0:T(8,128)S(1)}, f32[32,128]{1,0:T(8,128)S(1)}, u32[]{:S(2)}, u32[]{:S(2)}) collective-permute-start(f32[32,128]{1,0:T(8,128)S(1)} %pad_maximum_fusion.1), channel_id=1, source_target_pairs={{48,96},{96,48},{49,97},{97,49},{50,98},{98,50},{51,99},{99,51},{5... | collective-permute-start | bytes 49160 | tf_op jit(solution)/shard_map/ppermute | solution.py:276
  24.9 1.9 %collective-permute-start.81 = (f32[32,128]{1,0:T(8,128)S(1)}, f32[32,128]{1,0:T(8,128)S(1)}, u32[]{:S(2)}, u32[]{:S(2)}) collective-permute-start(f32[32,128]{1,0:T(8,128)S(1)} %pad_maximum_fusion), channel_id=1, source_target_pairs={{0,48},{48,0},{1,49},{49,1},{2,50},{50,2},{3,51},{51,3},{4,52},{52... | collective-permute-start | bytes 49160 | tf_op jit(solution)/shard_map/ppermute | solution.py:275
  26.8 3.3 %conditional.1 = (f32[144,128]{1,0:T(8,128)}, f32[144,128]{1,0:T(8,128)}, f32[144,128]{1,0:T(8,128)}) conditional(s32[]{:T(128)} %bitcast, f32[144,128]{1,0:T(8,128)S(1)} %get-tuple-element.51.y_rows, f32[144,128]{1,0:T(8,128)S(1)} %get-tuple-element.51.y_rows, f32[144,128]{1,0:T(8,128)S(1)} %get-tuple-element.51.y_rows, ...), branch_computations={%region_0.0_spmd, %region_1.0_spmd, %region_2.0_spmd, %region_3.0_... | conditional | bytes 884880 | solution.py:288
  26.9 1.3 %collective-permute-start.75 = (f32[144,128]{1,0:T(8,128)S(1)}, f32[144,128]{1,0:T(8,128)}, u32[]{:S(2)}, u32[]{:S(2)}) collective-permute-start(f32[144,128]{1,0:T(8,128)S(1)} %param.30), channel_id=1, source_target_pairs={{767,47},{719,95},{671,143},{623,191},{575,239},{527,287},{479,335... | collective-permute-start | bytes 221192 | tf_op jit(solution)/shard_map/cond/branch_30_fun/ppermute | solution.py:280
  28.2 1.3 %collective-permute-start.76 = (f32[144,128]{1,0:T(8,128)S(1)}, f32[144,128]{1,0:T(8,128)}, u32[]{:S(2)}, u32[]{:S(2)}) collective-permute-start(f32[144,128]{1,0:T(8,128)S(1)} %param.30), channel_id=1, source_target_pairs={{719,47},{671,95},{623,143},{575,191},{527,239},{479,287},{431,335... | collective-permute-start | bytes 221192 | tf_op jit(solution)/shard_map/cond/branch_30_fun/ppermute | solution.py:281
  29.4 0.0 collective-permute-done.75
  29.5 0.0 collective-permute-done.76
  29.5 0.6 %broadcast.47 = f32[144,128]{1,0:T(8,128)} broadcast(f32[]{:T(128)} %constant.32.clone), dimensions={} | broadcast | bytes 73732 | tf_op jit(solution)/shard_map/broadcast.31
  30.1 5.6 %collective-permute-done.81.first.refs_2_ = f32[32,128]{1,0:T(8,128)S(1)} collective-permute-done((f32[32,128]{1,0:T(8,128)S(1)}, f32[32,128]{1,0:T(8,128)S(1)}, u32[]{:S(2)}, u32[]{:S(2)}) %collective-permute-start.81) | collective-permute-done | bytes 16416 | tf_op jit(solution)/shard_map/ppermute | solution.py:275
  35.7 4.0 %collective-permute-start.83 = (f32[208,128]{1,0:T(8,128)S(1)}, f32[208,128]{1,0:T(8,128)S(1)}, u32[]{:S(2)}, u32[]{:S(2)}) collective-permute-start(f32[208,128]{1,0:T(8,128)S(1)} %get-tuple-element.53), channel_id=1, source_target_pairs={{0,1},{1,0},{2,3},{3,2},{4,5},{5,4},{6,7},{7,6},{8,9},{9,8},{10,11... | collective-permute-start | bytes 319496 | tf_op jit(solution)/shard_map/ppermute | solution.py:296
  39.7 2.9 %collective-permute-start.84 = (f32[176,128]{1,0:T(8,128)S(1)}, f32[176,128]{1,0:T(8,128)S(1)}, u32[]{:S(2)}, u32[]{:S(2)}) collective-permute-start(f32[176,128]{1,0:T(8,128)S(1)} %get-tuple-element.54), channel_id=1, source_target_pairs={{1,2},{2,1},{3,4},{4,3},{5,6},{6,5},{7,8},{8,7},{9,10},{10,9},{11,... | collective-permute-start | bytes 270344 | tf_op jit(solution)/shard_map/ppermute | solution.py:297
  42.6 5.0 %collective-permute-done.84.refs_5_ = f32[176,128]{1,0:T(8,128)S(1)} collective-permute-done((f32[176,128]{1,0:T(8,128)S(1)}, f32[176,128]{1,0:T(8,128)S(1)}, u32[]{:S(2)}, u32[]{:S(2)}) %collective-permute-start.84) | collective-permute-done | bytes 90144 | tf_op jit(solution)/shard_map/ppermute | solution.py:297
  47.7 0.0 collective-permute-done.83.refs_4_
  47.7 3.3 %shard_map.75 = f32[2,16,256]{2,1,0:T(8,128)} custom-call(s32[2]{0:T(128)S(1)} %get-tuple-element.47.refs_0_, f32[7,16,256]{2,1,0:T(8,128)S(1)} %get-tuple-element.48.refs_1_, f32[32,128]{1,0:T(8,128)S(1)} %collective-permute-done.81.first.refs_2_, f32[32,128]{1,0:T(8,128)S(1)} %collective-permute-done.82.second.refs_3_, ...), custom_call_target="tpu_custom_call" | custom-call | tf_op jit(solution)/shard_map/pallas_call | solution.py:302
  (15 shorter events, 0.0 us)
Async XLA Ops:
  0.0 0.7 %copy-start = (f32[16,256]{1,0:T(8,128)S(1)}, f32[16,256]{1,0:T(8,128)}, u32[]{:S(2)}) copy-start(f32[16,256]{1,0:T(8,128)} %refs_9_.1) | copy-start | bytes 49156
  0.7 0.8 %copy-start.2 = (f32[2,16,256]{2,1,0:T(8,128)S(1)}, f32[2,16,256]{2,1,0:T(8,128)}, u32[]{:S(2)}) copy-start(f32[2,16,256]{2,1,0:T(8,128)} %grad.1) | copy-start | bytes 98308
  1.5 0.8 %copy-start.3 = (f32[2,16,256]{2,1,0:T(8,128)S(1)}, f32[2,16,256]{2,1,0:T(8,128)}, u32[]{:S(2)}) copy-start(f32[2,16,256]{2,1,0:T(8,128)} %norm.1) | copy-start | bytes 98308
  2.2 0.8 %copy-start.4 = (f32[2,16,256]{2,1,0:T(8,128)S(1)}, f32[2,16,256]{2,1,0:T(8,128)}, u32[]{:S(2)}) copy-start(f32[2,16,256]{2,1,0:T(8,128)} %de.1) | copy-start | bytes 98308
  3.0 0.8 %copy-start.5 = (f32[2,16,256]{2,1,0:T(8,128)S(1)}, f32[2,16,256]{2,1,0:T(8,128)}, u32[]{:S(2)}) copy-start(f32[2,16,256]{2,1,0:T(8,128)} %dn.1) | copy-start | bytes 98308
  3.8 0.7 %copy-start.6 = (s32[4096]{0:T(1024)S(1)}, s32[4096]{0:T(1024)}, u32[]{:S(2)}) copy-start(s32[4096]{0:T(1024)} %partner.1) | copy-start | bytes 49156
  4.5 0.7 %copy-start.7 = (s32[16,256]{1,0:T(8,128)S(1)}, s32[16,256]{1,0:T(8,128)}, u32[]{:S(2)}) copy-start(s32[16,256]{1,0:T(8,128)} %mask.1) | copy-start | bytes 49156
  6.4 0.7 %collective-permute-start.80 = (f32[32,128]{1,0:T(8,128)S(1)}, f32[32,128]{1,0:T(8,128)S(1)}, u32[]{:S(2)}, u32[]{:S(2)}) collective-permute-start(f32[32,128]{1,0:T(8,128)S(1)} %get-tuple-element.49), channel_id=1, source_target_pairs={{47,46},{95,94},{143,142},{191,190},{239,238},{287,286},{335,334},... | collective-permute-start | bytes 49160 | tf_op jit(solution)/shard_map/ppermute | solution.py:274
  7.1 23.0 %collective-permute-start.82 = (f32[32,128]{1,0:T(8,128)S(1)}, f32[32,128]{1,0:T(8,128)S(1)}, u32[]{:S(2)}, u32[]{:S(2)}) collective-permute-start(f32[32,128]{1,0:T(8,128)S(1)} %pad_maximum_fusion.1), channel_id=1, source_target_pairs={{48,96},{96,48},{49,97},{97,49},{50,98},{98,50},{51,99},{99,51},{5... | collective-permute-start | bytes 49160 | tf_op jit(solution)/shard_map/ppermute | solution.py:276
  24.9 10.8 %collective-permute-start.81 = (f32[32,128]{1,0:T(8,128)S(1)}, f32[32,128]{1,0:T(8,128)S(1)}, u32[]{:S(2)}, u32[]{:S(2)}) collective-permute-start(f32[32,128]{1,0:T(8,128)S(1)} %pad_maximum_fusion), channel_id=1, source_target_pairs={{0,48},{48,0},{1,49},{49,1},{2,50},{50,2},{3,51},{51,3},{4,52},{52... | collective-permute-start | bytes 49160 | tf_op jit(solution)/shard_map/ppermute | solution.py:275
  26.9 2.6 %collective-permute-start.75 = (f32[144,128]{1,0:T(8,128)S(1)}, f32[144,128]{1,0:T(8,128)}, u32[]{:S(2)}, u32[]{:S(2)}) collective-permute-start(f32[144,128]{1,0:T(8,128)S(1)} %param.30), channel_id=1, source_target_pairs={{767,47},{719,95},{671,143},{623,191},{575,239},{527,287},{479,335... | collective-permute-start | bytes 221192 | tf_op jit(solution)/shard_map/cond/branch_30_fun/ppermute | solution.py:280
  28.2 1.3 %collective-permute-start.76 = (f32[144,128]{1,0:T(8,128)S(1)}, f32[144,128]{1,0:T(8,128)}, u32[]{:S(2)}, u32[]{:S(2)}) collective-permute-start(f32[144,128]{1,0:T(8,128)S(1)} %param.30), channel_id=1, source_target_pairs={{719,47},{671,95},{623,143},{575,191},{527,239},{479,287},{431,335... | collective-permute-start | bytes 221192 | tf_op jit(solution)/shard_map/cond/branch_30_fun/ppermute | solution.py:281
  35.7 12.0 %copy-start.1 = (f32[16,256]{1,0:T(8,128)S(1)}, f32[16,256]{1,0:T(8,128)}, u32[]{:S(2)}) copy-start(f32[16,256]{1,0:T(8,128)} %refs_9_.1) | copy-start | bytes 49156
  35.7 12.0 %collective-permute-start.83 = (f32[208,128]{1,0:T(8,128)S(1)}, f32[208,128]{1,0:T(8,128)S(1)}, u32[]{:S(2)}, u32[]{:S(2)}) collective-permute-start(f32[208,128]{1,0:T(8,128)S(1)} %get-tuple-element.53), channel_id=1, source_target_pairs={{0,1},{1,0},{2,3},{3,2},{4,5},{5,4},{6,7},{7,6},{8,9},{9,8},{10,11... | collective-permute-start | bytes 319496 | tf_op jit(solution)/shard_map/ppermute | solution.py:296
  39.7 8.0 %collective-permute-start.84 = (f32[176,128]{1,0:T(8,128)S(1)}, f32[176,128]{1,0:T(8,128)S(1)}, u32[]{:S(2)}, u32[]{:S(2)}) collective-permute-start(f32[176,128]{1,0:T(8,128)S(1)} %get-tuple-element.54), channel_id=1, source_target_pairs={{1,2},{2,1},{3,4},{4,3},{5,6},{6,5},{7,8},{8,7},{9,10},{10,9},{11,... | collective-permute-start | bytes 270344 | tf_op jit(solution)/shard_map/ppermute | solution.py:297

commit v3 on v2

v3 whole, which is shorter than its diff:
```python
import functools

import jax
import jax.numpy as jnp
from jax import lax
from jax.experimental import pallas as pl
from jax.experimental.pallas import tpu as pltpu
from jax.sharding import PartitionSpec as P

ITERS = 10
LANES = 128
TILE = 8
PER_ROW = LANES // ITERS
AXES = ("lon", "lat")


def lane_index(rows=TILE):
    return lax.broadcasted_iota(jnp.int32, (rows, LANES), 1)


def slots(arrays):
    places = [(k, t) for k in range(arrays) for t in range(2)]
    return [(k, t, m // PER_ROW, (m % PER_ROW) * ITERS) for m, (k, t) in enumerate(places)]


def pack_kernel(*refs):
    sources, (block, edges, x_rows, y_rows, area_out, root, place) = refs[:7], refs[7:14]
    held, (grad, norm, de, dn, area, mask), arrived = refs[14], refs[15:21], refs[21]
    levels, rows, cols = grad.shape
    arrays = block.shape[0]
    copies = [
        pltpu.make_async_copy(source, target, arrived.at[n])
        for n, (source, target) in enumerate(zip(sources[1:], (grad, norm, de, dn, area, mask)))
    ]
    copies.append(
        pltpu.make_async_copy(sources[0].at[pl.ds(0, held.shape[0])], held, arrived.at[len(copies)])
    )
    for copy in copies:
        copy.start()
    for copy in copies:
        copy.wait()
    block[0:levels] = norm[...] * grad[...]
    block[levels : 2 * levels] = de[...]
    block[2 * levels : 3 * levels] = dn[...]
    block[3 * levels] = mask[...].astype(jnp.float32) / area[...]
    area_out[...] = area[...]
    root[...] = jnp.sqrt(area[...])
    lane = lane_index()
    lat_even = lax.rem(lax.axis_index("lat"), 2) == 0

    def packed(col, first):
        out = {}
        for k, t, row, at in slots(arrays):
            tile = block[k, t * TILE : (t + 1) * TILE, col : col + LANES]
            moved = pltpu.roll(tile, (at - first) % LANES, 1)
            inside = (lane >= at) & (lane < at + ITERS)
            out[row] = jnp.where(inside, moved, out.get(row, jnp.zeros_like(moved)))
        return out

    east, west = packed(cols - LANES, LANES - ITERS), packed(0, 0)
    count = len(east)
    for row in range(count):
        here = slice(row * TILE, (row + 1) * TILE)
        there = slice((count + row) * TILE, (count + row + 1) * TILE)
        edges[here], edges[there] = east[row], west[row]

    sub = lax.broadcasted_iota(jnp.int32, (TILE, LANES), 0)
    for c in range(cols // LANES):
        at = slice(c * LANES, (c + 1) * LANES)
        base = c * (arrays + 2) * TILE
        extra = {}
        for k in range(arrays):
            low, high = block[k, 0:TILE, at], block[k, TILE : 2 * TILE, at]
            here = slice(base + k * TILE, base + (k + 1) * TILE)
            x_rows[here] = jnp.where(lat_even, high, low)
            y_rows[here] = jnp.where(lat_even, low, high)
            lift = 2 * (k % 4)
            inside = (sub >= lift) & (sub < lift + 2)
            north = pltpu.roll(low, (lift + 2) % TILE, 0)
            south = pltpu.roll(high, lift, 0)
            north_held, south_held = extra.get(k // 4, (jnp.zeros_like(low),) * 2)
            extra[k // 4] = (jnp.where(inside, north, north_held), jnp.where(inside, south, south_held))
        for e, (north, south) in extra.items():
            here = slice(base + (arrays + e) * TILE, base + (arrays + e + 1) * TILE)
            x_rows[here] = jnp.where(lat_even, north, south)
            y_rows[here] = jnp.where(lat_even, south, north)
    moved = held[0] + ITERS
    q = lax.rem(lax.div(moved, cols), lax.axis_size("lon"))
    offset = lax.rem(moved, cols) - ITERS
    place[...] = jnp.full((TILE, LANES), jnp.where(lax.broadcasted_iota(jnp.int32, (TILE, LANES), 1) == 0, 2 * q + jnp.where(offset < ITERS - 1, 1, 0), offset))


def join_kernel(edges, mate, to_east, to_west):
    half = edges.shape[0] // 2
    low, high = slice(0, half), slice(half, 2 * half)
    to_east[low], to_west[low] = edges[low], edges[high]
    to_east[high], to_west[high] = mate[low], mate[high]


def after_kernel(count, *refs):
    for source, target in zip(refs[:count], refs[-count:]):
        target[...] = source[...]


def near_kernel(x_rows, y_rows, even_east, even_west, odd_east, odd_west, x_out, y_out):
    rows, tall = x_rows.shape[0], even_east.shape[0]
    half = tall // 2
    lon_even = lax.rem(lax.axis_index("lon"), 2) == 0
    x_out[0:rows] = x_rows[...]
    y_out[0:rows] = y_rows[...]
    east = jnp.where(lon_even, even_east[...], odd_east[...])
    west = jnp.where(lon_even, even_west[...], odd_west[...])
    x_out[rows : rows + tall] = east
    x_out[rows + tall : rows + 2 * tall] = west
    y_out[rows : rows + half] = east[0:half]
    y_out[rows + half : rows + tall] = west[0:half]


def reversed_lanes(x):
    index = LANES - 1 - lane_index(x.shape[0])
    return jnp.take_along_axis(x, index, axis=1, mode="promise_in_bounds")


def fold_kernel(levels, place, f0, f1, f2, out, placed, arrived):
    copy = pltpu.make_async_copy(place, placed, arrived)
    copy.start()
    arrays, rows, wide = out.shape
    cols = wide - LANES
    tiles_across = cols // LANES
    band = (arrays + 2) * TILE
    copy.wait()
    offset = placed[0, 1]
    span = 3 * cols
    far = lane_index(rows)
    for k in range(arrays):
        east_face = levels <= k < 2 * levels
        north_face = 2 * levels <= k < 3 * levels
        pieces = []
        for f in (f0, f1, f2):
            for c in range(tiles_across - 1, -1, -1):
                main = f[c * band + k * TILE : c * band + (k + 1) * TILE]
                few = f[c * band + (arrays + k // 4) * TILE : c * band + (arrays + k // 4 + 1) * TILE]
                few = pltpu.roll(few, (TILE - 2 - 2 * (k % 4)) % TILE, 0)
                pieces.append(reversed_lanes(jnp.concatenate([few, main], axis=0)))
        shift = offset + span - cols + (0 if east_face else 1)
        turned = pltpu.roll(jnp.concatenate(pieces, axis=1), shift, 1)
        beyond = turned[:, cols : cols + LANES]
        before = turned[:, span - LANES :]
        side = jnp.where(far < ITERS, beyond, jnp.where(far >= LANES - ITERS, before, 0.0))
        mirrored = jnp.concatenate([turned[:, :cols], side], axis=1)
        skip = 1 if north_face else 0
        for row in range(rows - 1):
            source = max(rows - 1 - skip - row, 0)
            out[k, row : row + 1] = mirrored[source : source + 1]
        out[k, rows - 1 : rows] = mirrored[rows - 1 : rows]


def steps_kernel(levels, own, x_out, x_in, y_in, area, root, mirrored, out, ext):
    arrays, rows, cols = own.shape
    wide, tall = cols + LANES, 3 * rows
    tiles_across = cols // LANES
    band = (arrays + 2) * TILE
    data = band * tiles_across
    edge = (x_in.shape[0] - data) // 4
    lat = lax.axis_index("lat")
    lat_even = lax.rem(lat, 2) == 0
    at_top = lat == lax.axis_size("lat") - 1
    below_top = lat == lax.axis_size("lat") - 2
    lane = lane_index()

    def put_sides(start, from_east, from_west):
        for k, t, row, at in slots(arrays):
            here = slice(row * TILE, (row + 1) * TILE)
            east = pltpu.roll(from_east[here], (-at) % LANES, 1)
            west = pltpu.roll(from_west[here], (LANES - ITERS - at) % LANES, 1)
            side = jnp.where(lane < ITERS, east, jnp.where(lane >= LANES - ITERS, west, 0.0))
            ext[k, start + t * TILE : start + (t + 1) * TILE, cols:wide] = side

    def put_rows(start, main, spare, lift_base, rows_of):
        for c in range(tiles_across):
            at = slice(c * LANES, (c + 1) * LANES)
            for k in range(arrays):
                base = c * band
                ext[k, start + main * TILE : start + (main + 1) * TILE, at] = rows_of(base + k * TILE)
                few = rows_of(base + (arrays + k // 4) * TILE)
                lift = (lift_base - 2 * (k % 4)) % TILE
                ext[k, start + spare * TILE : start + (spare + 1) * TILE, at] = pltpu.roll(few, lift, 0)

    for k in range(arrays):
        ext[k, rows : 2 * rows, 0:cols] = own[k]
    def part(held, at):
        return held[data + at * edge : data + (at + 1) * edge]

    x_east, x_west = part(x_in, 0), part(x_in, 2)
    y_east, y_west = part(y_in, 0), part(y_in, 1)
    put_sides(
        rows,
        jnp.where(at_top, part(x_in, 1), part(x_out, 0)),
        jnp.where(at_top, part(x_in, 3), part(x_out, 2)),
    )

    def south_rows(at):
        return jnp.where(lat_even, y_in[at : at + TILE], x_in[at : at + TILE])

    def north_rows(at):
        return jnp.where(lat_even, x_in[at : at + TILE], y_in[at : at + TILE])

    put_rows(0, 1, 0, TILE - 2, south_rows)
    put_sides(0, jnp.where(lat_even, y_east, x_east), jnp.where(lat_even, y_west, x_west))

    @pl.when(jnp.logical_not(at_top))
    def _():
        put_rows(2 * rows, 0, 1, 0, north_rows)
        put_sides(
            2 * rows,
            jnp.where(below_top, part(x_out, 1), jnp.where(lat_even, x_east, y_east)),
            jnp.where(below_top, part(x_out, 3), jnp.where(lat_even, x_west, y_west)),
        )

    @pl.when(at_top)
    def _():
        for k in range(arrays):
            ext[k, 2 * rows : 3 * rows] = mirrored[k]
        for k in range(2 * levels, 3 * levels):
            face = ext[k, 2 * rows - 1 : 2 * rows]
            ext[k, 2 * rows - 1 : 2 * rows] = 0.5 * (face + mirrored[k, rows - 1 : rows])

    def east_of(x):
        return pltpu.roll(x, wide - 1, 1)

    def west_of(x):
        return pltpu.roll(x, 1, 1)

    def north_of(x):
        return pltpu.roll(x, x.shape[0] - 1, 0)

    def south_of(x):
        return pltpu.roll(x, 1, 0)

    weight = ext[3 * levels]
    sea = jnp.where(weight > 0.0, 1.0, 0.0)
    sea_east = sea * east_of(sea)
    sea_north = sea * north_of(sea)
    inner = slice(TILE, tall - TILE)
    coefs, values = [], []
    for level in range(levels):
        east = ext[levels + level] * sea_east
        north = ext[2 * levels + level] * sea_north
        west, south = west_of(east), south_of(north)
        rest = 1.0 - weight * ((east + west) + (north + south))
        coefs.append([rest] + [weight * x for x in (east, west, north, south)])
        values.append(weight * ext[level])
    for turn in range(ITERS):
        for level in range(levels):
            u = values[level]
            rest, east, west, north, south = coefs[level]
            u = (rest * u + (east * east_of(u) + west * west_of(u))) + (
                north * north_of(u) + south * south_of(u)
            )
            if turn == 1:
                u = u[inner]
                coefs[level] = [x[inner] for x in coefs[level]]
            values[level] = u
    start = rows - TILE
    own_weight = weight[rows : 2 * rows, :cols]
    for level in range(levels):
        u = values[level][start : start + rows, :cols]
        state = jnp.where(own_weight > 0.0, u * area[...], own[level])
        out[level] = state / root[...]


VMEM = pl.BlockSpec(memory_space=pltpu.VMEM)
SMEM = pl.BlockSpec(memory_space=pltpu.SMEM)
ANY = pl.BlockSpec(memory_space=pl.ANY)
HBM = pl.BlockSpec(memory_space=pltpu.HBM)
PARAMS = pltpu.CompilerParams(vmem_limit_bytes=8 * 1024 * 1024)


def per_device(gradient, norm_factor, diff_east, diff_north, cell_area, sea_mask, partner):
    levels, rows, cols = gradient.shape
    arrays = 3 * levels + 1
    lon_count, lat_count = lax.axis_size("lon"), lax.axis_size("lat")

    def held(*shape):
        return jax.ShapeDtypeStruct(shape, jnp.float32)

    inputs = (gradient, norm_factor, diff_east, diff_north, cell_area, sea_mask)
    edge = (slots(arrays)[-1][2] + 1) * TILE
    data = (arrays + 2) * TILE * (cols // LANES)
    block, edges, x_rows, y_rows, copied_area, root, place = pl.pallas_call(
        pack_kernel,
        out_shape=(
            held(arrays, rows, cols),
            held(2 * edge, LANES),
            held(data, LANES),
            held(data, LANES),
            held(rows, cols),
            held(rows, cols),
            jax.ShapeDtypeStruct((TILE, LANES), jnp.int32),
        ),
        in_specs=[HBM] * 7,
        out_specs=(VMEM,) * 7,
        scratch_shapes=[pltpu.SMEM((LANES,), jnp.int32)]
        + [pltpu.VMEM(x.shape, x.dtype) for x in inputs]
        + [pltpu.SemaphoreType.DMA((7,))],
        compiler_params=PARAMS,
    )(*[pltpu.with_memory_space_constraint(x, pltpu.HBM) for x in (partner, *inputs)])

    def flat(lon, lat):
        return (lon % lon_count) * lat_count + lat

    top = lat_count - 1
    around = range(lon_count)

    def swap(pairs):
        return [pair for a, b in pairs for pair in ((a, b), (b, a))]

    def sent(start, step):
        return [(flat(p, i), flat(p + step, i)) for p in around[start::2] for i in range(top)]

    def lat_swap(start):
        return swap([(flat(p, i), flat(p, i + 1)) for p in around for i in range(start, top, 2)])

    def mirror(total):
        return [(flat(total - p, top), flat(p, top)) for p in around]

    mate = lax.ppermute(edges, AXES, [(flat(p, top), flat(p, top - 1)) for p in around])
    to_east, to_west = pl.pallas_call(
        join_kernel,
        out_shape=(held(2 * edge, LANES),) * 2,
        in_specs=[VMEM] * 2,
        out_specs=(VMEM,) * 2,
        compiler_params=PARAMS,
    )(edges, mate)
    even_east = lax.ppermute(to_west, AXES, sent(1, -1))
    even_west = lax.ppermute(to_east, AXES, sent(1, 1))

    def after(values, first):
        return pl.pallas_call(
            functools.partial(after_kernel, len(values)),
            out_shape=tuple(jax.ShapeDtypeStruct(x.shape, x.dtype) for x in values),
            in_specs=[VMEM] * len(values) + [ANY] * len(first),
            out_specs=(VMEM,) * len(values),
            compiler_params=PARAMS,
        )(*values, *first)

    mirrored_shape = (arrays, rows, cols + LANES)

    def fold(total, third):
        def run(place, x):
            f0 = lax.ppermute(x, AXES, mirror(total))
            f1 = lax.ppermute(x, AXES, mirror(total - 1))
            f2 = lax.ppermute(x, AXES, mirror(total - 2)) if third else x
            return pl.pallas_call(
                functools.partial(fold_kernel, levels),
                out_shape=held(*mirrored_shape),
                in_specs=[ANY] + [VMEM] * 3,
                out_specs=VMEM,
                scratch_shapes=[pltpu.SMEM((TILE, LANES), jnp.int32), pltpu.SemaphoreType.DMA],
                compiler_params=PARAMS,
            )(place, f0, f1, f2)

        return run

    def no_fold(place, x):
        return jnp.zeros(mirrored_shape, jnp.float32)

    (where,) = after((place,), (to_east,))
    chosen = jnp.where(lax.axis_index("lat") == top, where[0, 0] + 1, 0)
    folds = [fold(total, third) for total in around for third in (False, True)]
    mirrored = lax.switch(chosen, [no_fold] + folds, where, y_rows)
    go_east, go_west = after((to_east, to_west), (even_east, even_west, mirrored))
    odd_west = lax.ppermute(go_east, AXES, sent(0, 1))
    odd_east = lax.ppermute(go_west, AXES, sent(0, -1))
    x_out, y_out = pl.pallas_call(
        near_kernel,
        out_shape=(held(data + 4 * edge, LANES), held(data + 2 * edge, LANES)),
        in_specs=[VMEM] * 6,
        out_specs=(VMEM, VMEM),
        compiler_params=PARAMS,
    )(x_rows, y_rows, even_east, even_west, odd_east, odd_west)
    x_in = lax.ppermute(x_out, AXES, lat_swap(0))
    y_in = lax.ppermute(y_out, AXES, lat_swap(1))
    return pl.pallas_call(
        functools.partial(steps_kernel, levels),
        out_shape=held(levels, rows, cols),
        in_specs=[VMEM] * 7,
        out_specs=VMEM,
        scratch_shapes=[pltpu.VMEM((arrays, 3 * rows, cols + LANES), jnp.float32)],
        compiler_params=PARAMS,
    )(block, x_out, x_in, y_in, copied_area, root, mirrored)


def solution(mesh):
    return jax.shard_map(
        per_device,
        mesh=mesh,
        in_specs=(
            P(None, "lat", "lon"),
            P(None, "lat", "lon"),
            P(None, "lat", "lon"),
            P(None, "lat", "lon"),
            P("lat", "lon"),
            P("lat", "lon"),
            P(),
        ),
        out_specs=P(None, "lat", "lon"),
        check_vma=False,
    )
```

time: 51.7 us -> 41.9 us (0.81)
  the two profiles are of different devices: /device:TPU:7 before, /device:TPU:1 now
where the time goes in v3:
time: 41.9 us; the launch traced here: 41.6 us
  waiting for transfers between devices  20 us (48%)
  starting transfers between devices  17.3 us (41%)
  Pallas kernels  2.92 us (7%)
  between operations  0.78 us (2%)
  local copies, waits for them, and re-layouts  0.53 us (1%)
    ppermute x1, waiting for transfers between devices, per_device(): even_west = lax.ppermute(to_east, AXES, sent(1, 1))  15.2 us
    ppermute x1, starting transfers between devices, per_device(): x_in = lax.ppermute(x_out, AXES, lat_swap(0))  7.47 us
    ppermute x1, waiting for transfers between devices, per_device(): y_in = lax.ppermute(y_out, AXES, lat_swap(1))  3.92 us
    ppermute x1, starting transfers between devices, per_device(): odd_east = lax.ppermute(go_west, AXES, sent(0, -1))  3.41 us
    ppermute x1, starting transfers between devices, per_device(): y_in = lax.ppermute(y_out, AXES, lat_swap(1))  1.92 us
    pallas_call x1, Pallas kernels, per_device(): pl.pallas_call(functools.partial(steps_kernel, levels), out_shape=held(le...  1.92 us
    ppermute x1, starting transfers between devices, per_device(): even_west = lax.ppermute(to_east, AXES, sent(1, 1))  1.29 us
    ppermute x1, starting transfers between devices, per_device(): even_east = lax.ppermute(to_west, AXES, sent(1, -1))  1.29 us
  transfers between devices with their start and end apart: 7, of which 3 were waited for; matrix products, arithmetic and copies ran while one was open for 1% of the time, Pallas kernels for 0%

profile of v3, /device:TPU:1, one launch (start us, length us, event | category | flops | bytes accessed | tf_op | source)
XLA Modules:
  0.0 41.6 jit_solution(1296995285237878135)
XLA Ops:
  0.0 1.0 %shard_map.73 = (f32[7,16,256]{2,1,0:T(8,128)S(1)}, f32[32,128]{1,0:T(8,128)S(1)}, f32[144,128]{1,0:T(8,128)S(1)}, f32[144,128]{1,0:T(8,128)S(1)}, f32[16,256]{1...) custom-call(s32[4096]{0:T(1024)} %refs_0_.1, f32[2,16,256]{2,1,0:T(8,128)} %refs_1_.1, ...), custom_call_target="tpu_custom_call" | custom-call | tf_op jit(solution)/shard_map/pallas_call | solution.py:290
  1.0 0.7 %collective-permute-start.80 = (f32[32,128]{1,0:T(8,128)S(1)}, f32[32,128]{1,0:T(8,128)S(1)}, u32[]{:S(2)}, u32[]{:S(2)}) collective-permute-start(f32[32,128]{1,0:T(8,128)S(1)} %get-tuple-element.247.edges), channel_id=1, source_target_pairs={{47,46},{95,94},{143,142},{191,190},{239,238},{287,286},{335,334},... | collective-permute-start | bytes 49160 | tf_op jit(solution)/shard_map/ppermute | solution.py:327
  1.7 0.0 collective-permute-done.80.mate
  1.7 1.3 %collective-permute-start.82 = (f32[32,128]{1,0:T(8,128)S(1)}, f32[32,128]{1,0:T(8,128)S(1)}, u32[]{:S(2)}, u32[]{:S(2)}) collective-permute-start(f32[32,128]{1,0:T(8,128)S(1)} %get-tuple-element.249.refs_1_.refs_0_), channel_id=1, source_target_pairs={{48,96},{49,97},{50,98},{51,99},{52,100},{53,101},{54,102},{55,103... | collective-permute-start | bytes 49160 | tf_op jit(solution)/shard_map/ppermute | solution.py:336
  3.0 1.3 %collective-permute-start.81 = (f32[32,128]{1,0:T(8,128)S(1)}, f32[32,128]{1,0:T(8,128)S(1)}, u32[]{:S(2)}, u32[]{:S(2)}) collective-permute-start(f32[32,128]{1,0:T(8,128)S(1)} %get-tuple-element.248.refs_1_), channel_id=1, source_target_pairs={{48,0},{49,1},{50,2},{51,3},{52,4},{53,5},{54,6},{55,7},{56,8},{57... | collective-permute-start | bytes 49160 | tf_op jit(solution)/shard_map/ppermute | solution.py:335
  4.3 0.5 %slice.3 = s32[1,1]{1,0:T(1,128)} slice(s32[8,128]{1,0:T(8,128)S(1)} %shard_map.75), slice={[0:1], [0:1]} | slice | bytes 8 | tf_op jit(solution)/shard_map/slice | solution.py:369
  5.5 0.1 conditional.1
  5.6 15.2 %collective-permute-done.82.refs_3_.even_west = f32[32,128]{1,0:T(8,128)S(1)} collective-permute-done((f32[32,128]{1,0:T(8,128)S(1)}, f32[32,128]{1,0:T(8,128)S(1)}, u32[]{:S(2)}, u32[]{:S(2)}) %collective-permute-start.82) | collective-permute-done | bytes 16416 | tf_op jit(solution)/shard_map/ppermute | solution.py:336
  20.8 0.0 collective-permute-done.81.refs_2_.even_east
  20.8 3.4 %collective-permute-start.83 = (f32[32,128]{1,0:T(8,128)S(1)}, f32[32,128]{1,0:T(8,128)S(1)}, u32[]{:S(2)}, u32[]{:S(2)}) collective-permute-start(f32[32,128]{1,0:T(8,128)S(1)} %get-tuple-element.251), channel_id=1, source_target_pairs={{0,720},{1,721},{2,722},{3,723},{4,724},{5,725},{6,726},{7,727},{8... | collective-permute-start | bytes 49160 | tf_op jit(solution)/shard_map/ppermute | solution.py:374
  24.2 1.3 %collective-permute-start.84 = (f32[32,128]{1,0:T(8,128)S(1)}, f32[32,128]{1,0:T(8,128)S(1)}, u32[]{:S(2)}, u32[]{:S(2)}) collective-permute-start(f32[32,128]{1,0:T(8,128)S(1)} %get-tuple-element.252), channel_id=1, source_target_pairs={{0,48},{1,49},{2,50},{3,51},{4,52},{5,53},{6,54},{7,55},{8,56},{9,... | collective-permute-start | bytes 49160 | tf_op jit(solution)/shard_map/ppermute | solution.py:373
  25.5 0.0 collective-permute-done.83.odd_east
  25.5 0.8 %collective-permute-done.84.odd_west = f32[32,128]{1,0:T(8,128)S(1)} collective-permute-done((f32[32,128]{1,0:T(8,128)S(1)}, f32[32,128]{1,0:T(8,128)S(1)}, u32[]{:S(2)}, u32[]{:S(2)}) %collective-permute-start.84) | collective-permute-done | bytes 16416 | tf_op jit(solution)/shard_map/ppermute | solution.py:373
  26.4 7.5 %collective-permute-start.85 = (f32[208,128]{1,0:T(8,128)S(1)}, f32[208,128]{1,0:T(8,128)S(1)}, u32[]{:S(2)}, u32[]{:S(2)}) collective-permute-start(f32[208,128]{1,0:T(8,128)S(1)} %get-tuple-element.253.x_out), channel_id=1, source_target_pairs={{0,1},{1,0},{2,3},{3,2},{4,5},{5,4},{6,7},{7,6},{8,9},{9,8},{10,11... | collective-permute-start | bytes 319496 | tf_op jit(solution)/shard_map/ppermute | solution.py:382
  33.8 1.9 %collective-permute-start.86 = (f32[176,128]{1,0:T(8,128)S(1)}, f32[176,128]{1,0:T(8,128)S(1)}, u32[]{:S(2)}, u32[]{:S(2)}) collective-permute-start(f32[176,128]{1,0:T(8,128)S(1)} %get-tuple-element.254), channel_id=1, source_target_pairs={{1,2},{2,1},{3,4},{4,3},{5,6},{6,5},{7,8},{8,7},{9,10},{10,9},{11,... | collective-permute-start | bytes 270344 | tf_op jit(solution)/shard_map/ppermute | solution.py:383
  35.8 3.9 %collective-permute-done.86.y_in = f32[176,128]{1,0:T(8,128)S(1)} collective-permute-done((f32[176,128]{1,0:T(8,128)S(1)}, f32[176,128]{1,0:T(8,128)S(1)}, u32[]{:S(2)}, u32[]{:S(2)}) %collective-permute-start.86) | collective-permute-done | bytes 90144 | tf_op jit(solution)/shard_map/ppermute | solution.py:383
  39.7 0.0 collective-permute-done.85.x_in
  39.7 1.9 %shard_map.78 = f32[2,16,256]{2,1,0:T(8,128)} custom-call(f32[7,16,256]{2,1,0:T(8,128)S(1)} %get-tuple-element.244.own, f32[208,128]{1,0:T(8,128)S(1)} %get-tuple-element.253.x_out, f32[208,128]{1,0:T(8,128)S(1)} %collective-permute-done.85.x_in, f32[176,128]{1,0:T(8,128)S(1)} %collective-permute-done.86.y_in, f32[16,256]{1,0:T(8,128)S(1)} %get-tuple-element.255.area, ...), custom_call_target="tpu_custom_call" | custom-call | tf_op jit(solution)/shard_map/pallas_call | solution.py:384
  (5 shorter events, 0.0 us)
Async XLA Ops:
  1.0 0.7 %collective-permute-start.80 = (f32[32,128]{1,0:T(8,128)S(1)}, f32[32,128]{1,0:T(8,128)S(1)}, u32[]{:S(2)}, u32[]{:S(2)}) collective-permute-start(f32[32,128]{1,0:T(8,128)S(1)} %get-tuple-element.247.edges), channel_id=1, source_target_pairs={{47,46},{95,94},{143,142},{191,190},{239,238},{287,286},{335,334},... | collective-permute-start | bytes 49160 | tf_op jit(solution)/shard_map/ppermute | solution.py:327
  1.7 19.1 %collective-permute-start.82 = (f32[32,128]{1,0:T(8,128)S(1)}, f32[32,128]{1,0:T(8,128)S(1)}, u32[]{:S(2)}, u32[]{:S(2)}) collective-permute-start(f32[32,128]{1,0:T(8,128)S(1)} %get-tuple-element.249.refs_1_.refs_0_), channel_id=1, source_target_pairs={{48,96},{49,97},{50,98},{51,99},{52,100},{53,101},{54,102},{55,103... | collective-permute-start | bytes 49160 | tf_op jit(solution)/shard_map/ppermute | solution.py:336
  3.0 17.8 %collective-permute-start.81 = (f32[32,128]{1,0:T(8,128)S(1)}, f32[32,128]{1,0:T(8,128)S(1)}, u32[]{:S(2)}, u32[]{:S(2)}) collective-permute-start(f32[32,128]{1,0:T(8,128)S(1)} %get-tuple-element.248.refs_1_), channel_id=1, source_target_pairs={{48,0},{49,1},{50,2},{51,3},{52,4},{53,5},{54,6},{55,7},{56,8},{57... | collective-permute-start | bytes 49160 | tf_op jit(solution)/shard_map/ppermute | solution.py:335
  20.8 4.7 %collective-permute-start.83 = (f32[32,128]{1,0:T(8,128)S(1)}, f32[32,128]{1,0:T(8,128)S(1)}, u32[]{:S(2)}, u32[]{:S(2)}) collective-permute-start(f32[32,128]{1,0:T(8,128)S(1)} %get-tuple-element.251), channel_id=1, source_target_pairs={{0,720},{1,721},{2,722},{3,723},{4,724},{5,725},{6,726},{7,727},{8... | collective-permute-start | bytes 49160 | tf_op jit(solution)/shard_map/ppermute | solution.py:374
  24.2 2.1 %collective-permute-start.84 = (f32[32,128]{1,0:T(8,128)S(1)}, f32[32,128]{1,0:T(8,128)S(1)}, u32[]{:S(2)}, u32[]{:S(2)}) collective-permute-start(f32[32,128]{1,0:T(8,128)S(1)} %get-tuple-element.252), channel_id=1, source_target_pairs={{0,48},{1,49},{2,50},{3,51},{4,52},{5,53},{6,54},{7,55},{8,56},{9,... | collective-permute-start | bytes 49160 | tf_op jit(solution)/shard_map/ppermute | solution.py:373
  26.4 13.3 %collective-permute-start.85 = (f32[208,128]{1,0:T(8,128)S(1)}, f32[208,128]{1,0:T(8,128)S(1)}, u32[]{:S(2)}, u32[]{:S(2)}) collective-permute-start(f32[208,128]{1,0:T(8,128)S(1)} %get-tuple-element.253.x_out), channel_id=1, source_target_pairs={{0,1},{1,0},{2,3},{3,2},{4,5},{5,4},{6,7},{7,6},{8,9},{9,8},{10,11... | collective-permute-start | bytes 319496 | tf_op jit(solution)/shard_map/ppermute | solution.py:382
  33.8 5.8 %collective-permute-start.86 = (f32[176,128]{1,0:T(8,128)S(1)}, f32[176,128]{1,0:T(8,128)S(1)}, u32[]{:S(2)}, u32[]{:S(2)}) collective-permute-start(f32[176,128]{1,0:T(8,128)S(1)} %get-tuple-element.254), channel_id=1, source_target_pairs={{1,2},{2,1},{3,4},{4,3},{5,6},{6,5},{7,8},{8,7},{9,10},{10,9},{11,... | collective-permute-start | bytes 270344 | tf_op jit(solution)/shard_map/ppermute | solution.py:383

commit v4 on v3

--- a/solution.py
+++ b/solution.py
@@ -24,8 +24,8 @@
 
 
 def pack_kernel(*refs):
-    sources, (block, edges, x_rows, y_rows, area_out, root, place) = refs[:7], refs[7:14]
-    held, (grad, norm, de, dn, area, mask), arrived = refs[14], refs[15:21], refs[21]
+    sources, (block, edges, x_rows, y_rows, area_out, root, place, chosen) = refs[:7], refs[7:15]
+    held, (grad, norm, de, dn, area, mask), arrived = refs[15], refs[16:22], refs[22]
     levels, rows, cols = grad.shape
     arrays = block.shape[0]
     copies = [
@@ -87,7 +87,9 @@
     moved = held[0] + ITERS
     q = lax.rem(lax.div(moved, cols), lax.axis_size("lon"))
     offset = lax.rem(moved, cols) - ITERS
-    place[...] = jnp.full((TILE, LANES), jnp.where(lax.broadcasted_iota(jnp.int32, (TILE, LANES), 1) == 0, 2 * q + jnp.where(offset < ITERS - 1, 1, 0), offset))
+    place[...] = jnp.full((TILE, LANES), offset)
+    at_top = lax.axis_index("lat") == lax.axis_size("lat") - 1
+    chosen[...] = jnp.full((1,), jnp.where(at_top, 1 + 2 * q + jnp.where(offset < ITERS - 1, 1, 0), 0))
 
 
 def join_kernel(edges, mate, to_east, to_west):
@@ -102,18 +104,28 @@
         target[...] = source[...]
 
 
-def near_kernel(x_rows, y_rows, even_east, even_west, odd_east, odd_west, x_out, y_out):
-    rows, tall = x_rows.shape[0], even_east.shape[0]
+def after(values, *first):
+    values = values if isinstance(values, tuple) else (values,)
+    handed = pl.pallas_call(
+        functools.partial(after_kernel, len(values)),
+        out_shape=tuple(jax.ShapeDtypeStruct(x.shape, x.dtype) for x in values),
+        in_specs=[VMEM] * len(values) + [ANY] * len(first),
+        out_specs=(VMEM,) * len(values),
+        compiler_params=PARAMS,
+    )(*values, *first)
+    return handed if len(values) > 1 else handed[0]
+
+
+def near_kernel(x_rows, y_rows, east, west, x_out, y_out):
+    rows, tall = x_rows.shape[0], east.shape[0]
     half = tall // 2
-    lon_even = lax.rem(lax.axis_index("lon"), 2) == 0
     x_out[0:rows] = x_rows[...]
     y_out[0:rows] = y_rows[...]
-    east = jnp.where(lon_even, even_east[...], odd_east[...])
-    west = jnp.where(lon_even, even_west[...], odd_west[...])
-    x_out[rows : rows + tall] = east
-    x_out[rows + tall : rows + 2 * tall] = west
+    x_out[rows : rows + tall] = east[...]
+    x_out[rows + tall : rows + 2 * tall] = west[...]
     y_out[rows : rows + half] = east[0:half]
     y_out[rows + half : rows + tall] = west[0:half]
+    y_out[rows + tall : y_out.shape[0]] = jnp.zeros((y_out.shape[0] - rows - tall, LANES), jnp.float32)
 
 
 def reversed_lanes(x):
@@ -121,7 +133,9 @@
     return jnp.take_along_axis(x, index, axis=1, mode="promise_in_bounds")
 
 
-def fold_kernel(levels, place, f0, f1, f2, out, placed, arrived):
+def fold_kernel(levels, order, place, behind, first, second, third, out, placed, arrived):
+    del behind
+    blocks = dict(zip(order, (first, second, third)))
     copy = pltpu.make_async_copy(place, placed, arrived)
     copy.start()
     arrays, rows, wide = out.shape
@@ -129,17 +143,19 @@
     tiles_across = cols // LANES
     band = (arrays + 2) * TILE
     copy.wait()
-    offset = placed[0, 1]
+    offset = placed[0, 0]
     span = 3 * cols
     far = lane_index(rows)
+
     for k in range(arrays):
         east_face = levels <= k < 2 * levels
         north_face = 2 * levels <= k < 3 * levels
         pieces = []
-        for f in (f0, f1, f2):
+        for f in (blocks[n] for n in range(3)):
             for c in range(tiles_across - 1, -1, -1):
-                main = f[c * band + k * TILE : c * band + (k + 1) * TILE]
-                few = f[c * band + (arrays + k // 4) * TILE : c * band + (arrays + k // 4 + 1) * TILE]
+                main_at = c * band + k * TILE
+                few_at = c * band + (arrays + k // 4) * TILE
+                main, few = f[main_at : main_at + TILE], f[few_at : few_at + TILE]
                 few = pltpu.roll(few, (TILE - 2 - 2 * (k % 4)) % TILE, 0)
                 pieces.append(reversed_lanes(jnp.concatenate([few, main], axis=0)))
         shift = offset + span - cols + (0 if east_face else 1)
@@ -287,7 +303,7 @@
     inputs = (gradient, norm_factor, diff_east, diff_north, cell_area, sea_mask)
     edge = (slots(arrays)[-1][2] + 1) * TILE
     data = (arrays + 2) * TILE * (cols // LANES)
-    block, edges, x_rows, y_rows, copied_area, root, place = pl.pallas_call(
+    block, edges, x_rows, y_rows, copied_area, root, place, chosen = pl.pallas_call(
         pack_kernel,
         out_shape=(
             held(arrays, rows, cols),
@@ -297,9 +313,10 @@
             held(rows, cols),
             held(rows, cols),
             jax.ShapeDtypeStruct((TILE, LANES), jnp.int32),
+            jax.ShapeDtypeStruct((1,), jnp.int32),
         ),
         in_specs=[HBM] * 7,
-        out_specs=(VMEM,) * 7,
+        out_specs=(VMEM,) * 8,
         scratch_shapes=[pltpu.SMEM((LANES,), jnp.int32)]
         + [pltpu.VMEM(x.shape, x.dtype) for x in inputs]
         + [pltpu.SemaphoreType.DMA((7,))],
@@ -318,8 +335,10 @@
     def sent(start, step):
         return [(flat(p, i), flat(p + step, i)) for p in around[start::2] for i in range(top)]
 
-    def lat_swap(start):
-        return swap([(flat(p, i), flat(p, i + 1)) for p in around for i in range(start, top, 2)])
+    def lat_swap(start, parity):
+        return swap(
+            [(flat(p, i), flat(p, i + 1)) for p in around[parity::2] for i in range(start, top, 2)]
+        )
 
     def mirror(total):
         return [(flat(total - p, top), flat(p, top)) for p in around]
@@ -335,60 +354,75 @@
     even_east = lax.ppermute(to_west, AXES, sent(1, -1))
     even_west = lax.ppermute(to_east, AXES, sent(1, 1))
 
-    def after(values, first):
-        return pl.pallas_call(
-            functools.partial(after_kernel, len(values)),
-            out_shape=tuple(jax.ShapeDtypeStruct(x.shape, x.dtype) for x in values),
-            in_specs=[VMEM] * len(values) + [ANY] * len(first),
-            out_specs=(VMEM,) * len(values),
-            compiler_params=PARAMS,
-        )(*values, *first)
-
     mirrored_shape = (arrays, rows, cols + LANES)
 
     def fold(total, third):
-        def run(place, x):
-            f0 = lax.ppermute(x, AXES, mirror(total))
-            f1 = lax.ppermute(x, AXES, mirror(total - 1))
-            f2 = lax.ppermute(x, AXES, mirror(total - 2)) if third else x
+        totals = [total, total - 1] + [total - 2] * third
+        order = sorted(range(3), key=lambda n: totals[n] % 2 if n < len(totals) else -1)
+
+        def run(x, place, behind):
+            blocks = [lax.ppermute(x, AXES, mirror(t)) for t in totals] + [x] * (3 - len(totals))
             return pl.pallas_call(
-                functools.partial(fold_kernel, levels),
+                functools.partial(fold_kernel, levels, order),
                 out_shape=held(*mirrored_shape),
-                in_specs=[ANY] + [VMEM] * 3,
+                in_specs=[ANY] * 2 + [VMEM] * 3,
                 out_specs=VMEM,
                 scratch_shapes=[pltpu.SMEM((TILE, LANES), jnp.int32), pltpu.SemaphoreType.DMA],
                 compiler_params=PARAMS,
-            )(place, f0, f1, f2)
+            )(place, behind, *(blocks[n] for n in order))
 
         return run
 
-    def no_fold(place, x):
+    def no_fold(x, place, behind):
         return jnp.zeros(mirrored_shape, jnp.float32)
 
-    (where,) = after((place,), (to_east,))
-    chosen = jnp.where(lax.axis_index("lat") == top, where[0, 0] + 1, 0)
     folds = [fold(total, third) for total in around for third in (False, True)]
-    mirrored = lax.switch(chosen, [no_fold] + folds, where, y_rows)
-    go_east, go_west = after((to_east, to_west), (even_east, even_west, mirrored))
+    mirrored = lax.switch(chosen[0], [no_fold] + folds, y_rows, place, to_east)
+
+    def near(east, west):
+        return pl.pallas_call(
+            near_kernel,
+            out_shape=(held(data + 4 * edge, LANES), held(data + 4 * edge + TILE, LANES)),
+            in_specs=[VMEM] * 4,
+            out_specs=(VMEM,) * 2,
+            compiler_params=PARAMS,
+        )(x_rows, y_rows, east, west)
+
+    def steps(x_out, x_in, y_in):
+        return pl.pallas_call(
+            functools.partial(steps_kernel, levels),
+            out_shape=held(levels, rows, cols),
+            in_specs=[VMEM] * 7,
+            out_specs=VMEM,
+            scratch_shapes=[pltpu.VMEM((arrays, 3 * rows, cols + LANES), jnp.float32)],
+            compiler_params=PARAMS,
+        )(block, x_out, x_in, y_in, copied_area, root, mirrored)
+
+    x_out, y_out = near(even_east, even_west)
+    go_east, go_west = after((to_east, to_west), y_out, mirrored)
+    y_in = lax.ppermute(y_out, AXES, lat_swap(1, 0))
     odd_west = lax.ppermute(go_east, AXES, sent(0, 1))
     odd_east = lax.ppermute(go_west, AXES, sent(0, -1))
-    x_out, y_out = pl.pallas_call(
-        near_kernel,
-        out_shape=(held(data + 4 * edge, LANES), held(data + 2 * edge, LANES)),
-        in_specs=[VMEM] * 6,
-        out_specs=(VMEM, VMEM),
-        compiler_params=PARAMS,
-    )(x_rows, y_rows, even_east, even_west, odd_east, odd_west)
-    x_in = lax.ppermute(x_out, AXES, lat_swap(0))
-    y_in = lax.ppermute(y_out, AXES, lat_swap(1))
-    return pl.pallas_call(
-        functools.partial(steps_kernel, levels),
-        out_shape=held(levels, rows, cols),
-        in_specs=[VMEM] * 7,
-        out_specs=VMEM,
-        scratch_shapes=[pltpu.VMEM((arrays, 3 * rows, cols + LANES), jnp.float32)],
-        compiler_params=PARAMS,
-    )(block, x_out, x_in, y_in, copied_area, root, mirrored)
+    x_in = lax.ppermute(after(x_out, odd_west, odd_east), AXES, lat_swap(0, 0))
+
+    def even_steps(x_out, x_in, y_in, east, west):
+        return steps(x_out, x_in, y_in)
+
+    def odd_steps(x_out, x_in, y_in, east, west):
+        x_out, y_out = near(east, west)
+        y_in = lax.ppermute(y_out, AXES, lat_swap(1, 1))
+        x_in = lax.ppermute(x_out, AXES, lat_swap(0, 1))
+        return steps(x_out, x_in, y_in)
+
+    return lax.switch(
+        lax.rem(lax.axis_index("lon"), 2),
+        [even_steps, odd_steps],
+        x_out,
+        x_in,
+        y_in,
+        odd_east,
+        odd_west,
+    )
 
 
 def solution(mesh):

time: 41.9 us -> 39.9 us (0.952)
  the two profiles are of different devices: /device:TPU:1 before, /device:TPU:343 now
where the time goes in v4:
time: 39.9 us; the launch traced here: 39.6 us
  starting transfers between devices  28.7 us (72%)
  waiting for transfers between devices  5.42 us (14%)
  Pallas kernels  3.72 us (9%)
  between operations  0.81 us (2%)
  local copies, waits for them, and re-layouts  0.61 us (2%)
    ppermute x3, starting transfers between devices, run(): lax.ppermute(x, AXES, mirror(t))  20.9 us
    ppermute x3, waiting for transfers between devices, run(): lax.ppermute(x, AXES, mirror(t))  3.33 us
    ppermute x1, starting transfers between devices, per_device(): lax.ppermute(edges, AXES, [(flat(p, top), flat(p, top - 1)) for p in arou...  2.58 us
    ppermute x1, starting transfers between devices, per_device(): x_in = lax.ppermute(after(x_out, odd_west, odd_east), AXES, lat_swap(0, 0))  1.92 us
    pallas_call x1, Pallas kernels, per_device(): pl.pallas_call(pack_kernel, out_shape=(held(arrays, rows, cols), held(2 *...  1.42 us
    ppermute x1, waiting for transfers between devices, per_device(): x_in = lax.ppermute(after(x_out, odd_west, odd_east), AXES, lat_swap(0, 0))  1.26 us
    pallas_call x1, Pallas kernels, steps(): pl.pallas_call(functools.partial(steps_kernel, levels), out_shape=held(le...  1.22 us
    pallas_call x1, Pallas kernels, run(): pl.pallas_call(functools.partial(fold_kernel, levels, order), out_shape=h...  1.05 us
  transfers between devices with their start and end apart: 10, of which 3 were waited for; matrix products, arithmetic and copies ran while one was open for 0% of the time, Pallas kernels for 3%

profile of v4, /device:TPU:343, one launch (start us, length us, event | category | flops | bytes accessed | tf_op | source)
XLA Modules:
  0.0 39.6 jit_solution(10852123051942495975)
XLA Ops:
  0.0 1.4 %shard_map.75 = (f32[7,16,256]{2,1,0:T(8,128)S(1)}, f32[32,128]{1,0:T(8,128)S(1)}, f32[144,128]{1,0:T(8,128)S(1)}, f32[144,128]{1,0:T(8,128)S(1)}, f32[16,256]{1...) custom-call(s32[4096]{0:T(1024)} %refs_0_.1, f32[2,16,256]{2,1,0:T(8,128)} %refs_1_.1, ...), custom_call_target="tpu_custom_call" | custom-call | tf_op jit(solution)/shard_map/pallas_call | solution.py:306
  1.4 2.6 %collective-permute-start.82 = (f32[32,128]{1,0:T(8,128)S(1)}, f32[32,128]{1,0:T(8,128)S(1)}, u32[]{:S(2)}, u32[]{:S(2)}) collective-permute-start(f32[32,128]{1,0:T(8,128)S(1)} %get-tuple-element.394.edges), channel_id=1, source_target_pairs={{47,46},{95,94},{143,142},{191,190},{239,238},{287,286},{335,334},... | collective-permute-start | bytes 49160 | tf_op jit(solution)/shard_map/ppermute | solution.py:346
  4.0 0.8 %collective-permute-done.82.mate = f32[32,128]{1,0:T(8,128)S(1)} collective-permute-done((f32[32,128]{1,0:T(8,128)S(1)}, f32[32,128]{1,0:T(8,128)S(1)}, u32[]{:S(2)}, u32[]{:S(2)}) %collective-permute-start.82) | collective-permute-done | bytes 16416 | tf_op jit(solution)/shard_map/ppermute | solution.py:346
  4.8 0.7 %collective-permute-start.83 = (f32[32,128]{1,0:T(8,128)S(1)}, f32[32,128]{1,0:T(8,128)S(1)}, u32[]{:S(2)}, u32[]{:S(2)}) collective-permute-start(f32[32,128]{1,0:T(8,128)S(1)} %get-tuple-element.395.refs_1_), channel_id=1, source_target_pairs={{48,0},{49,1},{50,2},{51,3},{52,4},{53,5},{54,6},{55,7},{56,8},{57... | collective-permute-start | bytes 49160 | tf_op jit(solution)/shard_map/ppermute | solution.py:354
  5.5 0.7 %collective-permute-start.84 = (f32[32,128]{1,0:T(8,128)S(1)}, f32[32,128]{1,0:T(8,128)S(1)}, u32[]{:S(2)}, u32[]{:S(2)}) collective-permute-start(f32[32,128]{1,0:T(8,128)S(1)} %get-tuple-element.396.refs_0_), channel_id=1, source_target_pairs={{48,96},{49,97},{50,98},{51,99},{52,100},{53,101},{54,102},{55,103... | collective-permute-start | bytes 49160 | tf_op jit(solution)/shard_map/ppermute | solution.py:355
  6.8 25.6 %conditional.2 = (f32[7,16,384]{2,1,0:T(8,128)S(1)}) conditional(s32[]{:T(128)} %bitcast, () %tuple.110, (f32[144,128]{1,0:T(8,128)S(1)}, s32[8,128]{1,0:T(8,128)S(1)}, f32[32,128]{1,0:T(8,128)S(1)}) %tuple.111, (f32[144,128]{1,0:T(8,128)S(1)}, s32[8,128]{1,0:T(8,128)S(1)}, f32[32,128]{1,0:T(8,128)S(1)}) %tuple.111, ...), branch_computations={%region_0.0_spmd, %region_1.0_spmd, %region_2.0_spmd, %region_3.0_... | conditional | bytes 884864 | solution.py:380
  6.9 12.5 %collective-permute-start.4 = (f32[144,128]{1,0:T(8,128)S(1)}, f32[144,128]{1,0:T(8,128)S(1)}, u32[]{:S(2)}, u32[]{:S(2)}) collective-permute-start(f32[144,128]{1,0:T(8,128)S(1)} %get-tuple-element.242), channel_id=1, source_target_pairs={{767,47},{719,95},{671,143},{623,191},{575,239},{527,287},{479,335... | collective-permute-start | bytes 221192 | tf_op jit(solution)/shard_map/cond/branch_2_fun/ppermute | solution.py:364
  19.4 2.8 %collective-permute-start.3 = (f32[144,128]{1,0:T(8,128)S(1)}, f32[144,128]{1,0:T(8,128)S(1)}, u32[]{:S(2)}, u32[]{:S(2)}) collective-permute-start(f32[144,128]{1,0:T(8,128)S(1)} %get-tuple-element.242), channel_id=1, source_target_pairs={{719,47},{671,95},{623,143},{575,191},{527,239},{479,287},{431,335... | collective-permute-start | bytes 221192 | tf_op jit(solution)/shard_map/cond/branch_2_fun/ppermute | solution.py:364
  22.1 5.7 %collective-permute-start.2 = (f32[144,128]{1,0:T(8,128)S(1)}, f32[144,128]{1,0:T(8,128)S(1)}, u32[]{:S(2)}, u32[]{:S(2)}) collective-permute-start(f32[144,128]{1,0:T(8,128)S(1)} %get-tuple-element.242), channel_id=1, source_target_pairs={{47,47},{767,95},{719,143},{671,191},{623,239},{575,287},{527,335}... | collective-permute-start | bytes 221192 | tf_op jit(solution)/shard_map/cond/branch_2_fun/ppermute | solution.py:364
  27.8 0.0 collective-permute-done.4.third
  27.8 3.3 %collective-permute-done.2.first = f32[144,128]{1,0:T(8,128)S(1)} collective-permute-done((f32[144,128]{1,0:T(8,128)S(1)}, f32[144,128]{1,0:T(8,128)S(1)}, u32[]{:S(2)}, u32[]{:S(2)}) %collective-permute-start.2) | collective-permute-done | bytes 73760 | tf_op jit(solution)/shard_map/cond/branch_2_fun/ppermute | solution.py:364
  31.1 1.0 %branch_2_fun.1 = f32[7,16,384]{2,1,0:T(8,128)S(1)} custom-call(s32[8,128]{1,0:T(8,128)S(1)} %get-tuple-element.236.place, f32[32,128]{1,0:T(8,128)S(1)} %get-tuple-element.237.behind, f32[144,128]{1,0:T(8,128)S(1)} %collective-permute-done.2.first, f32[144,128]{1,0:T(8,128)S(1)} %collective-permute-done.3.second, f32[144,128]{1,0:T(8,128)S(1)} %collective-permute-done.4.third), custom_call_target="tpu_custom_call" | custom-call | tf_op jit(solution)/shard_map/cond/branch_2_fun/pallas_call | solution.py:365
  32.4 0.0 collective-permute-done.83.east
  32.5 0.7 %collective-permute-start.85 = (f32[32,128]{1,0:T(8,128)S(1)}, f32[32,128]{1,0:T(8,128)S(1)}, u32[]{:S(2)}, u32[]{:S(2)}) collective-permute-start(f32[32,128]{1,0:T(8,128)S(1)} %get-tuple-element.401), channel_id=1, source_target_pairs={{0,48},{1,49},{2,50},{3,51},{4,52},{5,53},{6,54},{7,55},{8,56},{9,... | collective-permute-start | bytes 49160 | tf_op jit(solution)/shard_map/ppermute | solution.py:404
  33.1 0.7 %collective-permute-start.86 = (f32[32,128]{1,0:T(8,128)S(1)}, f32[32,128]{1,0:T(8,128)S(1)}, u32[]{:S(2)}, u32[]{:S(2)}) collective-permute-start(f32[32,128]{1,0:T(8,128)S(1)} %get-tuple-element.402), channel_id=1, source_target_pairs={{0,720},{1,721},{2,722},{3,723},{4,724},{5,725},{6,726},{7,727},{8... | collective-permute-start | bytes 49160 | tf_op jit(solution)/shard_map/ppermute | solution.py:405
  33.8 0.7 %collective-permute-start.88 = (f32[216,128]{1,0:T(8,128)S(1)}, f32[216,128]{1,0:T(8,128)S(1)}, u32[]{:S(2)}, u32[]{:S(2)}) collective-permute-start(f32[216,128]{1,0:T(8,128)S(1)} %get-tuple-element.398.refs_2_), channel_id=1, source_target_pairs={{1,2},{2,1},{3,4},{4,3},{5,6},{6,5},{7,8},{8,7},{9,10},{10,9},{11,... | collective-permute-start | bytes 331784 | tf_op jit(solution)/shard_map/ppermute | solution.py:403
  34.5 0.0 collective-permute-done.85.refs_1_
  34.5 0.0 collective-permute-done.86.refs_2_
  34.5 1.9 %collective-permute-start.87 = (f32[208,128]{1,0:T(8,128)S(1)}, f32[208,128]{1,0:T(8,128)S(1)}, u32[]{:S(2)}, u32[]{:S(2)}) collective-permute-start(f32[208,128]{1,0:T(8,128)S(1)} %shard_map.79), channel_id=1, source_target_pairs={{0,1},{1,0},{2,3},{3,2},{4,5},{5,4},{6,7},{7,6},{8,9},{9,8},{10,11... | collective-permute-start | bytes 319496 | tf_op jit(solution)/shard_map/ppermute | solution.py:406
  36.5 1.3 %collective-permute-done.87 = f32[208,128]{1,0:T(8,128)S(1)} collective-permute-done((f32[208,128]{1,0:T(8,128)S(1)}, f32[208,128]{1,0:T(8,128)S(1)}, u32[]{:S(2)}, u32[]{:S(2)}) %collective-permute-start.87) | collective-permute-done | bytes 106528 | tf_op jit(solution)/shard_map/ppermute | solution.py:406
  37.7 1.2 %conditional.3 = (f32[2,16,256]{2,1,0:T(8,128)S(1)}) conditional(s32[]{:T(128)} %clamp.9, (f32[7,16,256]{2,1,0:T(8,128)S(1)}, f32[208,128]{1,0:T(8,128)S(1)}, f32[208,128]{1,0:T(8,128)S(1)}, f32[216,128]{1,0:T(8,128)S(1)}, f32[16,256]{1,0:T(8,128)S(1)}, /*index=5*/f32[16,256]{1,0:T(8,128)S(1)}, f32[7,16,384]{2,1,0:T(8,128)S(1)}) %tuple.112, ...), branch_computations={%region_33.0_spmd, %region_34.0_spmd} | conditional | bytes 868440 | solution.py:417
  37.7 1.2 %branch_0_fun.1 = f32[2,16,256]{2,1,0:T(8,128)S(1)} custom-call(f32[7,16,256]{2,1,0:T(8,128)S(1)} %get-tuple-element.360.own, f32[208,128]{1,0:T(8,128)S(1)} %get-tuple-element.361.x_out, f32[208,128]{1,0:T(8,128)S(1)} %get-tuple-element.362.x_in, f32[216,128]{1,0:T(8,128)S(1)} %get-tuple-element.363.y_in, f32[16,256]{1,0:T(8,128)S(1)} %get-tuple-element.364.area, ...), custom_call_target="tpu_custom_call" | custom-call | tf_op jit(solution)/shard_map/cond/branch_0_fun/pallas_call | solution.py:392
  39.0 0.0 copy-start
  39.0 0.6 %copy-done = f32[2,16,256]{2,1,0:T(8,128)} copy-done((f32[2,16,256]{2,1,0:T(8,128)}, f32[2,16,256]{2,1,0:T(8,128)S(1)}, u32[]{:S(2)}) %copy-start) | copy-done | bytes 32792
  (7 shorter events, 0.0 us)
Async XLA Ops:
  1.4 3.4 %collective-permute-start.82 = (f32[32,128]{1,0:T(8,128)S(1)}, f32[32,128]{1,0:T(8,128)S(1)}, u32[]{:S(2)}, u32[]{:S(2)}) collective-permute-start(f32[32,128]{1,0:T(8,128)S(1)} %get-tuple-element.394.edges), channel_id=1, source_target_pairs={{47,46},{95,94},{143,142},{191,190},{239,238},{287,286},{335,334},... | collective-permute-start | bytes 49160 | tf_op jit(solution)/shard_map/ppermute | solution.py:346
  4.8 27.6 %collective-permute-start.83 = (f32[32,128]{1,0:T(8,128)S(1)}, f32[32,128]{1,0:T(8,128)S(1)}, u32[]{:S(2)}, u32[]{:S(2)}) collective-permute-start(f32[32,128]{1,0:T(8,128)S(1)} %get-tuple-element.395.refs_1_), channel_id=1, source_target_pairs={{48,0},{49,1},{50,2},{51,3},{52,4},{53,5},{54,6},{55,7},{56,8},{57... | collective-permute-start | bytes 49160 | tf_op jit(solution)/shard_map/ppermute | solution.py:354
  5.5 26.9 %collective-permute-start.84 = (f32[32,128]{1,0:T(8,128)S(1)}, f32[32,128]{1,0:T(8,128)S(1)}, u32[]{:S(2)}, u32[]{:S(2)}) collective-permute-start(f32[32,128]{1,0:T(8,128)S(1)} %get-tuple-element.396.refs_0_), channel_id=1, source_target_pairs={{48,96},{49,97},{50,98},{51,99},{52,100},{53,101},{54,102},{55,103... | collective-permute-start | bytes 49160 | tf_op jit(solution)/shard_map/ppermute | solution.py:355
  6.9 20.9 %collective-permute-start.4 = (f32[144,128]{1,0:T(8,128)S(1)}, f32[144,128]{1,0:T(8,128)S(1)}, u32[]{:S(2)}, u32[]{:S(2)}) collective-permute-start(f32[144,128]{1,0:T(8,128)S(1)} %get-tuple-element.242), channel_id=1, source_target_pairs={{767,47},{719,95},{671,143},{623,191},{575,239},{527,287},{479,335... | collective-permute-start | bytes 221192 | tf_op jit(solution)/shard_map/cond/branch_2_fun/ppermute | solution.py:364
  19.4 8.4 %collective-permute-start.3 = (f32[144,128]{1,0:T(8,128)S(1)}, f32[144,128]{1,0:T(8,128)S(1)}, u32[]{:S(2)}, u32[]{:S(2)}) collective-permute-start(f32[144,128]{1,0:T(8,128)S(1)} %get-tuple-element.242), channel_id=1, source_target_pairs={{719,47},{671,95},{623,143},{575,191},{527,239},{479,287},{431,335... | collective-permute-start | bytes 221192 | tf_op jit(solution)/shard_map/cond/branch_2_fun/ppermute | solution.py:364
  22.1 9.0 %collective-permute-start.2 = (f32[144,128]{1,0:T(8,128)S(1)}, f32[144,128]{1,0:T(8,128)S(1)}, u32[]{:S(2)}, u32[]{:S(2)}) collective-permute-start(f32[144,128]{1,0:T(8,128)S(1)} %get-tuple-element.242), channel_id=1, source_target_pairs={{47,47},{767,95},{719,143},{671,191},{623,239},{575,287},{527,335}... | collective-permute-start | bytes 221192 | tf_op jit(solution)/shard_map/cond/branch_2_fun/ppermute | solution.py:364
  32.5 2.0 %collective-permute-start.85 = (f32[32,128]{1,0:T(8,128)S(1)}, f32[32,128]{1,0:T(8,128)S(1)}, u32[]{:S(2)}, u32[]{:S(2)}) collective-permute-start(f32[32,128]{1,0:T(8,128)S(1)} %get-tuple-element.401), channel_id=1, source_target_pairs={{0,48},{1,49},{2,50},{3,51},{4,52},{5,53},{6,54},{7,55},{8,56},{9,... | collective-permute-start | bytes 49160 | tf_op jit(solution)/shard_map/ppermute | solution.py:404
  33.1 1.4 %collective-permute-start.86 = (f32[32,128]{1,0:T(8,128)S(1)}, f32[32,128]{1,0:T(8,128)S(1)}, u32[]{:S(2)}, u32[]{:S(2)}) collective-permute-start(f32[32,128]{1,0:T(8,128)S(1)} %get-tuple-element.402), channel_id=1, source_target_pairs={{0,720},{1,721},{2,722},{3,723},{4,724},{5,725},{6,726},{7,727},{8... | collective-permute-start | bytes 49160 | tf_op jit(solution)/shard_map/ppermute | solution.py:405
  33.8 2.7 %collective-permute-start.88 = (f32[216,128]{1,0:T(8,128)S(1)}, f32[216,128]{1,0:T(8,128)S(1)}, u32[]{:S(2)}, u32[]{:S(2)}) collective-permute-start(f32[216,128]{1,0:T(8,128)S(1)} %get-tuple-element.398.refs_2_), channel_id=1, source_target_pairs={{1,2},{2,1},{3,4},{4,3},{5,6},{6,5},{7,8},{8,7},{9,10},{10,9},{11,... | collective-permute-start | bytes 331784 | tf_op jit(solution)/shard_map/ppermute | solution.py:403
  34.5 3.2 %collective-permute-start.87 = (f32[208,128]{1,0:T(8,128)S(1)}, f32[208,128]{1,0:T(8,128)S(1)}, u32[]{:S(2)}, u32[]{:S(2)}) collective-permute-start(f32[208,128]{1,0:T(8,128)S(1)} %shard_map.79), channel_id=1, source_target_pairs={{0,1},{1,0},{2,3},{3,2},{4,5},{5,4},{6,7},{7,6},{8,9},{9,8},{10,11... | collective-permute-start | bytes 319496 | tf_op jit(solution)/shard_map/ppermute | solution.py:406
  39.0 0.6 %copy-start = (f32[2,16,256]{2,1,0:T(8,128)}, f32[2,16,256]{2,1,0:T(8,128)S(1)}, u32[]{:S(2)}) copy-start(f32[2,16,256]{2,1,0:T(8,128)S(1)} %get-tuple-element.587) | copy-start | bytes 98308

commit v5 on v4

--- a/solution.py
+++ b/solution.py
@@ -23,18 +23,51 @@
     return [(k, t, m // PER_ROW, (m % PER_ROW) * ITERS) for m, (k, t) in enumerate(places)]
 
 
+def early():
+    at_top = lax.axis_index("lat") == lax.axis_size("lat") - 1
+    return (lax.rem(lax.axis_index("lon"), 2) == 1) | at_top
+
+
 def pack_kernel(*refs):
-    sources, (block, edges, x_rows, y_rows, area_out, root, place, chosen) = refs[:7], refs[7:15]
-    held, (grad, norm, de, dn, area, mask), arrived = refs[15], refs[16:22], refs[22]
+    (partner, *sources), outs, place = refs[:7], refs[7:13], refs[13]
+    targets, held, arrived = refs[14:20], refs[20], refs[21]
+    cols = targets[0].shape[2]
+
+    @pl.when(early())
+    def _():
+        extra = pltpu.make_async_copy(partner.at[pl.ds(0, held.shape[0])], held, arrived.at[6])
+        extra.start()
+        pack(sources, targets, arrived, *outs)
+        extra.wait()
+        moved = held[0] + ITERS
+        q = lax.rem(lax.div(moved, cols), lax.axis_size("lon"))
+        offset = lax.rem(moved, cols) - ITERS
+        branch = 2 * q + jnp.where(offset < ITERS - 1, 1, 0)
+        place[...] = jnp.where(lane_index() == 0, branch, offset)
+
+
+def late_pack_kernel(*refs):
+    sources, firsts, outs = refs[:6], refs[6:12], refs[13:19]
+    targets, arrived = refs[19:25], refs[25]
+
+    @pl.when(jnp.logical_not(early()))
+    def _():
+        pack(sources, targets, arrived, *outs)
+
+    @pl.when(early() & (lax.rem(lax.axis_index("lon"), 2) == 0))
+    def _():
+        for first, out in zip(firsts, outs):
+            out[...] = first[...]
+
+
+def pack(sources, targets, arrived, block, edges, x_rows, y_rows, area_out, root):
+    grad, norm, de, dn, area, mask = targets
     levels, rows, cols = grad.shape
     arrays = block.shape[0]
     copies = [
         pltpu.make_async_copy(source, target, arrived.at[n])
-        for n, (source, target) in enumerate(zip(sources[1:], (grad, norm, de, dn, area, mask)))
+        for n, (source, target) in enumerate(zip(sources, targets))
     ]
-    copies.append(
-        pltpu.make_async_copy(sources[0].at[pl.ds(0, held.shape[0])], held, arrived.at[len(copies)])
-    )
     for copy in copies:
         copy.start()
     for copy in copies:
@@ -84,12 +117,6 @@
             here = slice(base + (arrays + e) * TILE, base + (arrays + e + 1) * TILE)
             x_rows[here] = jnp.where(lat_even, north, south)
             y_rows[here] = jnp.where(lat_even, south, north)
-    moved = held[0] + ITERS
-    q = lax.rem(lax.div(moved, cols), lax.axis_size("lon"))
-    offset = lax.rem(moved, cols) - ITERS
-    place[...] = jnp.full((TILE, LANES), offset)
-    at_top = lax.axis_index("lat") == lax.axis_size("lat") - 1
-    chosen[...] = jnp.full((1,), jnp.where(at_top, 1 + 2 * q + jnp.where(offset < ITERS - 1, 1, 0), 0))
 
 
 def join_kernel(edges, mate, to_east, to_west):
@@ -133,9 +160,9 @@
     return jnp.take_along_axis(x, index, axis=1, mode="promise_in_bounds")
 
 
-def fold_kernel(levels, order, place, behind, first, second, third, out, placed, arrived):
-    del behind
-    blocks = dict(zip(order, (first, second, third)))
+def fold_kernel(levels, used, place, *refs):
+    blocks, (out, placed, arrived) = refs[:-3], refs[-3:]
+    lon_even = lax.rem(lax.axis_index("lon"), 2) == 0
     copy = pltpu.make_async_copy(place, placed, arrived)
     copy.start()
     arrays, rows, wide = out.shape
@@ -143,7 +170,7 @@
     tiles_across = cols // LANES
     band = (arrays + 2) * TILE
     copy.wait()
-    offset = placed[0, 0]
+    offset = placed[0, 1]
     span = 3 * cols
     far = lane_index(rows)
 
@@ -151,11 +178,14 @@
         east_face = levels <= k < 2 * levels
         north_face = 2 * levels <= k < 3 * levels
         pieces = []
-        for f in (blocks[n] for n in range(3)):
+        for even, odd in used:
             for c in range(tiles_across - 1, -1, -1):
                 main_at = c * band + k * TILE
                 few_at = c * band + (arrays + k // 4) * TILE
-                main, few = f[main_at : main_at + TILE], f[few_at : few_at + TILE]
+                main, few = (
+                    jnp.where(lon_even, blocks[even][at : at + TILE], blocks[odd][at : at + TILE])
+                    for at in (main_at, few_at)
+                )
                 few = pltpu.roll(few, (TILE - 2 - 2 * (k % 4)) % TILE, 0)
                 pieces.append(reversed_lanes(jnp.concatenate([few, main], axis=0)))
         shift = offset + span - cols + (0 if east_face else 1)
@@ -303,26 +333,6 @@
     inputs = (gradient, norm_factor, diff_east, diff_north, cell_area, sea_mask)
     edge = (slots(arrays)[-1][2] + 1) * TILE
     data = (arrays + 2) * TILE * (cols // LANES)
-    block, edges, x_rows, y_rows, copied_area, root, place, chosen = pl.pallas_call(
-        pack_kernel,
-        out_shape=(
-            held(arrays, rows, cols),
-            held(2 * edge, LANES),
-            held(data, LANES),
-            held(data, LANES),
-            held(rows, cols),
-            held(rows, cols),
-            jax.ShapeDtypeStruct((TILE, LANES), jnp.int32),
-            jax.ShapeDtypeStruct((1,), jnp.int32),
-        ),
-        in_specs=[HBM] * 7,
-        out_specs=(VMEM,) * 8,
-        scratch_shapes=[pltpu.SMEM((LANES,), jnp.int32)]
-        + [pltpu.VMEM(x.shape, x.dtype) for x in inputs]
-        + [pltpu.SemaphoreType.DMA((7,))],
-        compiler_params=PARAMS,
-    )(*[pltpu.with_memory_space_constraint(x, pltpu.HBM) for x in (partner, *inputs)])
-
     def flat(lon, lat):
         return (lon % lon_count) * lat_count + lat
 
@@ -343,43 +353,117 @@
     def mirror(total):
         return [(flat(total - p, top), flat(p, top)) for p in around]
 
-    mate = lax.ppermute(edges, AXES, [(flat(p, top), flat(p, top - 1)) for p in around])
-    to_east, to_west = pl.pallas_call(
-        join_kernel,
-        out_shape=(held(2 * edge, LANES),) * 2,
-        in_specs=[VMEM] * 2,
-        out_specs=(VMEM,) * 2,
+    packed_shapes = (
+        held(arrays, rows, cols),
+        held(2 * edge, LANES),
+        held(data, LANES),
+        held(data, LANES),
+        held(rows, cols),
+        held(rows, cols),
+    )
+    joined_shapes = (held(2 * edge, LANES),) * 2
+    odd = lax.rem(lax.axis_index("lon"), 2)
+
+    def join(edges, mate):
+        return pl.pallas_call(
+            join_kernel,
+            out_shape=joined_shapes,
+            in_specs=[VMEM] * 2,
+            out_specs=(VMEM,) * 2,
+            compiler_params=PARAMS,
+        )(edges, mate)
+
+    def in_hbm(*arrays):
+        return [pltpu.with_memory_space_constraint(x, pltpu.HBM) for x in arrays]
+
+    buffers = [pltpu.VMEM(x.shape, x.dtype) for x in inputs]
+    *early_held, place = pl.pallas_call(
+        pack_kernel,
+        out_shape=packed_shapes + (jax.ShapeDtypeStruct((TILE, LANES), jnp.int32),),
+        in_specs=[HBM] * 7,
+        out_specs=(VMEM,) * 7,
+        scratch_shapes=buffers
+        + [pltpu.SMEM((LANES,), jnp.int32), pltpu.SemaphoreType.DMA((7,))],
         compiler_params=PARAMS,
-    )(edges, mate)
+    )(*in_hbm(partner, *inputs))
+
+    def mates(parity):
+        return [(flat(p, top), flat(p, top - 1)) for p in around[parity::2]]
+
+    def fetch(edges):
+        return join(edges, lax.ppermute(edges, AXES, mates(1)))
+
+    def no_fetch(edges):
+        return join(edges, edges)
+
+    near_top = lax.axis_index("lat") >= top - 1
+    edges = early_held[1]
+    to_east, to_west = lax.switch(
+        (near_top & (odd == 1)).astype(jnp.int32), [no_fetch, fetch], edges
+    )
     even_east = lax.ppermute(to_west, AXES, sent(1, -1))
     even_west = lax.ppermute(to_east, AXES, sent(1, 1))
 
+    def late_fetch(edges):
+        return after(lax.ppermute(edges, AXES, mates(0)))
+
+    late_mate = lax.switch(
+        (near_top & (odd == 0)).astype(jnp.int32), [after, late_fetch], after(edges, to_east)
+    )
+    late_held = pl.pallas_call(
+        late_pack_kernel,
+        out_shape=packed_shapes,
+        in_specs=[HBM] * 6 + [VMEM] * 6 + [ANY],
+        out_specs=(VMEM,) * 6,
+        scratch_shapes=buffers + [pltpu.SemaphoreType.DMA((6,))],
+        compiler_params=PARAMS,
+    )(*in_hbm(*inputs), *early_held, late_mate)
     mirrored_shape = (arrays, rows, cols + LANES)
 
     def fold(total, third):
         totals = [total, total - 1] + [total - 2] * third
-        order = sorted(range(3), key=lambda n: totals[n] % 2 if n < len(totals) else -1)
-
-        def run(x, place, behind):
-            blocks = [lax.ppermute(x, AXES, mirror(t)) for t in totals] + [x] * (3 - len(totals))
+        steps = [(n, 1) for n, t in enumerate(totals) if t % 2 == 0]
+        steps += [(n, None) for n, t in enumerate(totals) if t % 2]
+        steps += [(n, 0) for n, t in enumerate(totals) if t % 2 == 0]
+        used = [[0, 0] for _ in range(3)]
+        for at, (n, parity) in enumerate(steps):
+            for side in (0, 1):
+                if parity in (None, side):
+                    used[n][side] = at
+
+        def run(x, place):
+            blocks = []
+            for n, parity in steps:
+                pairs = [
+                    (flat(totals[n] - p, top), flat(p, top))
+                    for p in around
+                    if parity in (None, p % 2)
+                ]
+                blocks.append(lax.ppermute(x, AXES, pairs))
             return pl.pallas_call(
-                functools.partial(fold_kernel, levels, order),
+                functools.partial(fold_kernel, levels, used),
                 out_shape=held(*mirrored_shape),
-                in_specs=[ANY] * 2 + [VMEM] * 3,
+                in_specs=[ANY] + [VMEM] * len(blocks),
                 out_specs=VMEM,
                 scratch_shapes=[pltpu.SMEM((TILE, LANES), jnp.int32), pltpu.SemaphoreType.DMA],
                 compiler_params=PARAMS,
-            )(place, behind, *(blocks[n] for n in order))
+            )(place, *blocks)
 
         return run
 
-    def no_fold(x, place, behind):
+    def at_top(rows_held, place):
+        folds = [fold(total, third) for total in around for third in (False, True)]
+        return after(lax.switch(place[0, 0], folds, rows_held, place))
+
+    def below(rows_held, place):
         return jnp.zeros(mirrored_shape, jnp.float32)
 
-    folds = [fold(total, third) for total in around for third in (False, True)]
-    mirrored = lax.switch(chosen[0], [no_fold] + folds, y_rows, place, to_east)
-
-    def near(east, west):
+    mirrored = lax.switch(
+        (lax.axis_index("lat") == top).astype(jnp.int32), [below, at_top], early_held[3], after(place, late_mate)
+    )
+
+    def near(held_here, east, west):
+        _, _, x_rows, y_rows, _, _ = held_here
         return pl.pallas_call(
             near_kernel,
             out_shape=(held(data + 4 * edge, LANES), held(data + 4 * edge + TILE, LANES)),
@@ -388,7 +472,8 @@
             compiler_params=PARAMS,
         )(x_rows, y_rows, east, west)
 
-    def steps(x_out, x_in, y_in):
+    def steps(held_here, x_out, x_in, y_in):
+        block, _, _, _, area, root = held_here
         return pl.pallas_call(
             functools.partial(steps_kernel, levels),
             out_shape=held(levels, rows, cols),
@@ -396,26 +481,26 @@
             out_specs=VMEM,
             scratch_shapes=[pltpu.VMEM((arrays, 3 * rows, cols + LANES), jnp.float32)],
             compiler_params=PARAMS,
-        )(block, x_out, x_in, y_in, copied_area, root, mirrored)
-
-    x_out, y_out = near(even_east, even_west)
-    go_east, go_west = after((to_east, to_west), y_out, mirrored)
+        )(block, x_out, x_in, y_in, area, root, mirrored)
+
+    x_out, y_out = near(late_held, even_east, even_west)
+    go_east, go_west = join(after(late_held[1], y_out, mirrored), late_mate)
     y_in = lax.ppermute(y_out, AXES, lat_swap(1, 0))
     odd_west = lax.ppermute(go_east, AXES, sent(0, 1))
     odd_east = lax.ppermute(go_west, AXES, sent(0, -1))
     x_in = lax.ppermute(after(x_out, odd_west, odd_east), AXES, lat_swap(0, 0))
 
     def even_steps(x_out, x_in, y_in, east, west):
-        return steps(x_out, x_in, y_in)
+        return steps(late_held, x_out, x_in, y_in)
 
     def odd_steps(x_out, x_in, y_in, east, west):
-        x_out, y_out = near(east, west)
+        x_out, y_out = near(early_held, east, west)
         y_in = lax.ppermute(y_out, AXES, lat_swap(1, 1))
         x_in = lax.ppermute(x_out, AXES, lat_swap(0, 1))
-        return steps(x_out, x_in, y_in)
+        return steps(early_held, x_out, x_in, y_in)
 
     return lax.switch(
-        lax.rem(lax.axis_index("lon"), 2),
+        odd,
         [even_steps, odd_steps],
         x_out,
         x_in,

time: 39.9 us -> 37.7 us (0.945)
  starting transfers between devices: 28.7 us -> 21.8 us
  waiting for transfers between devices: 5.42 us -> 9.6 us
  loops' own time: 0.3 us -> 1.31 us
  between operations: 0.81 us -> 0.18 us
  local copies, waits for them, and re-layouts: 0.61 us -> 1.12 us
    ppermute x4, starting transfers between devices: 23.5 us -> 16.5 us  [the longest x3 14.9 us: run(): blocks.append(lax.ppermute(x, AXES, pairs))]
    ppermute x4, waiting for transfers between devices: 4.15 us -> 8.32 us  [the longest x3 7.5 us: run(): blocks.append(lax.ppermute(x, AXES, pairs))]
    another operation x2 -> x5, loops' own time: 0.3 us -> 1.31 us  [the longest x1 0.92 us: per_device(): lax.switch((lax.axis_index('lat') == top).astype(jnp.int32), [below, at_t...]
    slice x0 -> x1, local copies, waits for them, and re-layouts: none -> 0.51 us  [at_top(): return after(lax.switch(place[0, 0], folds, rows_held, place))]
    pallas_call x3 -> x5, Pallas kernels: 2.47 us -> 2.15 us  [the longest x1 1.05 us: run(): pl.pallas_call(functools.partial(fold_kernel, levels, used), out_shape=he...]
  transfers between devices with their start and end apart: 10 -> 10, of which waited for: 3 -> 3; matrix products, arithmetic and copies ran while one was open for 0% -> 0% of each run, Pallas kernels for 3% -> 0%
where the time goes in v5:
time: 37.7 us; the launch traced here: 37.4 us
  starting transfers between devices  21.8 us (58%)
  waiting for transfers between devices  9.6 us (25%)
  Pallas kernels  3.42 us (9%)
  loops' own time  1.31 us (3%)
  local copies, waits for them, and re-layouts  1.12 us (3%)
    ppermute x3, starting transfers between devices, run(): blocks.append(lax.ppermute(x, AXES, pairs))  14.9 us
    ppermute x3, waiting for transfers between devices, run(): blocks.append(lax.ppermute(x, AXES, pairs))  7.5 us
    ppermute x1, starting transfers between devices, per_device(): x_in = lax.ppermute(after(x_out, odd_west, odd_east), AXES, lat_swap(0, 0))  1.92 us
    ppermute x1, starting transfers between devices, late_fetch(): return after(lax.ppermute(edges, AXES, mates(0)))  1.66 us
    ppermute x1, waiting for transfers between devices, per_device(): x_in = lax.ppermute(after(x_out, odd_west, odd_east), AXES, lat_swap(0, 0))  1.26 us
    pallas_call x1, Pallas kernels, steps(): pl.pallas_call(functools.partial(steps_kernel, levels), out_shape=held(le...  1.22 us
    pallas_call x1, Pallas kernels, run(): pl.pallas_call(functools.partial(fold_kernel, levels, used), out_shape=he...  1.05 us
    pallas_call x1, Pallas kernels, per_device(): pl.pallas_call(pack_kernel, out_shape=packed_shapes + (jax.ShapeDtypeStru...  0.99 us
  transfers between devices with their start and end apart: 10, of which 3 were waited for; matrix products, arithmetic and copies ran while one was open for 0% of the time, Pallas kernels for 0%

profile of v5, /device:TPU:343, one launch (start us, length us, event | category | flops | bytes accessed | tf_op | source)
XLA Modules:
  0.0 37.4 jit_solution(12108189897319695435)
XLA Ops:
  0.0 1.0 %shard_map.75 = (f32[7,16,256]{2,1,0:T(8,128)S(1)}, f32[32,128]{1,0:T(8,128)S(1)}, f32[144,128]{1,0:T(8,128)S(1)}, f32[144,128]{1,0:T(8,128)S(1)}, f32[16,256]{1...) custom-call(s32[4096]{0:T(1024)} %refs_0_.3, f32[2,16,256]{2,1,0:T(8,128)} %refs_0_.4, ...), custom_call_target="tpu_custom_call" | custom-call | tf_op jit(solution)/shard_map/pallas_call | solution.py:380
  1.0 2.5 %conditional.6 = (f32[32,128]{1,0:T(8,128)S(1)}) conditional(s32[]{:T(128)} %clamp.19, f32[32,128]{1,0:T(8,128)S(1)} %shard_map.76, f32[32,128]{1,0:T(8,128)S(1)} %shard_map.76), branch_computations={%region_2.0_spmd, %region_3.0_spmd} | conditional | bytes 65584 | solution.py:410
  1.1 1.7 %collective-permute-start.1 = (f32[32,128]{1,0:T(8,128)S(1)}, f32[32,128]{1,0:T(8,128)S(1)}, u32[]{:S(2)}, u32[]{:S(2)}) collective-permute-start(f32[32,128]{1,0:T(8,128)S(1)} %param.3), channel_id=1, source_target_pairs={{47,46},{143,142},{239,238},{335,334},{431,430},{527,526},{623,622... | collective-permute-start | bytes 49160 | tf_op jit(solution)/shard_map/cond/branch_1_fun/ppermute | solution.py:408
  2.7 0.8 %collective-permute-done.1.refs_0_ = f32[32,128]{1,0:T(8,128)S(1)} collective-permute-done((f32[32,128]{1,0:T(8,128)S(1)}, f32[32,128]{1,0:T(8,128)S(1)}, u32[]{:S(2)}, u32[]{:S(2)}) %collective-permute-start.1) | collective-permute-done | bytes 16416 | tf_op jit(solution)/shard_map/cond/branch_1_fun/ppermute | solution.py:408
  3.6 25.2 %conditional.7 = (f32[7,16,384]{2,1,0:T(8,128)S(1)}) conditional(s32[]{:T(128)} %clamp.21, () %tuple.125, (s32[8,128]{1,0:T(8,128)S(1)}, f32[144,128]{1,0:T(8,128)S(1)}) %tuple.126), branch_computations={%region_4.0_spmd, %region_5.0_spmd} | conditional | flops 1 | bytes 1474816 | solution.py:461
  3.6 0.5 %slice.2 = s32[1,1]{1,0:T(1,128)} slice(s32[8,128]{1,0:T(8,128)S(1)} %get-tuple-element.277), slice={[0:1], [0:1]} | slice | bytes 8 | tf_op jit(solution)/shard_map/cond/branch_1_fun/slice | solution.py:456
  4.7 23.7 %conditional = (f32[7,16,384]{2,1,0:T(8,128)S(1)}) conditional(s32[]{:T(128)} %bitcast, (f32[144,128]{1,0:T(8,128)S(1)}, s32[8,128]{1,0:T(8,128)S(1)}) %tuple.89, (f32[144,128]{1,0:T(8,128)S(1)}, s32[8,128]{1,0:T(8,128)S(1)}) %tuple.89, (f32[144,128]{1,0:T(8,128)S(1)}, s32[8,128]{1,0:T(8,128)S(1)}) %tuple.89, ...), branch_computations={%region_6.0_spmd, %region_7.0_spmd, %region_8.0_spmd, %region_9.0_... | conditional | bytes 1474768 | solution.py:456
  4.8 5.7 %collective-permute-start.12 = (f32[144,128]{1,0:T(8,128)S(1)}, f32[144,128]{1,0:T(8,128)S(1)}, u32[]{:S(2)}, u32[]{:S(2)}) collective-permute-start(f32[144,128]{1,0:T(8,128)S(1)} %get-tuple-element.190), channel_id=1, source_target_pairs={{47,47},{719,143},{623,239},{527,335},{431,431},{335,527},{239,623... | collective-permute-start | bytes 221192 | tf_op jit(solution)/shard_map/cond/branch_1_fun/cond/branch_2_fun/ppermute | solution.py:442
  10.4 8.6 %collective-permute-start.11 = (f32[144,128]{1,0:T(8,128)S(1)}, f32[144,128]{1,0:T(8,128)S(1)}, u32[]{:S(2)}, u32[]{:S(2)}) collective-permute-start(f32[144,128]{1,0:T(8,128)S(1)} %get-tuple-element.190), channel_id=1, source_target_pairs={{95,47},{47,95},{767,143},{719,191},{671,239},{623,287},{575,335},... | collective-permute-start | bytes 221192 | tf_op jit(solution)/shard_map/cond/branch_1_fun/cond/branch_2_fun/ppermute | solution.py:442
  19.0 0.7 %collective-permute-start.10 = (f32[144,128]{1,0:T(8,128)S(1)}, f32[144,128]{1,0:T(8,128)S(1)}, u32[]{:S(2)}, u32[]{:S(2)}) collective-permute-start(f32[144,128]{1,0:T(8,128)S(1)} %get-tuple-element.190), channel_id=1, source_target_pairs={{767,95},{671,191},{575,287},{479,383},{383,479},{287,575},{191,67... | collective-permute-start | bytes 221192 | tf_op jit(solution)/shard_map/cond/branch_1_fun/cond/branch_2_fun/ppermute | solution.py:442
  19.7 7.5 %collective-permute-done.11.refs_1_ = f32[144,128]{1,0:T(8,128)S(1)} collective-permute-done((f32[144,128]{1,0:T(8,128)S(1)}, f32[144,128]{1,0:T(8,128)S(1)}, u32[]{:S(2)}, u32[]{:S(2)}) %collective-permute-start.11) | collective-permute-done | bytes 73760 | tf_op jit(solution)/shard_map/cond/branch_1_fun/cond/branch_2_fun/ppermute | solution.py:442
  27.2 1.0 %branch_2_fun.1 = f32[7,16,384]{2,1,0:T(8,128)S(1)} custom-call(s32[8,128]{1,0:T(8,128)S(1)} %get-tuple-element.189.place, f32[144,128]{1,0:T(8,128)S(1)} %collective-permute-done.10.refs_0_, f32[144,128]{1,0:T(8,128)S(1)} %collective-permute-done.11.refs_1_, f32[144,128]{1,0:T(8,128)S(1)} %collective-permute-done.12.refs_2_), custom_call_target="tpu_custom_call" | custom-call | tf_op jit(solution)/shard_map/cond/branch_1_fun/cond/branch_2_fun/pallas_call | solution.py:443
  28.8 0.7 %collective-permute-start.124 = (f32[32,128]{1,0:T(8,128)S(1)}, f32[32,128]{1,0:T(8,128)S(1)}, u32[]{:S(2)}, u32[]{:S(2)}) collective-permute-start(f32[32,128]{1,0:T(8,128)S(1)} %get-tuple-element.325), channel_id=1, source_target_pairs={{48,0},{49,1},{50,2},{51,3},{52,4},{53,5},{54,6},{55,7},{56,8},{57... | collective-permute-start | bytes 49160 | tf_op jit(solution)/shard_map/ppermute | solution.py:404
  29.4 0.7 %collective-permute-start.125 = (f32[32,128]{1,0:T(8,128)S(1)}, f32[32,128]{1,0:T(8,128)S(1)}, u32[]{:S(2)}, u32[]{:S(2)}) collective-permute-start(f32[32,128]{1,0:T(8,128)S(1)} %get-tuple-element.321.refs_1_), channel_id=1, source_target_pairs={{48,96},{49,97},{50,98},{51,99},{52,100},{53,101},{54,102},{55,103... | collective-permute-start | bytes 49160 | tf_op jit(solution)/shard_map/ppermute | solution.py:405
  30.1 0.1 shard_map.77
  30.3 0.7 %collective-permute-start.126 = (f32[32,128]{1,0:T(8,128)S(1)}, f32[32,128]{1,0:T(8,128)S(1)}, u32[]{:S(2)}, u32[]{:S(2)}) collective-permute-start(f32[32,128]{1,0:T(8,128)S(1)} %get-tuple-element.330), channel_id=1, source_target_pairs={{0,48},{1,49},{2,50},{3,51},{4,52},{5,53},{6,54},{7,55},{8,56},{9,... | collective-permute-start | bytes 49160 | tf_op jit(solution)/shard_map/ppermute | solution.py:489
  31.0 0.7 %collective-permute-start.127 = (f32[32,128]{1,0:T(8,128)S(1)}, f32[32,128]{1,0:T(8,128)S(1)}, u32[]{:S(2)}, u32[]{:S(2)}) collective-permute-start(f32[32,128]{1,0:T(8,128)S(1)} %get-tuple-element.331), channel_id=1, source_target_pairs={{0,720},{1,721},{2,722},{3,723},{4,724},{5,725},{6,726},{7,727},{8... | collective-permute-start | bytes 49160 | tf_op jit(solution)/shard_map/ppermute | solution.py:490
  31.6 0.7 %collective-permute-start.129 = (f32[216,128]{1,0:T(8,128)S(1)}, f32[216,128]{1,0:T(8,128)S(1)}, u32[]{:S(2)}, u32[]{:S(2)}) collective-permute-start(f32[216,128]{1,0:T(8,128)S(1)} %get-tuple-element.328.refs_1_), channel_id=1, source_target_pairs={{1,2},{2,1},{3,4},{4,3},{5,6},{6,5},{7,8},{8,7},{9,10},{10,9},{11,... | collective-permute-start | bytes 331784 | tf_op jit(solution)/shard_map/ppermute | solution.py:488
  32.3 1.9 %collective-permute-start.128 = (f32[208,128]{1,0:T(8,128)S(1)}, f32[208,128]{1,0:T(8,128)S(1)}, u32[]{:S(2)}, u32[]{:S(2)}) collective-permute-start(f32[208,128]{1,0:T(8,128)S(1)} %shard_map.82), channel_id=1, source_target_pairs={{0,1},{1,0},{2,3},{3,2},{4,5},{5,4},{6,7},{7,6},{8,9},{9,8},{10,11... | collective-permute-start | bytes 319496 | tf_op jit(solution)/shard_map/ppermute | solution.py:491
  34.3 1.3 %collective-permute-done.128 = f32[208,128]{1,0:T(8,128)S(1)} collective-permute-done((f32[208,128]{1,0:T(8,128)S(1)}, f32[208,128]{1,0:T(8,128)S(1)}, u32[]{:S(2)}, u32[]{:S(2)}) %collective-permute-start.128) | collective-permute-done | bytes 106528 | tf_op jit(solution)/shard_map/ppermute | solution.py:491
  35.5 1.2 %conditional.8 = (f32[2,16,256]{2,1,0:T(8,128)S(1)}) conditional(s32[]{:T(128)} %clamp.18, (f32[7,16,256]{2,1,0:T(8,128)S(1)}, f32[208,128]{1,0:T(8,128)S(1)}, f32[208,128]{1,0:T(8,128)S(1)}, f32[216,128]{1,0:T(8,128)S(1)}, f32[16,256]{1,0:T(8,128)S(1)}, /*index=5*/f32[16,256]{1,0:T(8,128)S(1)}, f32[7,16,384]{2,1,0:T(8,128)S(1)}) %tuple.127, ...), branch_computations={%region_38.0_spmd, %region_39.0_spmd} | conditional | bytes 868440 | solution.py:502
  35.5 1.2 %branch_0_fun.7 = f32[2,16,256]{2,1,0:T(8,128)S(1)} custom-call(f32[7,16,256]{2,1,0:T(8,128)S(1)} %get-tuple-element.279.own, f32[208,128]{1,0:T(8,128)S(1)} %get-tuple-element.280.x_out, f32[208,128]{1,0:T(8,128)S(1)} %get-tuple-element.281.x_in, f32[216,128]{1,0:T(8,128)S(1)} %get-tuple-element.282.y_in, f32[16,256]{1,0:T(8,128)S(1)} %get-tuple-element.283.area, ...), custom_call_target="tpu_custom_call" | custom-call | tf_op jit(solution)/shard_map/cond/branch_0_fun/pallas_call | solution.py:477
  36.8 0.0 copy-start
  36.8 0.6 %copy-done = f32[2,16,256]{2,1,0:T(8,128)} copy-done((f32[2,16,256]{2,1,0:T(8,128)}, f32[2,16,256]{2,1,0:T(8,128)S(1)}, u32[]{:S(2)}) %copy-start) | copy-done | bytes 32792
  (17 shorter events, 0.1 us)
Async XLA Ops:
  1.1 2.5 %collective-permute-start.1 = (f32[32,128]{1,0:T(8,128)S(1)}, f32[32,128]{1,0:T(8,128)S(1)}, u32[]{:S(2)}, u32[]{:S(2)}) collective-permute-start(f32[32,128]{1,0:T(8,128)S(1)} %param.3), channel_id=1, source_target_pairs={{47,46},{143,142},{239,238},{335,334},{431,430},{527,526},{623,622... | collective-permute-start | bytes 49160 | tf_op jit(solution)/shard_map/cond/branch_1_fun/ppermute | solution.py:408
  4.8 14.9 %collective-permute-start.12 = (f32[144,128]{1,0:T(8,128)S(1)}, f32[144,128]{1,0:T(8,128)S(1)}, u32[]{:S(2)}, u32[]{:S(2)}) collective-permute-start(f32[144,128]{1,0:T(8,128)S(1)} %get-tuple-element.190), channel_id=1, source_target_pairs={{47,47},{719,143},{623,239},{527,335},{431,431},{335,527},{239,623... | collective-permute-start | bytes 221192 | tf_op jit(solution)/shard_map/cond/branch_1_fun/cond/branch_2_fun/ppermute | solution.py:442
  10.4 16.7 %collective-permute-start.11 = (f32[144,128]{1,0:T(8,128)S(1)}, f32[144,128]{1,0:T(8,128)S(1)}, u32[]{:S(2)}, u32[]{:S(2)}) collective-permute-start(f32[144,128]{1,0:T(8,128)S(1)} %get-tuple-element.190), channel_id=1, source_target_pairs={{95,47},{47,95},{767,143},{719,191},{671,239},{623,287},{575,335},... | collective-permute-start | bytes 221192 | tf_op jit(solution)/shard_map/cond/branch_1_fun/cond/branch_2_fun/ppermute | solution.py:442
  19.0 8.2 %collective-permute-start.10 = (f32[144,128]{1,0:T(8,128)S(1)}, f32[144,128]{1,0:T(8,128)S(1)}, u32[]{:S(2)}, u32[]{:S(2)}) collective-permute-start(f32[144,128]{1,0:T(8,128)S(1)} %get-tuple-element.190), channel_id=1, source_target_pairs={{767,95},{671,191},{575,287},{479,383},{383,479},{287,575},{191,67... | collective-permute-start | bytes 221192 | tf_op jit(solution)/shard_map/cond/branch_1_fun/cond/branch_2_fun/ppermute | solution.py:442
  28.8 1.5 %collective-permute-start.124 = (f32[32,128]{1,0:T(8,128)S(1)}, f32[32,128]{1,0:T(8,128)S(1)}, u32[]{:S(2)}, u32[]{:S(2)}) collective-permute-start(f32[32,128]{1,0:T(8,128)S(1)} %get-tuple-element.325), channel_id=1, source_target_pairs={{48,0},{49,1},{50,2},{51,3},{52,4},{53,5},{54,6},{55,7},{56,8},{57... | collective-permute-start | bytes 49160 | tf_op jit(solution)/shard_map/ppermute | solution.py:404
  29.4 0.8 %collective-permute-start.125 = (f32[32,128]{1,0:T(8,128)S(1)}, f32[32,128]{1,0:T(8,128)S(1)}, u32[]{:S(2)}, u32[]{:S(2)}) collective-permute-start(f32[32,128]{1,0:T(8,128)S(1)} %get-tuple-element.321.refs_1_), channel_id=1, source_target_pairs={{48,96},{49,97},{50,98},{51,99},{52,100},{53,101},{54,102},{55,103... | collective-permute-start | bytes 49160 | tf_op jit(solution)/shard_map/ppermute | solution.py:405
  30.3 2.0 %collective-permute-start.126 = (f32[32,128]{1,0:T(8,128)S(1)}, f32[32,128]{1,0:T(8,128)S(1)}, u32[]{:S(2)}, u32[]{:S(2)}) collective-permute-start(f32[32,128]{1,0:T(8,128)S(1)} %get-tuple-element.330), channel_id=1, source_target_pairs={{0,48},{1,49},{2,50},{3,51},{4,52},{5,53},{6,54},{7,55},{8,56},{9,... | collective-permute-start | bytes 49160 | tf_op jit(solution)/shard_map/ppermute | solution.py:489
  31.0 1.4 %collective-permute-start.127 = (f32[32,128]{1,0:T(8,128)S(1)}, f32[32,128]{1,0:T(8,128)S(1)}, u32[]{:S(2)}, u32[]{:S(2)}) collective-permute-start(f32[32,128]{1,0:T(8,128)S(1)} %get-tuple-element.331), channel_id=1, source_target_pairs={{0,720},{1,721},{2,722},{3,723},{4,724},{5,725},{6,726},{7,727},{8... | collective-permute-start | bytes 49160 | tf_op jit(solution)/shard_map/ppermute | solution.py:490
  31.6 2.7 %collective-permute-start.129 = (f32[216,128]{1,0:T(8,128)S(1)}, f32[216,128]{1,0:T(8,128)S(1)}, u32[]{:S(2)}, u32[]{:S(2)}) collective-permute-start(f32[216,128]{1,0:T(8,128)S(1)} %get-tuple-element.328.refs_1_), channel_id=1, source_target_pairs={{1,2},{2,1},{3,4},{4,3},{5,6},{6,5},{7,8},{8,7},{9,10},{10,9},{11,... | collective-permute-start | bytes 331784 | tf_op jit(solution)/shard_map/ppermute | solution.py:488
  32.3 3.2 %collective-permute-start.128 = (f32[208,128]{1,0:T(8,128)S(1)}, f32[208,128]{1,0:T(8,128)S(1)}, u32[]{:S(2)}, u32[]{:S(2)}) collective-permute-start(f32[208,128]{1,0:T(8,128)S(1)} %shard_map.82), channel_id=1, source_target_pairs={{0,1},{1,0},{2,3},{3,2},{4,5},{5,4},{6,7},{7,6},{8,9},{9,8},{10,11... | collective-permute-start | bytes 319496 | tf_op jit(solution)/shard_map/ppermute | solution.py:491
  36.8 0.6 %copy-start = (f32[2,16,256]{2,1,0:T(8,128)}, f32[2,16,256]{2,1,0:T(8,128)S(1)}, u32[]{:S(2)}) copy-start(f32[2,16,256]{2,1,0:T(8,128)S(1)} %get-tuple-element.603) | copy-start | bytes 98308

commit v6 on v5

--- a/solution.py
+++ b/solution.py
@@ -422,9 +422,7 @@
 
     def fold(total, third):
         totals = [total, total - 1] + [total - 2] * third
-        steps = [(n, 1) for n, t in enumerate(totals) if t % 2 == 0]
-        steps += [(n, None) for n, t in enumerate(totals) if t % 2]
-        steps += [(n, 0) for n, t in enumerate(totals) if t % 2 == 0]
+        steps = [(n, None) for n in sorted(range(len(totals)), key=lambda n: totals[n] % 2)]
         used = [[0, 0] for _ in range(3)]
         for at, (n, parity) in enumerate(steps):
             for side in (0, 1):

time: 37.7 us -> 36.5 us (0.968)
  the two profiles are of different devices: /device:TPU:343 before, /device:TPU:351 now
where the time goes in v6:
time: 36.5 us; the launch traced here: 36.1 us
  starting transfers between devices  23 us (63%)
  waiting for transfers between devices  7.56 us (21%)
  Pallas kernels  3.26 us (9%)
  local copies, waits for them, and re-layouts  1.12 us (3%)
  loops' own time  0.99 us (3%)
    ppermute x2, starting transfers between devices, run(): blocks.append(lax.ppermute(x, AXES, pairs))  14.8 us
    ppermute x2, waiting for transfers between devices, run(): blocks.append(lax.ppermute(x, AXES, pairs))  5.46 us
    ppermute x1, starting transfers between devices, late_fetch(): return after(lax.ppermute(edges, AXES, mates(0)))  2.92 us
    ppermute x1, starting transfers between devices, per_device(): x_in = lax.ppermute(after(x_out, odd_west, odd_east), AXES, lat_swap(0, 0))  1.92 us
    ppermute x1, waiting for transfers between devices, per_device(): x_in = lax.ppermute(after(x_out, odd_west, odd_east), AXES, lat_swap(0, 0))  1.26 us
    pallas_call x1, Pallas kernels, steps(): pl.pallas_call(functools.partial(steps_kernel, levels), out_shape=held(le...  1.22 us
    pallas_call x1, Pallas kernels, per_device(): pl.pallas_call(pack_kernel, out_shape=packed_shapes + (jax.ShapeDtypeStru...  0.99 us
    pallas_call x1, Pallas kernels, run(): pl.pallas_call(functools.partial(fold_kernel, levels, used), out_shape=he...  0.88 us
  transfers between devices with their start and end apart: 9, of which 4 were waited for; matrix products, arithmetic and copies ran while one was open for 1% of the time, Pallas kernels for 3%

profile of v6, /device:TPU:351, one launch (start us, length us, event | category | flops | bytes accessed | tf_op | source)
XLA Modules:
  0.0 36.1 jit_solution(15093751835014331848)
XLA Ops:
  0.0 1.0 %shard_map.75 = (f32[7,16,256]{2,1,0:T(8,128)S(1)}, f32[32,128]{1,0:T(8,128)S(1)}, f32[144,128]{1,0:T(8,128)S(1)}, f32[144,128]{1,0:T(8,128)S(1)}, f32[16,256]{1...) custom-call(s32[4096]{0:T(1024)} %refs_0_.3, f32[2,16,256]{2,1,0:T(8,128)} %refs_0_.4, ...), custom_call_target="tpu_custom_call" | custom-call | tf_op jit(solution)/shard_map/pallas_call | solution.py:380
  1.0 0.7 %collective-permute-start.84 = (f32[32,128]{1,0:T(8,128)S(1)}, f32[32,128]{1,0:T(8,128)S(1)}, u32[]{:S(2)}, u32[]{:S(2)}) collective-permute-start(f32[32,128]{1,0:T(8,128)S(1)} %get-tuple-element.325), channel_id=1, source_target_pairs={{48,0},{49,1},{50,2},{51,3},{52,4},{53,5},{54,6},{55,7},{56,8},{57... | collective-permute-start | bytes 49160 | tf_op jit(solution)/shard_map/ppermute | solution.py:404
  1.7 0.7 %collective-permute-start.85 = (f32[32,128]{1,0:T(8,128)S(1)}, f32[32,128]{1,0:T(8,128)S(1)}, u32[]{:S(2)}, u32[]{:S(2)}) collective-permute-start(f32[32,128]{1,0:T(8,128)S(1)} %get-tuple-element.321.refs_1_), channel_id=1, source_target_pairs={{48,96},{49,97},{50,98},{51,99},{52,100},{53,101},{54,102},{55,103... | collective-permute-start | bytes 49160 | tf_op jit(solution)/shard_map/ppermute | solution.py:405
  2.4 3.8 %conditional.6 = (f32[32,128]{1,0:T(8,128)S(1)}) conditional(s32[]{:T(128)} %clamp.19, f32[32,128]{1,0:T(8,128)S(1)} %shard_map.76, f32[32,128]{1,0:T(8,128)S(1)} %shard_map.76), branch_computations={%region_2.0_spmd, %region_3.0_spmd} | conditional | bytes 65584 | solution.py:410
  2.4 2.9 %collective-permute-start.1 = (f32[32,128]{1,0:T(8,128)S(1)}, f32[32,128]{1,0:T(8,128)S(1)}, u32[]{:S(2)}, u32[]{:S(2)}) collective-permute-start(f32[32,128]{1,0:T(8,128)S(1)} %param.3), channel_id=1, source_target_pairs={{47,46},{143,142},{239,238},{335,334},{431,430},{527,526},{623,622... | collective-permute-start | bytes 49160 | tf_op jit(solution)/shard_map/cond/branch_1_fun/ppermute | solution.py:408
  5.3 0.8 %collective-permute-done.1.refs_0_ = f32[32,128]{1,0:T(8,128)S(1)} collective-permute-done((f32[32,128]{1,0:T(8,128)S(1)}, f32[32,128]{1,0:T(8,128)S(1)}, u32[]{:S(2)}, u32[]{:S(2)}) %collective-permute-start.1) | collective-permute-done | bytes 16416 | tf_op jit(solution)/shard_map/cond/branch_1_fun/ppermute | solution.py:408
  6.2 22.6 %conditional.7 = (f32[7,16,384]{2,1,0:T(8,128)S(1)}) conditional(s32[]{:T(128)} %clamp.21, () %tuple.125, (s32[8,128]{1,0:T(8,128)S(1)}, f32[144,128]{1,0:T(8,128)S(1)}) %tuple.126), branch_computations={%region_4.0_spmd, %region_5.0_spmd} | conditional | flops 1 | bytes 884912 | solution.py:459
  6.2 0.5 %slice.2 = s32[1,1]{1,0:T(1,128)} slice(s32[8,128]{1,0:T(8,128)S(1)} %get-tuple-element.277), slice={[0:1], [0:1]} | slice | bytes 8 | tf_op jit(solution)/shard_map/cond/branch_1_fun/slice | solution.py:454
  7.3 21.3 %conditional = (f32[7,16,384]{2,1,0:T(8,128)S(1)}) conditional(s32[]{:T(128)} %bitcast, (f32[144,128]{1,0:T(8,128)S(1)}, s32[8,128]{1,0:T(8,128)S(1)}) %tuple.89, (f32[144,128]{1,0:T(8,128)S(1)}, s32[8,128]{1,0:T(8,128)S(1)}) %tuple.89, (f32[144,128]{1,0:T(8,128)S(1)}, s32[8,128]{1,0:T(8,128)S(1)}) %tuple.89, ...), branch_computations={%region_6.0_spmd, %region_7.0_spmd, %region_8.0_spmd, %region_9.0_... | conditional | bytes 884864 | solution.py:454
  7.4 11.3 %collective-permute-start.23 = (f32[144,128]{1,0:T(8,128)S(1)}, f32[144,128]{1,0:T(8,128)S(1)}, u32[]{:S(2)}, u32[]{:S(2)}) collective-permute-start(f32[144,128]{1,0:T(8,128)S(1)} %get-tuple-element.211), channel_id=1, source_target_pairs={{191,47},{143,95},{95,143},{47,191},{767,239},{719,287},{671,335},... | collective-permute-start | bytes 221192 | tf_op jit(solution)/shard_map/cond/branch_1_fun/cond/branch_8_fun/ppermute | solution.py:440
  18.7 3.5 %collective-permute-start.22 = (f32[144,128]{1,0:T(8,128)S(1)}, f32[144,128]{1,0:T(8,128)S(1)}, u32[]{:S(2)}, u32[]{:S(2)}) collective-permute-start(f32[144,128]{1,0:T(8,128)S(1)} %get-tuple-element.211), channel_id=1, source_target_pairs={{239,47},{191,95},{143,143},{95,191},{47,239},{767,287},{719,335},... | collective-permute-start | bytes 221192 | tf_op jit(solution)/shard_map/cond/branch_1_fun/cond/branch_8_fun/ppermute | solution.py:440
  22.2 0.7 %collective-permute-done.23.refs_1_ = f32[144,128]{1,0:T(8,128)S(1)} collective-permute-done((f32[144,128]{1,0:T(8,128)S(1)}, f32[144,128]{1,0:T(8,128)S(1)}, u32[]{:S(2)}, u32[]{:S(2)}) %collective-permute-start.23) | collective-permute-done | bytes 73760 | tf_op jit(solution)/shard_map/cond/branch_1_fun/cond/branch_8_fun/ppermute | solution.py:440
  22.9 4.8 %collective-permute-done.22.refs_0_ = f32[144,128]{1,0:T(8,128)S(1)} collective-permute-done((f32[144,128]{1,0:T(8,128)S(1)}, f32[144,128]{1,0:T(8,128)S(1)}, u32[]{:S(2)}, u32[]{:S(2)}) %collective-permute-start.22) | collective-permute-done | bytes 73760 | tf_op jit(solution)/shard_map/cond/branch_1_fun/cond/branch_8_fun/ppermute | solution.py:440
  27.7 0.9 %branch_8_fun.1 = f32[7,16,384]{2,1,0:T(8,128)S(1)} custom-call(s32[8,128]{1,0:T(8,128)S(1)} %get-tuple-element.210.place, f32[144,128]{1,0:T(8,128)S(1)} %collective-permute-done.22.refs_0_, f32[144,128]{1,0:T(8,128)S(1)} %collective-permute-done.23.refs_1_), custom_call_target="tpu_custom_call" | custom-call | tf_op jit(solution)/shard_map/cond/branch_1_fun/cond/branch_8_fun/pallas_call | solution.py:441
  28.8 0.1 shard_map.77
  29.0 0.7 %collective-permute-start.86 = (f32[32,128]{1,0:T(8,128)S(1)}, f32[32,128]{1,0:T(8,128)S(1)}, u32[]{:S(2)}, u32[]{:S(2)}) collective-permute-start(f32[32,128]{1,0:T(8,128)S(1)} %get-tuple-element.330), channel_id=1, source_target_pairs={{0,48},{1,49},{2,50},{3,51},{4,52},{5,53},{6,54},{7,55},{8,56},{9,... | collective-permute-start | bytes 49160 | tf_op jit(solution)/shard_map/ppermute | solution.py:487
  29.7 0.7 %collective-permute-start.87 = (f32[32,128]{1,0:T(8,128)S(1)}, f32[32,128]{1,0:T(8,128)S(1)}, u32[]{:S(2)}, u32[]{:S(2)}) collective-permute-start(f32[32,128]{1,0:T(8,128)S(1)} %get-tuple-element.331), channel_id=1, source_target_pairs={{0,720},{1,721},{2,722},{3,723},{4,724},{5,725},{6,726},{7,727},{8... | collective-permute-start | bytes 49160 | tf_op jit(solution)/shard_map/ppermute | solution.py:488
  30.3 0.7 %collective-permute-start.89 = (f32[216,128]{1,0:T(8,128)S(1)}, f32[216,128]{1,0:T(8,128)S(1)}, u32[]{:S(2)}, u32[]{:S(2)}) collective-permute-start(f32[216,128]{1,0:T(8,128)S(1)} %get-tuple-element.328.refs_1_), channel_id=1, source_target_pairs={{1,2},{2,1},{3,4},{4,3},{5,6},{6,5},{7,8},{8,7},{9,10},{10,9},{11,... | collective-permute-start | bytes 331784 | tf_op jit(solution)/shard_map/ppermute | solution.py:486
  31.0 1.9 %collective-permute-start.88 = (f32[208,128]{1,0:T(8,128)S(1)}, f32[208,128]{1,0:T(8,128)S(1)}, u32[]{:S(2)}, u32[]{:S(2)}) collective-permute-start(f32[208,128]{1,0:T(8,128)S(1)} %shard_map.82), channel_id=1, source_target_pairs={{0,1},{1,0},{2,3},{3,2},{4,5},{5,4},{6,7},{7,6},{8,9},{9,8},{10,11... | collective-permute-start | bytes 319496 | tf_op jit(solution)/shard_map/ppermute | solution.py:489
  33.0 1.3 %collective-permute-done.88 = f32[208,128]{1,0:T(8,128)S(1)} collective-permute-done((f32[208,128]{1,0:T(8,128)S(1)}, f32[208,128]{1,0:T(8,128)S(1)}, u32[]{:S(2)}, u32[]{:S(2)}) %collective-permute-start.88) | collective-permute-done | bytes 106528 | tf_op jit(solution)/shard_map/ppermute | solution.py:489
  34.2 1.2 %conditional.8 = (f32[2,16,256]{2,1,0:T(8,128)S(1)}) conditional(s32[]{:T(128)} %clamp.18, (f32[7,16,256]{2,1,0:T(8,128)S(1)}, f32[208,128]{1,0:T(8,128)S(1)}, f32[208,128]{1,0:T(8,128)S(1)}, f32[216,128]{1,0:T(8,128)S(1)}, f32[16,256]{1,0:T(8,128)S(1)}, /*index=5*/f32[16,256]{1,0:T(8,128)S(1)}, f32[7,16,384]{2,1,0:T(8,128)S(1)}) %tuple.127, ...), branch_computations={%region_38.0_spmd, %region_39.0_spmd} | conditional | bytes 868440 | solution.py:500
  34.2 1.2 %branch_0_fun.7 = f32[2,16,256]{2,1,0:T(8,128)S(1)} custom-call(f32[7,16,256]{2,1,0:T(8,128)S(1)} %get-tuple-element.279.own, f32[208,128]{1,0:T(8,128)S(1)} %get-tuple-element.280.x_out, f32[208,128]{1,0:T(8,128)S(1)} %get-tuple-element.281.x_in, f32[216,128]{1,0:T(8,128)S(1)} %get-tuple-element.282.y_in, f32[16,256]{1,0:T(8,128)S(1)} %get-tuple-element.283.area, ...), custom_call_target="tpu_custom_call" | custom-call | tf_op jit(solution)/shard_map/cond/branch_0_fun/pallas_call | solution.py:475
  35.5 0.0 copy-start
  35.5 0.6 %copy-done = f32[2,16,256]{2,1,0:T(8,128)} copy-done((f32[2,16,256]{2,1,0:T(8,128)}, f32[2,16,256]{2,1,0:T(8,128)S(1)}, u32[]{:S(2)}) %copy-start) | copy-done | bytes 32792
  (15 shorter events, 0.1 us)
Async XLA Ops:
  1.0 27.9 %collective-permute-start.84 = (f32[32,128]{1,0:T(8,128)S(1)}, f32[32,128]{1,0:T(8,128)S(1)}, u32[]{:S(2)}, u32[]{:S(2)}) collective-permute-start(f32[32,128]{1,0:T(8,128)S(1)} %get-tuple-element.325), channel_id=1, source_target_pairs={{48,0},{49,1},{50,2},{51,3},{52,4},{53,5},{54,6},{55,7},{56,8},{57... | collective-permute-start | bytes 49160 | tf_op jit(solution)/shard_map/ppermute | solution.py:404
  1.7 27.2 %collective-permute-start.85 = (f32[32,128]{1,0:T(8,128)S(1)}, f32[32,128]{1,0:T(8,128)S(1)}, u32[]{:S(2)}, u32[]{:S(2)}) collective-permute-start(f32[32,128]{1,0:T(8,128)S(1)} %get-tuple-element.321.refs_1_), channel_id=1, source_target_pairs={{48,96},{49,97},{50,98},{51,99},{52,100},{53,101},{54,102},{55,103... | collective-permute-start | bytes 49160 | tf_op jit(solution)/shard_map/ppermute | solution.py:405
  2.4 3.7 %collective-permute-start.1 = (f32[32,128]{1,0:T(8,128)S(1)}, f32[32,128]{1,0:T(8,128)S(1)}, u32[]{:S(2)}, u32[]{:S(2)}) collective-permute-start(f32[32,128]{1,0:T(8,128)S(1)} %param.3), channel_id=1, source_target_pairs={{47,46},{143,142},{239,238},{335,334},{431,430},{527,526},{623,622... | collective-permute-start | bytes 49160 | tf_op jit(solution)/shard_map/cond/branch_1_fun/ppermute | solution.py:408
  7.4 15.5 %collective-permute-start.23 = (f32[144,128]{1,0:T(8,128)S(1)}, f32[144,128]{1,0:T(8,128)S(1)}, u32[]{:S(2)}, u32[]{:S(2)}) collective-permute-start(f32[144,128]{1,0:T(8,128)S(1)} %get-tuple-element.211), channel_id=1, source_target_pairs={{191,47},{143,95},{95,143},{47,191},{767,239},{719,287},{671,335},... | collective-permute-start | bytes 221192 | tf_op jit(solution)/shard_map/cond/branch_1_fun/cond/branch_8_fun/ppermute | solution.py:440
  18.7 9.0 %collective-permute-start.22 = (f32[144,128]{1,0:T(8,128)S(1)}, f32[144,128]{1,0:T(8,128)S(1)}, u32[]{:S(2)}, u32[]{:S(2)}) collective-permute-start(f32[144,128]{1,0:T(8,128)S(1)} %get-tuple-element.211), channel_id=1, source_target_pairs={{239,47},{191,95},{143,143},{95,191},{47,239},{767,287},{719,335},... | collective-permute-start | bytes 221192 | tf_op jit(solution)/shard_map/cond/branch_1_fun/cond/branch_8_fun/ppermute | solution.py:440
  29.0 2.0 %collective-permute-start.86 = (f32[32,128]{1,0:T(8,128)S(1)}, f32[32,128]{1,0:T(8,128)S(1)}, u32[]{:S(2)}, u32[]{:S(2)}) collective-permute-start(f32[32,128]{1,0:T(8,128)S(1)} %get-tuple-element.330), channel_id=1, source_target_pairs={{0,48},{1,49},{2,50},{3,51},{4,52},{5,53},{6,54},{7,55},{8,56},{9,... | collective-permute-start | bytes 49160 | tf_op jit(solution)/shard_map/ppermute | solution.py:487
  29.7 1.4 %collective-permute-start.87 = (f32[32,128]{1,0:T(8,128)S(1)}, f32[32,128]{1,0:T(8,128)S(1)}, u32[]{:S(2)}, u32[]{:S(2)}) collective-permute-start(f32[32,128]{1,0:T(8,128)S(1)} %get-tuple-element.331), channel_id=1, source_target_pairs={{0,720},{1,721},{2,722},{3,723},{4,724},{5,725},{6,726},{7,727},{8... | collective-permute-start | bytes 49160 | tf_op jit(solution)/shard_map/ppermute | solution.py:488
  30.3 2.7 %collective-permute-start.89 = (f32[216,128]{1,0:T(8,128)S(1)}, f32[216,128]{1,0:T(8,128)S(1)}, u32[]{:S(2)}, u32[]{:S(2)}) collective-permute-start(f32[216,128]{1,0:T(8,128)S(1)} %get-tuple-element.328.refs_1_), channel_id=1, source_target_pairs={{1,2},{2,1},{3,4},{4,3},{5,6},{6,5},{7,8},{8,7},{9,10},{10,9},{11,... | collective-permute-start | bytes 331784 | tf_op jit(solution)/shard_map/ppermute | solution.py:486
  31.0 3.2 %collective-permute-start.88 = (f32[208,128]{1,0:T(8,128)S(1)}, f32[208,128]{1,0:T(8,128)S(1)}, u32[]{:S(2)}, u32[]{:S(2)}) collective-permute-start(f32[208,128]{1,0:T(8,128)S(1)} %shard_map.82), channel_id=1, source_target_pairs={{0,1},{1,0},{2,3},{3,2},{4,5},{5,4},{6,7},{7,6},{8,9},{9,8},{10,11... | collective-permute-start | bytes 319496 | tf_op jit(solution)/shard_map/ppermute | solution.py:489
  35.5 0.6 %copy-start = (f32[2,16,256]{2,1,0:T(8,128)}, f32[2,16,256]{2,1,0:T(8,128)S(1)}, u32[]{:S(2)}) copy-start(f32[2,16,256]{2,1,0:T(8,128)S(1)} %get-tuple-element.523) | copy-start | bytes 98308
